TPU v7x, 32 devices: a whole 2x2x4 slice. The times are simulated.
32 devices in a mesh: seq: 4 (over y, x), exp: 8 (over z, core).
Axes of the slice: x: 2, y: 2, z: 4, core: 2. Of those that a mesh axis runs over, the one named last changes fastest.
Arguments:
- x_in: bfloat16 [1024, 8192], P('seq', 'exp'), may hold values from -6 to 6
- z_gate: bfloat16 [1024, 8192], P('seq', 'exp'), may hold values from -6 to 6
- b_in: bfloat16 [1024, 128], P('seq'), may hold values from -0.52734375 to 0.52734375
- c_out: bfloat16 [1024, 128], P('seq'), may hold values from -0.375 to 0.375
- dt_step: float32 [1024, 128], P('seq', 'exp'), may hold values from 0.12 to 516, as said below
- rate: float32 [128], P('exp'), may hold values from 0 to 0.06, as said below
- skip: float32 [128], P('exp'), may hold values from 0.5 to 1.5
- init_state: float32 [128, 64, 128], P('exp'), may hold values from -8.485281 to 8.485281
- residual: bfloat16 [1024, 8192], P(('seq', 'exp')), may hold values from -6 to 6
- norm_gain: float32 [8192], replicated, may hold values from 0.5 to 1.5
- expert_ids: int32 [1024, 2], P(('seq', 'exp')), may hold values from 0 to 7, all different within a row; in each aligned block of 32 rows (0 to 31, 32 to 63, ...) at most 9 rows name the same one
- gate_weights: float32 [1024, 2], P(('seq', 'exp')), may hold values from 0.2 to 1
- w_gate: bfloat16 [8, 8192, 2048], P('exp', None, 'seq'), may hold values from -0.0625 to 0.0625
- w_up: bfloat16 [8, 8192, 2048], P('exp', None, 'seq'), may hold values from -0.0625 to 0.0625
- w_down: bfloat16 [8, 2048, 8192], P('exp', 'seq'), may hold values from -0.125 to 0.125
Outputs:
- layer_out: bfloat16 [1024, 8192], P(('seq', 'exp'))
Inputs may be any that keep to these rules, and one draw needn't show every extreme that they name: `dt_step`: positive step sizes. `rate`: positive rates. `expert_ids`: each row names two different experts; among the rows of one device (aligned blocks of 32 rows) no expert is named by more than 9 rows, and in every draw some expert is named by exactly 9 rows of some block.
All inputs are finite; a program needn't handle non-finite values.
Results may differ from a plain program's by a relative error of at most 0.0095.
Values may be sent and summed in bfloat16 or wider, within the bound.
No kernel may reach another device: no remote copies, remote signals or barrier semaphores. Data moves between devices by JAX's collectives and lax.ppermute only.
A program may use at most 128 MiB of HBM per device.

v0:
```python
import functools

import jax
import jax.numpy as jnp
from jax import lax
from jax.experimental import pallas as pl
from jax.experimental.pallas import tpu as pltpu
from jax.sharding import PartitionSpec as P

GROUP = 128
PRECISE = lax.Precision.HIGHEST
F32 = jnp.float32
BF16 = jnp.bfloat16
MIB = 1 << 20
NO_COST = pl.CostEstimate(flops=0, bytes_accessed=0, transcendentals=0)


def block_call(body, outs, scalars, args, held=0, keep=0, after=(), limit=16, out_blocks=False, name=None):
    n_args = len(args)
    kept = [jax.ShapeDtypeStruct(v.shape, v.dtype) for v in args[scalars : scalars + held]]

    def kernel(*refs):
        refs, sems = (refs[:-1], refs[-1]) if held else (refs, None)
        inputs, refs = refs[:n_args], refs[n_args + len(after) :]
        results, refs = refs[: len(outs)], refs[len(outs) :]
        copies = [
            pltpu.make_async_copy(src, dst, sems.at[k])
            for k, (src, dst) in enumerate(zip(inputs[scalars : scalars + held], refs))
        ]
        for copy in copies:
            copy.start()
        for copy in copies:
            copy.wait()
        body(*inputs[:scalars], *refs, *inputs[scalars + held :], *results)

    scratch = [pltpu.VMEM(v.shape, v.dtype) for v in kept[keep:]]
    if held:
        scratch.append(pltpu.SemaphoreType.DMA((held,)))
    return pl.pallas_call(
        kernel,
        name=name or getattr(body, "func", body).__name__,
        out_shape=list(outs) + kept[:keep],
        in_specs=[pl.BlockSpec(memory_space=pltpu.SMEM)] * scalars
        + [pl.BlockSpec(memory_space=pltpu.HBM)] * held
        + [pl.BlockSpec(memory_space=pltpu.VMEM)] * (n_args - scalars - held)
        + [pl.BlockSpec(memory_space=pl.ANY)] * len(after),
        out_specs=[pl.BlockSpec() if out_blocks else pl.BlockSpec(memory_space=pltpu.VMEM)]
        * (len(outs) + keep),
        scratch_shapes=scratch,
        compiler_params=pltpu.CompilerParams(vmem_limit_bytes=limit * MIB),
        cost_estimate=NO_COST,
    )(*args, *after)


def iota(shape, dim):
    return lax.broadcasted_iota(jnp.int32, shape, dim)


def dot(a, b, precision=None):
    return jnp.dot(a, b, precision=precision, preferred_element_type=F32)


def head_spread(heads, channels):
    shape = (heads, channels)
    return (iota(shape, 1) // (channels // heads) == iota(shape, 0)).astype(F32)


def running_logs(dt_t_ref, rate_ref):
    logs = -rate_ref[...] * dt_t_ref[...].T
    tokens = logs.shape[0]
    tri = (iota((tokens, tokens), 0) >= iota((tokens, tokens), 1)).astype(F32)
    return dot(tri, logs, PRECISE)


def pack_kernel(ids_t_ref, residual_ref, out_ref):
    parts, rows, wide = out_ref.shape
    part = wide - 128
    ids = ids_t_ref[...].astype(F32).T
    lane = iota((rows, 128), 1)
    named = jnp.where(lane == 0, ids[:, 0:1], jnp.where(lane == 1, ids[:, 1:2], 0.0)).astype(BF16)
    for k in range(parts):
        out_ref[k, :, 0:part] = residual_ref[:, k * part : (k + 1) * part]
        out_ref[k, :, part:wide] = named


def state_kernel(place, x_ref, b_ref, dt_t_ref, rate_ref, init_ref, payload_ref, init_t_ref):
    tokens, channels = x_ref.shape
    heads = dt_t_ref.shape[0]
    width = b_ref.shape[1]
    cum = running_logs(dt_t_ref, rate_ref)
    total = cum[tokens - 1 : tokens, :]
    spread = head_spread(heads, channels)
    tail = dot(jnp.exp(total - cum), spread, PRECISE)
    scaled = (x_ref[...].astype(F32) * tail).astype(BF16)
    keys = b_ref[...].astype(F32).T.astype(BF16)
    own = dot(keys, scaled)
    decay = dot(jnp.broadcast_to(jnp.exp(total), (8, heads)), spread, PRECISE)
    init_t = init_ref[...].T
    init_t_ref[...] = init_t.astype(BF16)
    first = (place[0] == 0).astype(F32)
    payload_ref[0:width, :] = (own + first * (decay[0:1, :] * init_t)).astype(BF16)
    high = decay.astype(BF16).astype(F32)
    rows = iota((16, channels), 0)
    high16 = jnp.broadcast_to(high[0:1, :], (16, channels))
    low16 = jnp.broadcast_to(decay[0:1, :], (16, channels)) - high16
    payload_ref[width : width + 16, :] = jnp.where(
        rows == 0, high16, jnp.where(rows == 1, low16, 0.0)
    ).astype(BF16)


def intra_kernel(x_ref, z_ref, b_ref, c_ref, dt_t_ref, rate_ref, skip_ref, own_ref, fade_ref, token_ref):
    tokens, channels = x_ref.shape
    heads = dt_t_ref.shape[0]
    width = channels // heads
    token_ref[...] = jnp.zeros_like(token_ref)
    shape = (tokens, tokens)
    causal = iota(shape, 0) >= iota(shape, 1)
    cum = running_logs(dt_t_ref, rate_ref)
    cum_t = cum.T
    scores = lax.dot_general(
        c_ref[...], b_ref[...], (((1,), (1,)), ((), ())), preferred_element_type=F32
    )
    spread = head_spread(heads, channels)
    direct = dot(jnp.broadcast_to(skip_ref[...], (8, heads)), spread, PRECISE)[0:1, :]
    fade = dot(jnp.exp(cum), spread, PRECISE)
    per = 128 // width
    lane_head = iota((tokens, 128), 1) // width
    for group in range(heads // per):
        cols = slice(group * 128, (group + 1) * 128)
        x = x_ref[:, cols]
        total = x.astype(F32) * direct[:, cols]
        for k in range(per):
            h = group * per + k
            gap = jnp.where(causal, cum[:, h : h + 1] - cum_t[h : h + 1, :], -1e30)
            weights = (jnp.exp(gap) * scores).astype(BF16)
            part = dot(weights, x)
            total = total + jnp.where(lane_head == k, part, 0.0)
        z = z_ref[:, cols].astype(F32)
        gate = z / (1.0 + jnp.exp(-z))
        own_ref[:, cols] = total * gate
        fade_ref[:, cols] = fade[:, cols] * gate


def place_kernel(cap, experts, me, packed_ref, *refs):
    count = (len(refs) - 1) // 2
    out_ref = refs[count]
    for source, target in zip(refs[:count], refs[count + 1 :]):
        target[...] = source[...]
    blocks, rows, wide = packed_ref.shape
    tokens = blocks * rows
    slots = out_ref.shape[1] - rows
    ids = packed_ref[:, :, wide - 128 : wide].astype(F32).reshape(tokens, 128).T
    ids = ids[0:8, :].astype(jnp.int32)
    shape = (tokens, tokens)
    before = (iota(shape, 0) < iota(shape, 1)) & (iota(shape, 0) // rows == iota(shape, 1) // rows)
    named = iota((experts, tokens), 0) ^ me[0]
    hit = (ids[0:1, :] == named) | (ids[1:2, :] == named)
    rank = dot(hit.astype(BF16), before.astype(BF16)).astype(jnp.int32)
    block = (iota((experts, tokens), 1) // rows) ^ named
    whole = cap - 1
    row = jnp.where(rank < whole, block * whole + rank, blocks * whole + block)
    row = jnp.where(hit, row, -1)
    shape = (rows + slots, tokens)
    for e in range(experts):
        owned = ((me[0] ^ e) * rows + iota(shape, 0) == iota(shape, 1)) & (iota(shape, 0) < rows)
        placed = (iota(shape, 0) - rows == row[e : e + 1, :]) & (iota(shape, 0) >= rows)
        out_ref[e] = (owned | placed).astype(F32).astype(BF16)


def join_kernel(place, own_ref, other_ref, out_ref):
    width = out_ref.shape[0]
    odd = place[0] % 2 == 1
    own, other = own_ref[0:width, :].astype(F32), other_ref[0:width, :].astype(F32)
    own_decay = own_ref[width : width + 16, :].astype(F32)
    other_decay = other_ref[width : width + 16, :].astype(F32)
    own_decay = own_decay[0:1, :] + own_decay[1:2, :]
    other_decay = other_decay[0:1, :] + other_decay[1:2, :]
    early = jnp.where(odd, other, own)
    late = jnp.where(odd, own, other)
    decay = jnp.where(odd, own_decay, other_decay)
    out_ref[...] = (decay * early + late).astype(BF16)


def stream_kernel(
    place, c_ref, own_ref, fade_ref, init_t_ref, pair_ref, early_ref, res_ref, sel_ref, near_a_ref, near_b_ref, same_ref, other_ref
):
    width = init_t_ref.shape[0]
    at = place[0]
    zero = (at == 0).astype(F32)
    odd = (at % 2 == 1).astype(F32)
    pair = pair_ref[...].astype(F32)
    decay = pair[width : width + 1, :] + pair[width + 1 : width + 2, :]
    factor = jnp.where(at >= 2, jnp.where(at % 2 == 1, decay, 1.0), 0.0)
    entering = zero * init_t_ref[...].astype(F32) + odd * pair[0:width, :] + factor * early_ref[...].astype(F32)
    mixed = own_ref[...] + fade_ref[...] * dot(c_ref[...], entering.astype(BF16))
    mixer = mixed.astype(BF16).astype(F32)
    tokens, channels = mixer.shape
    residual = res_ref[:, :, 0:channels].astype(F32).reshape(tokens, channels)
    stream = (residual + mixer).astype(BF16)
    owned = sel_ref.shape[1] - near_a_ref.shape[0]
    near_a_ref[...] = dot(sel_ref[2, owned:, :], stream).astype(BF16)
    near_b_ref[...] = dot(sel_ref[3, owned:, :], stream).astype(BF16)
    for at, k in enumerate((0, 2, 3, 1)):
        same_ref[at] = dot(sel_ref[2 * k], stream).astype(BF16)
        other_ref[at] = dot(sel_ref[2 * k + 1], stream).astype(BF16)


def up_kernel(first, features, after, me, *refs):
    own, rx, ry, even, odd, gain, wg, wu = refs[:8]
    carry = () if first else refs[8:11]
    rest = refs[(8 if first else 11) + after :]
    sums = rest[2:5] if features else rest
    step = pl.program_id(0)
    steps = pl.num_programs(0)

    if first or features:

        @pl.when(step == 0)
        def _():
            for i, acc in enumerate(sums):
                acc[...] = jnp.zeros_like(acc) if first else carry[i][...]

    gate, up, square = sums
    slots = own.shape[1]
    rows = [r[0].astype(F32) for r in (own, rx, ry)]
    rows.append(jnp.where(step == 0, even[0].astype(F32), odd[0].astype(F32)))
    rows = jnp.concatenate(rows, axis=0)
    square[...] += jnp.broadcast_to(jnp.sum(rows * rows, axis=1, keepdims=True), square.shape)
    scaled = (rows * gain[0]).astype(BF16)
    gate[...] += dot(scaled, wg[0])
    up[...] += dot(scaled, wu[0])

    if features:
        outs, stages = rest[:2], rest[5:]

        @pl.when(step == steps - 1)
        def _():
            inverse = lax.rsqrt(square[:, 0:1] * (1.0 / features) + 1e-06)
            g = gate[...] * inverse
            active = g / (1.0 + jnp.exp(-g)) * (up[...] * inverse)
            main, ninths = slots // 9 * 8, slots // 9
            for d in range(4):
                at = d * slots
                stage, d, shards = (stages[0], 0, 1) if d == 3 else (stages[1], d, 3)
                stage[d * main : (d + 1) * main, :] = active[at : at + main]
                low = shards * main + d * ninths
                stage[low : low + ninths, :] = active[at + main : at + slots]
            for out, stage in zip(outs, stages):
                out[...] = stage[...].astype(BF16)


def up_project(group, last, me, near, far, gain, w_gate, w_up, carry, after=()):
    slots, part = near[0][0].shape[1:]
    hidden = w_gate.shape[2]
    total = 4 * slots
    source = lambda i, me: me[0] ^ (2 * group + i)
    rows = [
        pl.BlockSpec((1, slots, part), lambda i, me, start=start: (start + i, 0, 0))
        for _, start in near
    ] + [
        pl.BlockSpec((1, slots, part), lambda i, me, start=start: (start, 0, 0)) for _, start in far
    ]
    weight = pl.BlockSpec((1, part, hidden), lambda i, me: (source(i, me), 0, 0))
    in_place = pl.BlockSpec(memory_space=pltpu.VMEM)
    specs = rows + [pl.BlockSpec((1, 1, part), lambda i, me: (source(i, me), 0, 0)), weight, weight]
    sums = [
        jax.ShapeDtypeStruct((total, hidden), F32),
        jax.ShapeDtypeStruct((total, hidden), F32),
        jax.ShapeDtypeStruct((total, 128), F32),
    ]
    aliases = {}
    if carry is not None:
        specs += [in_place] * 3
        if not last:
            aliases = {9 + i: i for i in range(3)}
    specs += [pl.BlockSpec(memory_space=pl.ANY)] * len(after)
    sizes = (slots, 3 * slots)
    outs = [jax.ShapeDtypeStruct((n, hidden), BF16) for n in sizes] if last else sums
    scratch = [pltpu.VMEM(s.shape, s.dtype) for s in sums]
    scratch += [pltpu.VMEM((n, hidden), F32) for n in sizes]
    features = gain.shape[0] * part if last else 0
    return pl.pallas_call(
        functools.partial(up_kernel, carry is None, features, len(after)),
        name=f"up_{group}",
        out_shape=outs,
        grid_spec=pltpu.PrefetchScalarGridSpec(
            num_scalar_prefetch=1,
            grid=(2,),
            in_specs=specs,
            out_specs=[in_place] * len(outs),
            scratch_shapes=scratch if last else [],
        ),
        input_output_aliases=aliases,
        compiler_params=pltpu.CompilerParams(vmem_limit_bytes=48 * MIB),
        cost_estimate=NO_COST,
    )(me, *(array for array, _ in near + far), gain, w_gate, w_up, *(carry or ()), *after)


def cut_of(group):
    return 5 if group % 2 else 4


def down_kernel(groups, act_ref, w_ref, *refs):
    outs, (spare, held, sems) = refs[:-3], refs[-3:]
    step = pl.program_id(0)
    steps, _, tile = held.shape

    def load(k):
        columns = pl.ds(pl.multiple_of(k * tile, tile), tile)
        return pltpu.make_async_copy(w_ref.at[:, columns], held.at[k], sems.at[k])

    @pl.when(step == 0)
    def _():
        for k in range(steps):
            load(k).start()

    load(step).wait()
    part = dot(act_ref[...], held[step])
    ninths = part.shape[0] // 9
    main = part.shape[0] - ninths
    shards = ninths // (2 * groups)

    def through(group, tile):
        to_x, to_y = outs[2 * (group // 2) : 2 * (group // 2) + 2]
        cut = cut_of(group)
        return to_x, tile + (0 if group % 2 else 5), to_y, tile - cut + (0 if group % 2 else 4)

    for shard in range(shards):
        for group in range(groups):
            at = (shard * groups + group) * 16
            rows = part[at : at + 16, :].astype(BF16)
            if shards > 1:
                outs[shards * group + shard][step] = rows
                continue
            to_x, place_x, to_y, place_y = through(group, step)

            @pl.when(step < cut_of(group))
            def _():
                to_x[place_x] = rows

            @pl.when(step >= cut_of(group))
            def _():
                to_y[place_y] = rows

    for lanes in range(spare.shape[0]):
        spare[lanes, pl.ds(pl.multiple_of(step * ninths, 8), ninths), :] = part[
            main:, lanes * 128 : (lanes + 1) * 128
        ]

    @pl.when(step == steps - 1)
    def _():
        for shard in range(shards):
            for group in range(groups):
                pair = []
                for side in range(2):
                    row = pl.ds((shard * groups + group) * 2 + side, 8, stride=ninths)
                    ninth = [spare[lanes, row, :] for lanes in range(spare.shape[0])]
                    pair.append(jnp.concatenate(ninth, axis=1))
                pair = jnp.concatenate(pair, axis=0).astype(BF16)
                if shards > 1:
                    outs[shards * group + shard][8] = pair
                else:
                    _, _, to_y, place_y = through(group, 8)
                    to_y[place_y] = pair


def down_project(name, groups, active, w_down):
    total, hidden = active.shape
    features = w_down.shape[1]
    tile = features // 8
    outs = [jax.ShapeDtypeStruct((9, 16, tile), BF16)] * (total // 18)
    return pl.pallas_call(
        functools.partial(down_kernel, groups),
        name=name,
        grid=(8,),
        out_shape=outs,
        in_specs=[
            pl.BlockSpec(memory_space=pltpu.VMEM),
            pl.BlockSpec(memory_space=pltpu.HBM),
        ],
        out_specs=[pl.BlockSpec(memory_space=pltpu.VMEM)] * len(outs),
        scratch_shapes=[
            pltpu.VMEM((tile // 128, 8 * total // 9, 128), F32),
            pltpu.VMEM((8, hidden, tile), BF16),
            pltpu.SemaphoreType.DMA((8,)),
        ],
        compiler_params=pltpu.CompilerParams(vmem_limit_bytes=48 * MIB),
        cost_estimate=NO_COST,
    )(active, w_down)


def pair_kernel(same, other, own_stream, own, far, last_stream, last, near_stream):
    owned = own_stream.shape[1]
    for side, rows in enumerate((same, other)):
        own_stream[side], own[side] = rows[0, 0:owned, :], rows[0, owned:, :]
        far[side] = rows[1]
        last_stream[side], last[side] = rows[2, 0:owned, :], rows[2, owned:, :]
        near_stream[side] = rows[3, 0:owned, :]


def near_kernel(same, other, rows):
    rows[0], rows[1] = same[...], other[...]


def second_kernel(*refs):
    parts, out = refs[:-1], refs[-1]
    for h in range(out.shape[0]):
        for k in range(out.shape[1]):
            pair = [ref[k].astype(F32)[8:16] for ref in parts[2 * h : 2 * h + 2]]
            out[h, k] = jnp.concatenate(pair, axis=0).astype(BF16)


def hold_kernel(*refs):
    for source, target in zip(refs[: len(refs) // 2], refs[len(refs) // 2 :]):
        target[...] = source[...]


def half_message_kernel(rx, ry, out_x, out_y):
    out_x[0], out_y[0] = ry[1], rx[0]


def join_message_kernel(own, rx, ry, out_x, out_y, *parts):
    owned = own.shape[1] - out_x.shape[1]
    for side in range(2):
        rows = own[side, owned:, :]
        out_x[side], out_y[side] = rows, rows
        if parts:
            parts[0][side], parts[1][side] = rows, own[side, 0:owned, :]
    out_x[2], out_y[2] = ry[1], rx[0]


def relay_kernel(through_x, through_y, *refs):
    ahead = refs[4 : 4 + (len(refs) - 8) // 2]
    outs, copies = refs[4 + len(ahead) :][:4], refs[8 + len(ahead) :]
    for group in range(2):
        cut = cut_of(group)
        at_x, at_y = (0, -cut) if group else (5, 0)
        for own, out, through, tiles, at in (
            (refs[2 * group], outs[2 * group], through_y, range(cut, 9), at_y),
            (refs[2 * group + 1], outs[2 * group + 1], through_x, range(cut), at_x),
        ):
            for k in range(9):
                if k in tiles:
                    out[k] = (own[k].astype(F32) + through[k + at].astype(F32)).astype(BF16)
                else:
                    out[k] = own[k]
    for source, copy in zip(ahead, copies):
        copy[...] = source[...]


def finish_kernel(own, rx, ry, *refs):
    ahead = refs[: (len(refs) - 1) // 2]
    out, copies = refs[len(ahead)], refs[len(ahead) + 1 :]
    for k in range(9):
        out[k] = (own[k].astype(F32) + rx[k].astype(F32) + ry[k].astype(F32)).astype(BF16)
    for source, copy in zip(ahead, copies):
        copy[...] = source[...]


def mix_kernel(me, ids_t_ref, weight_t_ref, swap_ref, *refs):
    groups = (len(refs) - 1) // 2
    firsts, streams, out_ref = refs[:groups], refs[groups:-1], refs[-1]
    rows = ids_t_ref.shape[1]
    experts = 2 * groups
    pieces = firsts[0].shape[0] - 1
    tile = firsts[0].shape[2]
    ids, weights = ids_t_ref[...].T, weight_t_ref[...].T
    named = iota((rows, experts), 1) ^ me[0]
    first, second = ids[:, 0:1] == named, ids[:, 1:2] == named
    weight = jnp.where(first, weights[:, 0:1], jnp.where(second, weights[:, 1:2], 0.0))
    hit = (first | second).astype(F32)
    before = (iota((rows, rows), 0) > iota((rows, rows), 1)).astype(F32)
    rank = dot(before, hit)
    lanes = 2 * experts * 8
    shape = (experts, lanes)
    spread = ((iota(shape, 1) // 8) % experts == iota(shape, 0)).astype(F32)
    weight = dot(weight, spread, PRECISE)
    rank = dot(rank, spread, PRECISE).astype(jnp.int32)
    lane = iota((rows, lanes), 1)
    main = (lane < experts * 8) & (rank == lane % 8)
    extra = (lane >= experts * 8) & (rank == 8)

    def rows_of(k):
        data = []
        for g in range(groups):
            data.append(firsts[g][k].astype(F32)[0:8])
            data.append(swap_ref[g // 2, k].astype(F32)[g % 2 * 8 : g % 2 * 8 + 8])
        return data

    last = rows_of(pieces)
    for m in range(experts):
        k = me[0] ^ m
        coef = jnp.where(main | (extra & (lane % 8 == k)), weight, 0.0)
        high = coef.astype(BF16)
        low = (coef - high.astype(F32)).astype(BF16)
        data = jnp.concatenate(rows_of(k) + last, axis=0).astype(BF16)
        stream = streams[m // 2][m % 2].astype(F32)
        out_ref[:, pl.ds(pl.multiple_of(k * tile, 128), tile)] = (
            stream + (dot(high, data) + dot(low, data))
        ).astype(BF16)


def on_square(
    x_in,
    z_gate,
    b_in,
    c_out,
    dt_step,
    rate,
    skip,
    init_state,
    residual,
    norm_gain,
    expert_ids,
    gate_weights,
    w_gate,
    w_up,
    w_down,
):
    tokens, channels = x_in.shape
    heads = rate.shape[0]
    state = b_in.shape[1]
    owners = lax.axis_size("exp")
    rows, features = residual.shape
    experts = owners
    cap = max(2, 2 * rows // experts + 1)
    slots = owners * cap
    at = lax.axis_index("seq")
    me = lax.axis_index("exp")
    place = jnp.reshape(at, (1,)).astype(jnp.int32)
    self_id = jnp.reshape(me, (1,)).astype(jnp.int32)

    def over_x(v):
        return lax.ppermute(v, "seq", [(i, i ^ 1) for i in range(4)])

    def over_y(v):
        return lax.ppermute(v, "seq", [(i, i ^ 2) for i in range(4)])

    def along(v, mask):
        return lax.ppermute(v, "exp", [(i, i ^ mask) for i in range(owners)])

    rate_row = rate[None, :]
    dt_t = dt_step.T
    ids_t = expert_ids.T
    packed = block_call(
        pack_kernel,
        [jax.ShapeDtypeStruct((owners, rows, channels + 128), BF16)],
        0,
        (ids_t, residual),
        held=2,
        limit=48,
    )[0]
    packed = lax.all_to_all(packed, "exp", split_axis=0, concat_axis=0, tiled=True)
    payload, init_t = block_call(
        state_kernel,
        [
            jax.ShapeDtypeStruct((state + 16, channels), BF16),
            jax.ShapeDtypeStruct((state, channels), BF16),
        ],
        1,
        (place, x_in, b_in, dt_t, rate_row, init_state.reshape(channels, state)),
        held=5,
        limit=62,
    )
    pair = over_x(payload)
    own_part, fade, token = block_call(
        intra_kernel,
        [
            jax.ShapeDtypeStruct((tokens, channels), F32),
            jax.ShapeDtypeStruct((tokens, channels), F32),
            jax.ShapeDtypeStruct((8, 128), F32),
        ],
        0,
        (x_in, z_gate, b_in, c_out, dt_t, rate_row, skip[None, :]),
        held=7,
        limit=61,
    )
    joined = block_call(
        join_kernel,
        [jax.ShapeDtypeStruct((state, channels), BF16)],
        1,
        (place, payload, pair),
        after=(token,),
    )[0]
    early = over_y(joined)
    handed = (own_part, fade, c_out, init_t)
    select, own_part, fade, c, init_t = block_call(
        functools.partial(place_kernel, cap, experts),
        [jax.ShapeDtypeStruct((experts, rows + slots, tokens), BF16)]
        + [jax.ShapeDtypeStruct(v.shape, v.dtype) for v in handed],
        1,
        (self_id, packed, *handed),
        after=(joined,),
    )
    groups = owners // 2
    lanes = jax.ShapeDtypeStruct((groups, rows + slots, channels), BF16)
    one = jax.ShapeDtypeStruct((slots, channels), BF16)
    near_a, near_b, same, other = block_call(
        stream_kernel,
        [one, one, lanes, lanes],
        1,
        (place, c, own_part, fade, init_t, pair, early, packed, select),
    )

    gain = norm_gain.reshape(owners, 1, channels)
    wg = w_gate.reshape(owners, channels, w_gate.shape[2])
    wu = w_up.reshape(owners, channels, w_up.shape[2])
    expert_rows = jax.ShapeDtypeStruct((2, slots, channels), BF16)
    stream_rows = jax.ShapeDtypeStruct((2, rows, channels), BF16)
    both_rows = jax.ShapeDtypeStruct((2, rows + slots, channels), BF16)
    near_a, near_b = along(near_a, 2), along(near_b, 3)
    stream0, first, far, stream3, farthest, stream1 = block_call(
        pair_kernel,
        [stream_rows, expert_rows, both_rows, stream_rows, expert_rows, stream_rows],
        0,
        (same, along(other, 1)),
    )
    gain = norm_gain.reshape(owners, 1, channels)
    wg = w_gate.reshape(owners, channels, w_gate.shape[2])
    wu = w_up.reshape(owners, channels, w_up.shape[2])
    gain = norm_gain.reshape(owners, 1, channels)
    wg = w_gate.reshape(owners, channels, w_gate.shape[2])
    wu = w_up.reshape(owners, channels, w_up.shape[2])

    def hold(values, after, name):
        outs = [jax.ShapeDtypeStruct(v.shape, BF16) for v in values]
        return block_call(hold_kernel, outs, 0, values, after=after, name=name)

    def project(group, near, far, carry, after=()):
        last = group == groups - 1
        return up_project(group, last, self_id, near, far, gain, wg, wu, carry, after)

    def message(count):
        return [jax.ShapeDtypeStruct((count, slots, channels), BF16)] * 2

    far = along(far, 4)
    rx0, ry0 = over_x(first), over_y(first)
    near = block_call(near_kernel, [expert_rows], 0, (near_a, near_b))[0]
    rx1, ry1 = over_x(near), over_y(near)
    to_x, to_y = block_call(
        half_message_kernel, message(1), 0, (rx0, ry0), after=(near,), name="half_0"
    )
    fx0, fy0 = over_x(to_x), over_y(to_y)
    farthest_held = hold((farthest,), (far,), "hold_farthest")[0]
    farthest = along(farthest_held, 6)
    to_x, to_y, far, stream2 = block_call(
        join_message_kernel,
        message(3) + [expert_rows, stream_rows],
        0,
        (far, rx1, ry1),
        after=(fx0, fy0, farthest_held),
        name="join_2",
    )
    rx2, ry2 = over_x(to_x), over_y(to_y)
    carry = project(0, [(first, 0), (rx0, 0), (ry0, 0)], [(fy0, 0), (fx0, 0)], None)
    to_x, to_y = block_call(
        join_message_kernel, message(3), 0, (farthest, rx2, ry2), after=(carry[2],), name="join_3"
    )
    rx3, ry3 = over_x(to_x), over_y(to_y)
    held, stream1 = hold((stream3, stream1), (to_x,), "hold_streams")
    stream3, stream1 = along(held, 6), along(stream1, 2)
    carry = project(1, [(near, 0), (rx1, 0), (ry1, 0)], [(ry2, 2), (rx2, 2)], carry, (held,))
    to_x, to_y = block_call(
        half_message_kernel, message(1), 0, (rx3, ry3), after=(carry[2], stream1, stream3), name="half_3"
    )
    fx3, fy3 = over_x(to_x), over_y(to_y)
    carry = project(2, [(far, 0), (rx2, 0), (ry2, 0)], [(ry3, 2), (rx3, 2)], carry)
    active_far, active = project(
        3, [(farthest, 0), (rx3, 0), (ry3, 0)], [(fy3, 0), (fx3, 0)], carry
    )

    wd = w_down.reshape(w_down.shape[1], features)
    tiles = jax.ShapeDtypeStruct((9, 16, features // 8), BF16)
    sent = down_project("down_through", groups, active_far, wd)
    rest = down_project("down_rest", groups, active, wd)
    own, own_x, own_y = ([rest[3 * g + k] for g in range(groups)] for k in range(3))

    def relay(name, through_x, through_y, low, ahead=(), after=()):
        shares = (own_x[low], own_y[low], own_x[low + 1], own_y[low + 1])
        return block_call(
            relay_kernel,
            [tiles] * (4 + len(ahead)),
            0,
            (through_x, through_y, *shares, *ahead),
            after=after,
            name=name,
        )

    def finish(group, rx, ry, ahead=(), after=()):
        return block_call(
            finish_kernel,
            [tiles] * (1 + len(ahead)),
            0,
            (own[group], rx, ry, *ahead),
            after=after,
            name=f"finish_{group}",
        )

    through_x, through_y = over_x(sent[2]), over_y(sent[3])
    x2, y2, x3, y3, next_x, next_y = relay(
        "relay_far", through_x, through_y, 2, (sent[0], sent[1])
    )
    rx3, ry3 = over_x(x3), over_y(y3)
    through_x, through_y = over_x(next_x), over_y(next_y)
    both3, x2, y2 = finish(3, rx3, ry3, (x2, y2))
    back3 = along(both3, 6)
    rx2, ry2 = over_x(x2), over_y(y2)
    x0, y0, x1, y1 = relay("relay_near", through_x, through_y, 0, after=(both3,))
    rx1, ry1 = over_x(x1), over_y(y1)
    both2, x0, y0 = finish(2, rx2, ry2, (x0, y0))
    back2 = along(both2, 4)
    rx0, ry0 = over_x(x0), over_y(y0)
    back1 = along(finish(1, rx1, ry1, after=(back3,))[0], 2)
    back = [finish(0, rx0, ry0)[0], back1, back2, back3]
    swap = block_call(second_kernel, [jax.ShapeDtypeStruct((2,) + tiles.shape, BF16)], 0, back)[0]
    swap = along(swap, 1)
    return block_call(
        mix_kernel,
        [jax.ShapeDtypeStruct((rows, features), BF16)],
        1,
        (self_id, ids_t, gate_weights.T, swap, *back, stream0, stream1, stream2, stream3),
    )[0]


def entering_2(array, axis, combine, identity):
    devices, mine = (lax.axis_size(axis), lax.axis_index(axis))
    everything = jax.tree.map(
        lambda part, kind: lax.all_gather(part.astype(kind), axis),
        array,
        (jnp.bfloat16, jnp.bfloat16),
    )
    start = jax.tree.map(
        lambda part, zero: jnp.broadcast_to(jnp.asarray(zero, part.dtype), part.shape),
        array,
        identity,
    )

    def hop(k, before):
        reached = k < mine
        new = combine(
            before, jax.tree.map(lambda part, own: part[k].astype(own.dtype), everything, array)
        )
        return jax.tree.map(lambda a, b: jnp.where(reached, a, b), new, before)

    return lax.fori_loop(0, devices, hop, start)


def chain_combine(earlier, later):
    return (earlier[0] + later[0], jnp.exp(later[0])[:, None, None] * earlier[1] + later[1])


def on_device(
    x_in,
    z_gate,
    b_in,
    c_out,
    dt_step,
    rate,
    skip,
    init_state,
    residual,
    norm_gain,
    expert_ids,
    gate_weights,
    w_gate,
    w_up,
    w_down,
):
    token_count, channels = x_in.shape
    heads_here = rate.shape[0]
    head_width = channels // heads_here
    state_width = b_in.shape[1]
    blocks = token_count // GROUP
    inputs = x_in.astype(jnp.float32).reshape(blocks, GROUP, heads_here, head_width)
    keys_in = b_in.astype(jnp.float32).reshape(blocks, GROUP, state_width)
    queries = c_out.astype(jnp.float32).reshape(blocks, GROUP, state_width)
    log_steps = (-rate[None, :] * dt_step).reshape(blocks, GROUP, heads_here)
    cumulative = jnp.cumsum(log_steps, axis=1)
    scores = jnp.einsum("ctn,csn->cts", queries, keys_in, precision=PRECISE)
    causal = jnp.arange(GROUP)[:, None] >= jnp.arange(GROUP)[None, :]
    spread = cumulative[:, :, None, :] - cumulative[:, None, :, :]
    weights = jnp.exp(jnp.where(causal[None, :, :, None], spread, -jnp.inf)) * scores[..., None]
    intra_out = jnp.einsum("ctsh,cshp->cthp", weights, inputs, precision=PRECISE)
    tail_decay = jnp.exp(cumulative[:, -1:, :] - cumulative)
    block_state = jnp.einsum("csh,cshp,csn->chpn", tail_decay, inputs, keys_in, precision=PRECISE)
    block_log = cumulative[:, -1, :]

    def advance(carried, element):
        total_log, total_state = carried
        step_log, step_state = element
        updated = (
            total_log + step_log,
            jnp.exp(step_log)[:, None, None] * total_state + step_state,
        )
        return (updated, (total_log, total_state))

    zero_state = jnp.zeros((heads_here, head_width, state_width), jnp.float32)
    zero_log = jnp.zeros((heads_here,), jnp.float32)
    (device_log, device_state), (enter_log, enter_state) = lax.scan(
        advance, (zero_log, zero_state), (block_log, block_state)
    )
    prior_log, prior_state = entering_2(
        (device_log, device_state), "seq", chain_combine, (zero_log, zero_state)
    )
    incoming = prior_state + jnp.exp(prior_log)[:, None, None] * init_state
    entering = enter_state + jnp.exp(enter_log)[:, :, None, None] * incoming[None]
    inter_out = jnp.exp(cumulative)[..., None] * jnp.einsum(
        "chpn,ctn->cthp", entering, queries, precision=PRECISE
    )
    mixed_out = (intra_out + inter_out + skip[None, None, :, None] * inputs).reshape(
        token_count, channels
    )
    mixer = (mixed_out * jax.nn.silu(z_gate.astype(jnp.float32))).astype(jnp.bfloat16)
    token_mix = lax.all_to_all(mixer, "exp", split_axis=0, concat_axis=1, tiled=True)
    stream = (residual.astype(jnp.float32) + token_mix.astype(jnp.float32)).astype(jnp.bfloat16)
    widened = stream.astype(jnp.float32)
    normed = (
        widened
        * lax.rsqrt(jnp.mean(widened * widened, axis=-1, keepdims=True) + 1e-06)
        * norm_gain[None, :]
    ).astype(jnp.bfloat16)
    rows_here = residual.shape[0]
    owners = lax.axis_size("exp")
    local_experts = w_gate.shape[0]
    experts = owners * local_experts
    capacity = max(2, 2 * rows_here // experts + 1)
    width = residual.shape[1]
    chosen = expert_ids.reshape(-1)
    onehot = (chosen[:, None] == jnp.arange(experts)[None, :]).astype(jnp.int32)
    slot_index = jnp.sum((jnp.cumsum(onehot, axis=0) - onehot) * onehot, axis=1)
    target = chosen * capacity + slot_index
    placing = (target[None, :] == jnp.arange(experts * capacity)[:, None]).astype(jnp.bfloat16)
    pair_rows = jnp.repeat(normed, 2, axis=0)
    outgoing = jnp.dot(placing, pair_rows, preferred_element_type=jnp.float32).astype(jnp.bfloat16)
    outgoing = outgoing.reshape(owners, local_experts, 1, capacity, width)
    arrived = lax.all_to_all(outgoing, "exp", split_axis=0, concat_axis=2, tiled=True)
    segment = lax.all_gather(arrived, "seq", axis=1, tiled=True)
    flattened = segment.reshape(segment.shape[0], -1, segment.shape[-1])
    gate_proj = jnp.einsum("erd,edf->erf", flattened, w_gate, preferred_element_type=jnp.float32)
    up_proj = jnp.einsum("erd,edf->erf", flattened, w_up, preferred_element_type=jnp.float32)
    active = (jax.nn.silu(gate_proj) * up_proj).astype(jnp.bfloat16)
    partial_value = jnp.einsum("erf,efd->erd", active, w_down, preferred_element_type=jnp.float32)
    partials = partial_value.reshape(segment.shape[:-1] + (partial_value.shape[-1],))
    summed = lax.psum_scatter(partials.astype(jnp.bfloat16), "seq", scatter_dimension=1, tiled=True)
    returned = lax.all_to_all(summed, "exp", split_axis=2, concat_axis=0, tiled=True)
    results = returned.reshape(experts * capacity, width)
    picked = results[target].astype(jnp.float32).reshape(rows_here, 2, width)
    mixture = jnp.sum(picked * gate_weights[:, :, None], axis=1)
    return (widened + mixture).astype(jnp.bfloat16)


def solution(mesh):
    square = mesh.shape["seq"] == 4 and mesh.shape["exp"] == 8

    def body(*args):
        rows = args[8].shape[0]
        experts = mesh.shape["exp"] * args[12].shape[0]
        fits = args[12].shape[0] == 1 and 2 * rows // experts + 1 == 9
        return (on_square if square and fits else on_device)(*args)

    return jax.shard_map(
        body,
        mesh=mesh,
        in_specs=(
            P("seq", "exp"),
            P("seq", "exp"),
            P("seq", None),
            P("seq", None),
            P("seq", "exp"),
            P("exp"),
            P("exp"),
            P("exp", None, None),
            P(("seq", "exp"), None),
            P(),
            P(("seq", "exp"), None),
            P(("seq", "exp"), None),
            P("exp", None, "seq"),
            P("exp", None, "seq"),
            P("exp", "seq", None),
        ),
        out_specs=P(("seq", "exp"), None),
        check_vma=False,
    )
```

profile of v0, /device:TPU:0, one launch (start us, length us, event | category | flops | bytes accessed | tf_op | source)
XLA Modules:
  0.0 153.5 jit_solution(8818073624501807749)
XLA Ops:
  0.0 1.0 copy-done.3
  1.0 0.7 copy-done.8
  1.7 1.0 pack_kernel.1
  2.8 6.3 %all-to-all-start = ((bf16[8,32,1152]{2,1,0:T(8,128)(2,1)}), bf16[8,32,1152]{2,1,0:T(8,128)(2,1)S(1)}, u32[]{:S(2)}, u32[]{:S(2)}) async-start(bf16[8,32,1152]{2,1,0:T(8,128)(2,1)} %pack_kernel.1), calls=%async_computation | async-start | bytes 1179648 | tf_op jit(solution)/shard_map/all_to_all | solution.py:553
  9.1 4.1 %state_kernel.1 = (bf16[144,1024]{1,0:T(8,128)(2,1)}, bf16[128,1024]{1,0:T(8,128)(2,1)}) custom-call(s32[1]{0:T(128)} %bitcast.3.refs_0_, bf16[256,1024]{1,0:T(8,128)(2,1)} %refs_1_.5, bf16[256,128]{1,0:T(8,128)(2,1)} %refs_2_.3, f32[16,256]{1,0:T(8,128)} %bitcast.30, f32[1,16]{1,0:T(1,128)} %bitcast.32, f32[1024,128]{1,0:T(8,128)} %bitcast.29), custom_call_target="tpu_custom_call" | custom-call | tf_op jit(solution)/shard_map/state_kernel/pallas_call | solution.py:39
  13.2 1.6 %collective-permute-start = (bf16[144,1024]{1,0:T(8,128)(2,1)}, bf16[144,1024]{1,0:T(8,128)(2,1)S(1)}, u32[]{:S(2)}, u32[]{:S(2)}) collective-permute-start(bf16[144,1024]{1,0:T(8,128)(2,1)} %get-tuple-element.83.refs_1_), channel_id=1, source_target_pairs={{0,8},{8,0},{16,24},{24,16},{1,9},{9,1},{17,25},{25,17},{2,10},{10... | collective-permute-start | bytes 884744 | tf_op jit(solution)/shard_map/ppermute | solution.py:534
  14.8 4.7 %intra_kernel.1 = (f32[256,1024]{1,0:T(8,128)}, f32[256,1024]{1,0:T(8,128)}, f32[8,128]{1,0:T(8,128)}) custom-call(bf16[256,1024]{1,0:T(8,128)(2,1)} %refs_1_.5, bf16[256,1024]{1,0:T(8,128)(2,1)} %refs_1_.4, bf16[256,128]{1,0:T(8,128)(2,1)} %refs_2_.3, bf16[256,128]{1,0:T(8,128)(2,1)} %refs_4_.1, f32[16,256]{1,0:T(8,128)} %bitcast.31, f32[1,16]{1,0:T(1,128)} %bitcast.33, ...), custom_call_target="tpu_custom_call" | custom-call | tf_op jit(solution)/shard_map/intra_kernel/pallas_call | solution.py:39
  19.5 3.4 %collective-permute-done.refs_2_.refs_5_ = bf16[144,1024]{1,0:T(8,128)(2,1)S(1)} collective-permute-done((bf16[144,1024]{1,0:T(8,128)(2,1)}, bf16[144,1024]{1,0:T(8,128)(2,1)S(1)}, u32[]{:S(2)}, u32[]{:S(2)}) %collective-permute-start) | collective-permute-done | bytes 294944 | tf_op jit(solution)/shard_map/ppermute | solution.py:534
  22.9 1.0 copy-done.4
  23.9 0.7 copy-done.7
  24.7 1.6 %collective-permute-start.1 = (bf16[128,1024]{1,0:T(8,128)(2,1)S(1)}, bf16[128,1024]{1,0:T(8,128)(2,1)S(1)}, u32[]{:S(2)}, u32[]{:S(2)}) collective-permute-start(bf16[128,1024]{1,0:T(8,128)(2,1)S(1)} %join_kernel.1.refs_6_), channel_id=1, source_target_pairs={{0,16},{8,24},{16,0},{24,8},{1,17},{9,25},{17,1},{25,9},{2,18},{10... | collective-permute-start | bytes 786440 | tf_op jit(solution)/shard_map/ppermute | solution.py:537
  26.3 1.2 copy-done
  27.5 1.2 copy-done.1
  28.7 0.9 copy-done.5
  29.7 0.8 copy-done.6
  30.9 1.8 %collective-permute-done.1.refs_6_ = bf16[128,1024]{1,0:T(8,128)(2,1)S(1)} collective-permute-done((bf16[128,1024]{1,0:T(8,128)(2,1)S(1)}, bf16[128,1024]{1,0:T(8,128)(2,1)S(1)}, u32[]{:S(2)}, u32[]{:S(2)}) %collective-permute-start.1) | collective-permute-done | bytes 262176 | tf_op jit(solution)/shard_map/ppermute | solution.py:537
  32.7 1.3 stream_kernel.1
  34.1 1.3 collective-permute-start.5
  35.4 1.0 collective-permute-done.2.refs_1_
  36.6 1.6 %collective-permute-start.10 = (bf16[2,72,1024]{2,1,0:T(8,128)(2,1)S(1)}, bf16[2,72,1024]{2,1,0:T(8,128)(2,1)S(1)}, u32[]{:S(2)}, u32[]{:S(2)}) collective-permute-start(bf16[2,72,1024]{2,1,0:T(8,128)(2,1)S(1)} %get-tuple-element.96.refs_0_), channel_id=1, source_target_pairs={{0,16},{8,24},{16,0},{24,8},{1,17},{9,25},{17,1},{25,9},{2,18},{10... | collective-permute-start | bytes 884744 | tf_op jit(solution)/shard_map/ppermute | solution.py:537
  38.2 1.5 collective-permute-start.9
  40.1 2.4 %collective-permute-start.3 = (bf16[2,104,1024]{2,1,0:T(8,128)(2,1)S(1)}, bf16[2,104,1024]{2,1,0:T(8,128)(2,1)S(1)}, u32[]{:S(2)}, u32[]{:S(2)}) collective-permute-start(bf16[2,104,1024]{2,1,0:T(8,128)(2,1)S(1)} %get-tuple-element.93), channel_id=1, source_target_pairs={{0,4},{1,5},{2,6},{3,7},{4,0},{5,1},{6,2},{7,3},{8,12},{9,13},{10,... | collective-permute-start | bytes 1277960 | tf_op jit(solution)/shard_map/ppermute | solution.py:540
  42.5 6.0 %collective-permute-done.6.refs_1_ = bf16[72,1024]{1,0:T(8,128)(2,1)S(1)} collective-permute-done((bf16[72,1024]{1,0:T(8,128)(2,1)S(1)}, bf16[72,1024]{1,0:T(8,128)(2,1)S(1)}, u32[]{:S(2)}, u32[]{:S(2)}) %collective-permute-start.6) | collective-permute-done | bytes 147488 | tf_op jit(solution)/shard_map/ppermute | solution.py:540
  49.7 1.5 collective-permute-start.11
  51.2 1.5 collective-permute-start.12
  52.7 10.1 %collective-permute-done.3.refs_1_.refs_0_ = bf16[2,104,1024]{2,1,0:T(8,128)(2,1)S(1)} collective-permute-done((bf16[2,104,1024]{2,1,0:T(8,128)(2,1)S(1)}, bf16[2,104,1024]{2,1,0:T(8,128)(2,1)S(1)}, u32[]{:S(2)}, u32[]{:S(2)}) %collective-permute-start.3) | collective-permute-done | bytes 426016 | tf_op jit(solution)/shard_map/ppermute | solution.py:540
  64.1 2.4 %collective-permute-start.4 = (bf16[2,72,1024]{2,1,0:T(8,128)(2,1)S(1)}, bf16[2,72,1024]{2,1,0:T(8,128)(2,1)S(1)}, u32[]{:S(2)}, u32[]{:S(2)}) collective-permute-start(bf16[2,72,1024]{2,1,0:T(8,128)(2,1)S(1)} %hold_farthest.1.refs_5_), channel_id=1, source_target_pairs={{0,6},{1,7},{2,4},{3,5},{4,2},{5,3},{6,0},{7,1},{8,14},{9,15},{10,... | collective-permute-start | bytes 884744 | tf_op jit(solution)/shard_map/ppermute | solution.py:540
  66.5 3.3 %up_0.1 = (f32[288,512]{1,0:T(8,128)S(1)}, f32[288,512]{1,0:T(8,128)S(1)}, f32[288,128]{1,0:T(8,128)S(1)}) custom-call(s32[1]{0:T(128)} %bitcast.refs_0_.me, bf16[2,72,1024]{2,1,0:T(8,128)(2,1)S(1)} %get-tuple-element.96.refs_0_, bf16[2,72,1024]{2,1,0:T(8,128)(2,1)S(1)} %collective-permute-done.9.refs_0_.refs_1_, ...), custom_call_target="tpu_custom_call" | custom-call | tf_op jit(solution)/shard_map/up_0/pallas_call | solution.py:282
  69.7 4.7 %collective-permute-done.4.refs_0_ = bf16[2,72,1024]{2,1,0:T(8,128)(2,1)S(1)} collective-permute-done((bf16[2,72,1024]{2,1,0:T(8,128)(2,1)S(1)}, bf16[2,72,1024]{2,1,0:T(8,128)(2,1)S(1)}, u32[]{:S(2)}, u32[]{:S(2)}) %collective-permute-start.4) | collective-permute-done | bytes 294944 | tf_op jit(solution)/shard_map/ppermute | solution.py:540
  74.4 0.8 collective-permute-done.13.refs_1_.refs_4_
  76.1 1.5 collective-permute-start.15
  77.6 3.7 %collective-permute-start.17 = (bf16[2,32,1024]{2,1,0:T(8,128)(2,1)S(1)}, bf16[2,32,1024]{2,1,0:T(8,128)(2,1)S(1)}, u32[]{:S(2)}, u32[]{:S(2)}) collective-permute-start(bf16[2,32,1024]{2,1,0:T(8,128)(2,1)S(1)} %get-tuple-element.110), channel_id=1, source_target_pairs={{0,2},{1,3},{2,0},{3,1},{4,6},{5,7},{6,4},{7,5},{8,10},{9,11},{10,... | collective-permute-start | bytes 393224 | tf_op jit(solution)/shard_map/ppermute | solution.py:540
  81.3 1.8 %collective-permute-start.18 = (bf16[2,32,1024]{2,1,0:T(8,128)(2,1)S(1)}, bf16[2,32,1024]{2,1,0:T(8,128)(2,1)S(1)}, u32[]{:S(2)}, u32[]{:S(2)}) collective-permute-start(bf16[2,32,1024]{2,1,0:T(8,128)(2,1)S(1)} %get-tuple-element.108.refs_11_), channel_id=1, source_target_pairs={{0,6},{1,7},{2,4},{3,5},{4,2},{5,3},{6,0},{7,1},{8,14},{9,15},{10,... | collective-permute-start | bytes 393224 | tf_op jit(solution)/shard_map/ppermute | solution.py:540
  83.1 3.2 %up_1.1 = (f32[288,512]{1,0:T(8,128)S(1)}, f32[288,512]{1,0:T(8,128)S(1)}, f32[288,128]{1,0:T(8,128)S(1)}) custom-call(s32[1]{0:T(128)} %bitcast.refs_0_.me, bf16[2,72,1024]{2,1,0:T(8,128)(2,1)S(1)} %near_kernel.1.refs_2_.refs_0_, ...), custom_call_target="tpu_custom_call", output_to_operand_aliasing={{0}: (9, {}), {1}: (10, {}), {2}: (11, {})} | custom-call | tf_op jit(solution)/shard_map/up_1/pallas_call | solution.py:282
  86.3 1.8 %collective-permute-done.18.refs_4_.refs_11_ = bf16[2,32,1024]{2,1,0:T(8,128)(2,1)S(1)} collective-permute-done((bf16[2,32,1024]{2,1,0:T(8,128)(2,1)S(1)}, bf16[2,32,1024]{2,1,0:T(8,128)(2,1)S(1)}, u32[]{:S(2)}, u32[]{:S(2)}) %collective-permute-start.18) | collective-permute-done | bytes 131104 | tf_op jit(solution)/shard_map/ppermute | solution.py:540
  88.7 1.2 collective-permute-start.20
  89.9 3.2 %up_2.1 = (f32[288,512]{1,0:T(8,128)S(1)}, f32[288,512]{1,0:T(8,128)S(1)}, f32[288,128]{1,0:T(8,128)S(1)}) custom-call(s32[1]{0:T(128)} %bitcast.refs_0_.me, bf16[2,72,1024]{2,1,0:T(8,128)(2,1)S(1)} %get-tuple-element.113.refs_0_, ...), custom_call_target="tpu_custom_call", output_to_operand_aliasing={{0}: (9, {}), {1}: (10, {}), {2}: (11, {})} | custom-call | tf_op jit(solution)/shard_map/up_2/pallas_call | solution.py:282
  93.9 3.5 %up_3.1 = (bf16[72,512]{1,0:T(8,128)(2,1)S(1)}, bf16[216,512]{1,0:T(8,128)(2,1)S(1)}) custom-call(s32[1]{0:T(128)} %bitcast.refs_0_.me, bf16[2,72,1024]{2,1,0:T(8,128)(2,1)S(1)} %collective-permute-done.4.refs_0_, bf16[3,72,1024]{2,1,0:T(8,128)(2,1)S(1)} %collective-permute-done.15.refs_0_.refs_4_.refs_1_, ...), custom_call_target="tpu_custom_call" | custom-call | tf_op jit(solution)/shard_map/up_3/pallas_call | solution.py:282
  97.4 4.2 %down_through.1 = (bf16[9,16,1024]{2,1,0:T(8,128)(2,1)S(1)}, bf16[9,16,1024]{2,1,0:T(8,128)(2,1)S(1)}, bf16[9,16,1024]{2,1,0:T(8,128)(2,1)S(1)}, bf16[9,16,1024]{2,1,0:T(8,128)(2,1)S(1)}) custom-call(bf16[72,512]{1,0:T(8,128)(2,1)S(1)} %get-tuple-element.123.act_ref, bf16[512,8192]{1,0:T(8,128)(2,1)} %bitcast.27), custom_call_target="tpu_custom_call" | custom-call | tf_op jit(solution)/shard_map/down_through/pallas_call | solution.py:372
  101.6 1.3 collective-permute-start.21
  102.8 0.9 collective-permute-start.22
  103.7 5.1 %down_rest.1 = (bf16[9,16,1024]{2,1,0:T(8,128)(2,1)S(1)}, bf16[9,16,1024]{2,1,0:T(8,128)(2,1)S(1)}, bf16[9,16,1024]{2,1,0:T(8,128)(2,1)S(1)}, bf16[9,16,1024]{2,...) custom-call(bf16[216,512]{1,0:T(8,128)(2,1)S(1)} %get-tuple-element., ...), custom_call_target="tpu_custom_call" | custom-call | tf_op jit(solution)/shard_map/down_rest/pallas_call | solution.py:372
  109.4 1.7 %collective-permute-done.22.refs_1_ = bf16[9,16,1024]{2,1,0:T(8,128)(2,1)S(1)} collective-permute-done((bf16[9,16,1024]{2,1,0:T(8,128)(2,1)S(1)}, bf16[9,16,1024]{2,1,0:T(8,128)(2,1)S(1)}, u32[]{:S(2)}, u32[]{:S(2)}) %collective-permute-start.22) | collective-permute-done | bytes 294944 | tf_op jit(solution)/shard_map/ppermute | solution.py:537
  111.3 0.7 collective-permute-start.23
  111.9 1.6 %collective-permute-start.24 = (bf16[9,16,1024]{2,1,0:T(8,128)(2,1)S(1)}, bf16[9,16,1024]{2,1,0:T(8,128)(2,1)S(1)}, u32[]{:S(2)}, u32[]{:S(2)}) collective-permute-start(bf16[9,16,1024]{2,1,0:T(8,128)(2,1)S(1)} %get-tuple-element.133), channel_id=1, source_target_pairs={{0,16},{8,24},{16,0},{24,8},{1,17},{9,25},{17,1},{25,9},{2,18},{10... | collective-permute-start | bytes 884744 | tf_op jit(solution)/shard_map/ppermute | solution.py:537
  113.8 1.5 collective-permute-start.28
  115.4 5.5 %collective-permute-done.23.refs_1_ = bf16[9,16,1024]{2,1,0:T(8,128)(2,1)S(1)} collective-permute-done((bf16[9,16,1024]{2,1,0:T(8,128)(2,1)S(1)}, bf16[9,16,1024]{2,1,0:T(8,128)(2,1)S(1)}, u32[]{:S(2)}, u32[]{:S(2)}) %collective-permute-start.23) | collective-permute-done | bytes 294944 | tf_op jit(solution)/shard_map/ppermute | solution.py:534
  120.8 1.0 collective-permute-done.24.refs_2_
  122.0 1.2 collective-permute-start.25
  123.3 0.7 collective-permute-start.26
  124.0 2.1 %collective-permute-start.33 = (bf16[9,16,1024]{2,1,0:T(8,128)(2,1)S(1)}, bf16[9,16,1024]{2,1,0:T(8,128)(2,1)S(1)}, u32[]{:S(2)}, u32[]{:S(2)}) collective-permute-start(bf16[9,16,1024]{2,1,0:T(8,128)(2,1)S(1)} %get-tuple-element.144.refs_6_), channel_id=1, source_target_pairs={{0,6},{1,7},{2,4},{3,5},{4,2},{5,3},{6,0},{7,1},{8,14},{9,15},{10,... | collective-permute-start | bytes 884744 | tf_op jit(solution)/shard_map/ppermute | solution.py:540
  126.1 1.1 collective-permute-done.27.refs_0_
  127.2 1.0 collective-permute-done.28.refs_1_
  128.4 1.2 collective-permute-start.31
  129.6 0.7 collective-permute-start.32
  130.3 3.1 %collective-permute-done.25.refs_1_ = bf16[9,16,1024]{2,1,0:T(8,128)(2,1)S(1)} collective-permute-done((bf16[9,16,1024]{2,1,0:T(8,128)(2,1)S(1)}, bf16[9,16,1024]{2,1,0:T(8,128)(2,1)S(1)}, u32[]{:S(2)}, u32[]{:S(2)}) %collective-permute-start.25) | collective-permute-done | bytes 294944 | tf_op jit(solution)/shard_map/ppermute | solution.py:534
  133.5 1.0 collective-permute-done.26.refs_2_
  134.7 1.2 collective-permute-start.29
  135.9 0.7 collective-permute-start.30
  136.6 5.0 %collective-permute-start.35 = (bf16[9,16,1024]{2,1,0:T(8,128)(2,1)S(1)}, bf16[9,16,1024]{2,1,0:T(8,128)(2,1)S(1)}, u32[]{:S(2)}, u32[]{:S(2)}) collective-permute-start(bf16[9,16,1024]{2,1,0:T(8,128)(2,1)S(1)} %get-tuple-element.152), channel_id=1, source_target_pairs={{0,4},{1,5},{2,6},{3,7},{4,0},{5,1},{6,2},{7,3},{8,12},{9,13},{10,... | collective-permute-start | bytes 884744 | tf_op jit(solution)/shard_map/ppermute | solution.py:540
  141.9 0.7 collective-permute-done.30.refs_2_
  142.7 6.8 %collective-permute-done.35.refs_2_.refs_6_ = bf16[9,16,1024]{2,1,0:T(8,128)(2,1)S(1)} collective-permute-done((bf16[9,16,1024]{2,1,0:T(8,128)(2,1)S(1)}, bf16[9,16,1024]{2,1,0:T(8,128)(2,1)S(1)}, u32[]{:S(2)}, u32[]{:S(2)}) %collective-permute-start.35) | collective-permute-done | bytes 294944 | tf_op jit(solution)/shard_map/ppermute | solution.py:540
  149.7 2.0 %collective-permute-done.36.refs_3_ = bf16[2,9,16,1024]{3,2,1,0:T(8,128)(2,1)S(1)} collective-permute-done((bf16[2,9,16,1024]{3,2,1,0:T(8,128)(2,1)S(1)}, bf16[2,9,16,1024]{3,2,1,0:T(8,128)(2,1)S(1)}, u32[]{:S(2)}, u32[]{:S(2)}) %collective-permute-start.36) | collective-permute-done | bytes 589856 | tf_op jit(solution)/shard_map/ppermute | solution.py:540
  151.6 1.9 %mix_kernel.1 = bf16[32,8192]{1,0:T(8,128)(2,1)} custom-call(s32[1]{0:T(128)} %bitcast.refs_0_.me, s32[2,32]{1,0:T(2,128)S(1)} %bitcast.17, f32[2,32]{1,0:T(2,128)S(1)} %bitcast.18, bf16[2,9,16,1024]{3,2,1,0:T(8,128)(2,1)S(1)} %collective-permute-done.36.refs_3_, bf16[9,16,1024]{2,1,0:T(8,128)(2,1)S(1)} %finish_0.1.refs_0_.refs_4_, ...), custom_call_target="tpu_custom_call" | custom-call | tf_op jit(solution)/shard_map/mix_kernel/pallas_call | solution.py:39
  (62 shorter events, 7.7 us)
Async XLA Ops:
  0.0 1.0 copy-start.3
  1.0 0.7 copy-start.8
  2.8 23.5 %all-to-all-start = ((bf16[8,32,1152]{2,1,0:T(8,128)(2,1)}), bf16[8,32,1152]{2,1,0:T(8,128)(2,1)S(1)}, u32[]{:S(2)}, u32[]{:S(2)}) async-start(bf16[8,32,1152]{2,1,0:T(8,128)(2,1)} %pack_kernel.1), calls=%async_computation | async-start | bytes 1179648 | tf_op jit(solution)/shard_map/all_to_all | solution.py:553
  9.1 57.4 %copy-start.2 = (f32[8192]{0:T(1024)S(1)}, f32[8192]{0:T(1024)}, u32[]{:S(2)}) copy-start(f32[8192]{0:T(1024)} %param.24) | copy-start | bytes 98308
  13.2 9.7 %collective-permute-start = (bf16[144,1024]{1,0:T(8,128)(2,1)}, bf16[144,1024]{1,0:T(8,128)(2,1)S(1)}, u32[]{:S(2)}, u32[]{:S(2)}) collective-permute-start(bf16[144,1024]{1,0:T(8,128)(2,1)} %get-tuple-element.83.refs_1_), channel_id=1, source_target_pairs={{0,8},{8,0},{16,24},{24,16},{1,9},{9,1},{17,25},{25,17},{2,10},{10... | collective-permute-start | bytes 884744 | tf_op jit(solution)/shard_map/ppermute | solution.py:534
  22.9 1.0 copy-start.4
  23.9 0.7 copy-start.7
  24.7 8.0 %collective-permute-start.1 = (bf16[128,1024]{1,0:T(8,128)(2,1)S(1)}, bf16[128,1024]{1,0:T(8,128)(2,1)S(1)}, u32[]{:S(2)}, u32[]{:S(2)}) collective-permute-start(bf16[128,1024]{1,0:T(8,128)(2,1)S(1)} %join_kernel.1.refs_6_), channel_id=1, source_target_pairs={{0,16},{8,24},{16,0},{24,8},{1,17},{9,25},{17,1},{25,9},{2,18},{10... | collective-permute-start | bytes 786440 | tf_op jit(solution)/shard_map/ppermute | solution.py:537
  26.3 1.2 copy-start
  27.5 1.2 copy-start.1
  28.7 0.9 copy-start.5
  29.7 0.8 copy-start.6
  34.0 2.4 %collective-permute-start.2 = (bf16[4,104,1024]{2,1,0:T(8,128)(2,1)S(1)}, bf16[4,104,1024]{2,1,0:T(8,128)(2,1)S(1)}, u32[]{:S(2)}, u32[]{:S(2)}) collective-permute-start(bf16[4,104,1024]{2,1,0:T(8,128)(2,1)S(1)} %get-tuple-element.91), channel_id=1, source_target_pairs={{0,1},{1,0},{2,3},{3,2},{4,5},{5,4},{6,7},{7,6},{8,9},{9,8},{10,11... | collective-permute-start | bytes 2555912 | tf_op jit(solution)/shard_map/ppermute | solution.py:540
  34.1 8.4 %collective-permute-start.5 = (bf16[72,1024]{1,0:T(8,128)(2,1)S(1)}, bf16[72,1024]{1,0:T(8,128)(2,1)S(1)}, u32[]{:S(2)}, u32[]{:S(2)}) collective-permute-start(bf16[72,1024]{1,0:T(8,128)(2,1)S(1)} %get-tuple-element.94), channel_id=1, source_target_pairs={{0,2},{1,3},{2,0},{3,1},{4,6},{5,7},{6,4},{7,5},{8,10},{9,11},{10,... | collective-permute-start | bytes 442376 | tf_op jit(solution)/shard_map/ppermute | solution.py:540
  36.6 13.1 %collective-permute-start.10 = (bf16[2,72,1024]{2,1,0:T(8,128)(2,1)S(1)}, bf16[2,72,1024]{2,1,0:T(8,128)(2,1)S(1)}, u32[]{:S(2)}, u32[]{:S(2)}) collective-permute-start(bf16[2,72,1024]{2,1,0:T(8,128)(2,1)S(1)} %get-tuple-element.96.refs_0_), channel_id=1, source_target_pairs={{0,16},{8,24},{16,0},{24,8},{1,17},{9,25},{17,1},{25,9},{2,18},{10... | collective-permute-start | bytes 884744 | tf_op jit(solution)/shard_map/ppermute | solution.py:537
  38.2 11.5 %collective-permute-start.9 = (bf16[2,72,1024]{2,1,0:T(8,128)(2,1)S(1)}, bf16[2,72,1024]{2,1,0:T(8,128)(2,1)S(1)}, u32[]{:S(2)}, u32[]{:S(2)}) collective-permute-start(bf16[2,72,1024]{2,1,0:T(8,128)(2,1)S(1)} %get-tuple-element.96.refs_0_), channel_id=1, source_target_pairs={{0,8},{8,0},{16,24},{24,16},{1,9},{9,1},{17,25},{25,17},{2,10},{10... | collective-permute-start | bytes 884744 | tf_op jit(solution)/shard_map/ppermute | solution.py:534
  39.6 8.9 %collective-permute-start.6 = (bf16[72,1024]{1,0:T(8,128)(2,1)S(1)}, bf16[72,1024]{1,0:T(8,128)(2,1)S(1)}, u32[]{:S(2)}, u32[]{:S(2)}) collective-permute-start(bf16[72,1024]{1,0:T(8,128)(2,1)S(1)} %get-tuple-element.95), channel_id=1, source_target_pairs={{0,3},{1,2},{2,1},{3,0},{4,7},{5,6},{6,5},{7,4},{8,11},{9,10},{10,... | collective-permute-start | bytes 442376 | tf_op jit(solution)/shard_map/ppermute | solution.py:540
  40.1 22.7 %collective-permute-start.3 = (bf16[2,104,1024]{2,1,0:T(8,128)(2,1)S(1)}, bf16[2,104,1024]{2,1,0:T(8,128)(2,1)S(1)}, u32[]{:S(2)}, u32[]{:S(2)}) collective-permute-start(bf16[2,104,1024]{2,1,0:T(8,128)(2,1)S(1)} %get-tuple-element.93), channel_id=1, source_target_pairs={{0,4},{1,5},{2,6},{3,7},{4,0},{5,1},{6,2},{7,3},{8,12},{9,13},{10,... | collective-permute-start | bytes 1277960 | tf_op jit(solution)/shard_map/ppermute | solution.py:540
  48.5 14.3 %collective-permute-start.8 = (bf16[2,72,1024]{2,1,0:T(8,128)(2,1)S(1)}, bf16[2,72,1024]{2,1,0:T(8,128)(2,1)S(1)}, u32[]{:S(2)}, u32[]{:S(2)}) collective-permute-start(bf16[2,72,1024]{2,1,0:T(8,128)(2,1)S(1)} %near_kernel.1.refs_2_.refs_0_), channel_id=1, source_target_pairs={{0,16},{8,24},{16,0},{24,8},{1,17},{9,25},{17,1},{25,9},{2,18},{10... | collective-permute-start | bytes 884744 | tf_op jit(solution)/shard_map/ppermute | solution.py:537
  49.1 13.7 %collective-permute-start.7 = (bf16[2,72,1024]{2,1,0:T(8,128)(2,1)S(1)}, bf16[2,72,1024]{2,1,0:T(8,128)(2,1)S(1)}, u32[]{:S(2)}, u32[]{:S(2)}) collective-permute-start(bf16[2,72,1024]{2,1,0:T(8,128)(2,1)S(1)} %near_kernel.1.refs_2_.refs_0_), channel_id=1, source_target_pairs={{0,8},{8,0},{16,24},{24,16},{1,9},{9,1},{17,25},{25,17},{2,10},{10... | collective-permute-start | bytes 884744 | tf_op jit(solution)/shard_map/ppermute | solution.py:534
  49.7 13.2 %collective-permute-start.11 = (bf16[1,72,1024]{2,1,0:T(8,128)(2,1)S(1)}, bf16[1,72,1024]{2,1,0:T(8,128)(2,1)S(1)}, u32[]{:S(2)}, u32[]{:S(2)}) collective-permute-start(bf16[1,72,1024]{2,1,0:T(8,128)(2,1)S(1)} %get-tuple-element.97), channel_id=1, source_target_pairs={{0,8},{8,0},{16,24},{24,16},{1,9},{9,1},{17,25},{25,17},{2,10},{10... | collective-permute-start | bytes 442376 | tf_op jit(solution)/shard_map/ppermute | solution.py:534
  51.2 11.6 %collective-permute-start.12 = (bf16[1,72,1024]{2,1,0:T(8,128)(2,1)S(1)}, bf16[1,72,1024]{2,1,0:T(8,128)(2,1)S(1)}, u32[]{:S(2)}, u32[]{:S(2)}) collective-permute-start(bf16[1,72,1024]{2,1,0:T(8,128)(2,1)S(1)} %get-tuple-element.98), channel_id=1, source_target_pairs={{0,16},{8,24},{16,0},{24,8},{1,17},{9,25},{17,1},{25,9},{2,18},{10... | collective-permute-start | bytes 442376 | tf_op jit(solution)/shard_map/ppermute | solution.py:537
  63.0 12.2 %collective-permute-start.13 = (bf16[3,72,1024]{2,1,0:T(8,128)(2,1)S(1)}, bf16[3,72,1024]{2,1,0:T(8,128)(2,1)S(1)}, u32[]{:S(2)}, u32[]{:S(2)}) collective-permute-start(bf16[3,72,1024]{2,1,0:T(8,128)(2,1)S(1)} %get-tuple-element.99), channel_id=1, source_target_pairs={{0,8},{8,0},{16,24},{24,16},{1,9},{9,1},{17,25},{25,17},{2,10},{10... | collective-permute-start | bytes 1327112 | tf_op jit(solution)/shard_map/ppermute | solution.py:534
  63.6 11.9 %collective-permute-start.14 = (bf16[3,72,1024]{2,1,0:T(8,128)(2,1)S(1)}, bf16[3,72,1024]{2,1,0:T(8,128)(2,1)S(1)}, u32[]{:S(2)}, u32[]{:S(2)}) collective-permute-start(bf16[3,72,1024]{2,1,0:T(8,128)(2,1)S(1)} %get-tuple-element.100), channel_id=1, source_target_pairs={{0,16},{8,24},{16,0},{24,8},{1,17},{9,25},{17,1},{25,9},{2,18},{10... | collective-permute-start | bytes 1327112 | tf_op jit(solution)/shard_map/ppermute | solution.py:537
  64.1 10.3 %collective-permute-start.4 = (bf16[2,72,1024]{2,1,0:T(8,128)(2,1)S(1)}, bf16[2,72,1024]{2,1,0:T(8,128)(2,1)S(1)}, u32[]{:S(2)}, u32[]{:S(2)}) collective-permute-start(bf16[2,72,1024]{2,1,0:T(8,128)(2,1)S(1)} %hold_farthest.1.refs_5_), channel_id=1, source_target_pairs={{0,6},{1,7},{2,4},{3,5},{4,2},{5,3},{6,0},{7,1},{8,14},{9,15},{10,... | collective-permute-start | bytes 884744 | tf_op jit(solution)/shard_map/ppermute | solution.py:540
  75.5 12.6 %collective-permute-start.16 = (bf16[3,72,1024]{2,1,0:T(8,128)(2,1)S(1)}, bf16[3,72,1024]{2,1,0:T(8,128)(2,1)S(1)}, u32[]{:S(2)}, u32[]{:S(2)}) collective-permute-start(bf16[3,72,1024]{2,1,0:T(8,128)(2,1)S(1)} %get-tuple-element.103), channel_id=1, source_target_pairs={{0,16},{8,24},{16,0},{24,8},{1,17},{9,25},{17,1},{25,9},{2,18},{10... | collective-permute-start | bytes 1327112 | tf_op jit(solution)/shard_map/ppermute | solution.py:537
  76.1 12.0 %collective-permute-start.15 = (bf16[3,72,1024]{2,1,0:T(8,128)(2,1)S(1)}, bf16[3,72,1024]{2,1,0:T(8,128)(2,1)S(1)}, u32[]{:S(2)}, u32[]{:S(2)}) collective-permute-start(bf16[3,72,1024]{2,1,0:T(8,128)(2,1)S(1)} %get-tuple-element.102.refs_2_), channel_id=1, source_target_pairs={{0,8},{8,0},{16,24},{24,16},{1,9},{9,1},{17,25},{25,17},{2,10},{10... | collective-permute-start | bytes 1327112 | tf_op jit(solution)/shard_map/ppermute | solution.py:534
  77.6 8.7 %collective-permute-start.17 = (bf16[2,32,1024]{2,1,0:T(8,128)(2,1)S(1)}, bf16[2,32,1024]{2,1,0:T(8,128)(2,1)S(1)}, u32[]{:S(2)}, u32[]{:S(2)}) collective-permute-start(bf16[2,32,1024]{2,1,0:T(8,128)(2,1)S(1)} %get-tuple-element.110), channel_id=1, source_target_pairs={{0,2},{1,3},{2,0},{3,1},{4,6},{5,7},{6,4},{7,5},{8,10},{9,11},{10,... | collective-permute-start | bytes 393224 | tf_op jit(solution)/shard_map/ppermute | solution.py:540
  81.3 6.8 %collective-permute-start.18 = (bf16[2,32,1024]{2,1,0:T(8,128)(2,1)S(1)}, bf16[2,32,1024]{2,1,0:T(8,128)(2,1)S(1)}, u32[]{:S(2)}, u32[]{:S(2)}) collective-permute-start(bf16[2,32,1024]{2,1,0:T(8,128)(2,1)S(1)} %get-tuple-element.108.refs_11_), channel_id=1, source_target_pairs={{0,6},{1,7},{2,4},{3,5},{4,2},{5,3},{6,0},{7,1},{8,14},{9,15},{10,... | collective-permute-start | bytes 393224 | tf_op jit(solution)/shard_map/ppermute | solution.py:540
  88.1 5.2 %collective-permute-start.19 = (bf16[1,72,1024]{2,1,0:T(8,128)(2,1)S(1)}, bf16[1,72,1024]{2,1,0:T(8,128)(2,1)S(1)}, u32[]{:S(2)}, u32[]{:S(2)}) collective-permute-start(bf16[1,72,1024]{2,1,0:T(8,128)(2,1)S(1)} %get-tuple-element.111), channel_id=1, source_target_pairs={{0,16},{8,24},{16,0},{24,8},{1,17},{9,25},{17,1},{25,9},{2,18},{10... | collective-permute-start | bytes 442376 | tf_op jit(solution)/shard_map/ppermute | solution.py:537
  88.7 5.1 %collective-permute-start.20 = (bf16[1,72,1024]{2,1,0:T(8,128)(2,1)S(1)}, bf16[1,72,1024]{2,1,0:T(8,128)(2,1)S(1)}, u32[]{:S(2)}, u32[]{:S(2)}) collective-permute-start(bf16[1,72,1024]{2,1,0:T(8,128)(2,1)S(1)} %get-tuple-element.112), channel_id=1, source_target_pairs={{0,8},{8,0},{16,24},{24,16},{1,9},{9,1},{17,25},{25,17},{2,10},{10... | collective-permute-start | bytes 442376 | tf_op jit(solution)/shard_map/ppermute | solution.py:534
  101.6 7.8 %collective-permute-start.21 = (bf16[9,16,1024]{2,1,0:T(8,128)(2,1)S(1)}, bf16[9,16,1024]{2,1,0:T(8,128)(2,1)S(1)}, u32[]{:S(2)}, u32[]{:S(2)}) collective-permute-start(bf16[9,16,1024]{2,1,0:T(8,128)(2,1)S(1)} %get-tuple-element.124), channel_id=1, source_target_pairs={{0,8},{8,0},{16,24},{24,16},{1,9},{9,1},{17,25},{25,17},{2,10},{10... | collective-permute-start | bytes 884744 | tf_op jit(solution)/shard_map/ppermute | solution.py:534
  102.8 8.3 %collective-permute-start.22 = (bf16[9,16,1024]{2,1,0:T(8,128)(2,1)S(1)}, bf16[9,16,1024]{2,1,0:T(8,128)(2,1)S(1)}, u32[]{:S(2)}, u32[]{:S(2)}) collective-permute-start(bf16[9,16,1024]{2,1,0:T(8,128)(2,1)S(1)} %get-tuple-element.125), channel_id=1, source_target_pairs={{0,16},{8,24},{16,0},{24,8},{1,17},{9,25},{17,1},{25,9},{2,18},{10... | collective-permute-start | bytes 884744 | tf_op jit(solution)/shard_map/ppermute | solution.py:537
  103.7 47.9 %copy-start.9 = (s32[32,2]{0,1:T(2,128)S(1)}, s32[32,2]{0,1:T(2,128)}, u32[]{:S(2)}) copy-start(s32[32,2]{0,1:T(2,128)} %param.25) | copy-start | bytes 772
  103.7 47.9 %copy-start.10 = (f32[32,2]{0,1:T(2,128)S(1)}, f32[32,2]{0,1:T(2,128)}, u32[]{:S(2)}) copy-start(f32[32,2]{0,1:T(2,128)} %param.26) | copy-start | bytes 772
  111.3 9.6 %collective-permute-start.23 = (bf16[9,16,1024]{2,1,0:T(8,128)(2,1)S(1)}, bf16[9,16,1024]{2,1,0:T(8,128)(2,1)S(1)}, u32[]{:S(2)}, u32[]{:S(2)}) collective-permute-start(bf16[9,16,1024]{2,1,0:T(8,128)(2,1)S(1)} %get-tuple-element.132), channel_id=1, source_target_pairs={{0,8},{8,0},{16,24},{24,16},{1,9},{9,1},{17,25},{25,17},{2,10},{10... | collective-permute-start | bytes 884744 | tf_op jit(solution)/shard_map/ppermute | solution.py:534
  111.9 9.9 %collective-permute-start.24 = (bf16[9,16,1024]{2,1,0:T(8,128)(2,1)S(1)}, bf16[9,16,1024]{2,1,0:T(8,128)(2,1)S(1)}, u32[]{:S(2)}, u32[]{:S(2)}) collective-permute-start(bf16[9,16,1024]{2,1,0:T(8,128)(2,1)S(1)} %get-tuple-element.133), channel_id=1, source_target_pairs={{0,16},{8,24},{16,0},{24,8},{1,17},{9,25},{17,1},{25,9},{2,18},{10... | collective-permute-start | bytes 884744 | tf_op jit(solution)/shard_map/ppermute | solution.py:537
  113.6 13.6 %collective-permute-start.27 = (bf16[9,16,1024]{2,1,0:T(8,128)(2,1)S(1)}, bf16[9,16,1024]{2,1,0:T(8,128)(2,1)S(1)}, u32[]{:S(2)}, u32[]{:S(2)}) collective-permute-start(bf16[9,16,1024]{2,1,0:T(8,128)(2,1)S(1)} %get-tuple-element.138), channel_id=1, source_target_pairs={{0,8},{8,0},{16,24},{24,16},{1,9},{9,1},{17,25},{25,17},{2,10},{10... | collective-permute-start | bytes 884744 | tf_op jit(solution)/shard_map/ppermute | solution.py:534
  113.8 14.4 %collective-permute-start.28 = (bf16[9,16,1024]{2,1,0:T(8,128)(2,1)S(1)}, bf16[9,16,1024]{2,1,0:T(8,128)(2,1)S(1)}, u32[]{:S(2)}, u32[]{:S(2)}) collective-permute-start(bf16[9,16,1024]{2,1,0:T(8,128)(2,1)S(1)} %get-tuple-element.139), channel_id=1, source_target_pairs={{0,16},{8,24},{16,0},{24,8},{1,17},{9,25},{17,1},{25,9},{2,18},{10... | collective-permute-start | bytes 884744 | tf_op jit(solution)/shard_map/ppermute | solution.py:537
  122.0 11.5 %collective-permute-start.25 = (bf16[9,16,1024]{2,1,0:T(8,128)(2,1)S(1)}, bf16[9,16,1024]{2,1,0:T(8,128)(2,1)S(1)}, u32[]{:S(2)}, u32[]{:S(2)}) collective-permute-start(bf16[9,16,1024]{2,1,0:T(8,128)(2,1)S(1)} %get-tuple-element.136), channel_id=1, source_target_pairs={{0,8},{8,0},{16,24},{24,16},{1,9},{9,1},{17,25},{25,17},{2,10},{10... | collective-permute-start | bytes 884744 | tf_op jit(solution)/shard_map/ppermute | solution.py:534
  123.3 11.3 %collective-permute-start.26 = (bf16[9,16,1024]{2,1,0:T(8,128)(2,1)S(1)}, bf16[9,16,1024]{2,1,0:T(8,128)(2,1)S(1)}, u32[]{:S(2)}, u32[]{:S(2)}) collective-permute-start(bf16[9,16,1024]{2,1,0:T(8,128)(2,1)S(1)} %get-tuple-element.137), channel_id=1, source_target_pairs={{0,16},{8,24},{16,0},{24,8},{1,17},{9,25},{17,1},{25,9},{2,18},{10... | collective-permute-start | bytes 884744 | tf_op jit(solution)/shard_map/ppermute | solution.py:537
  124.0 12.6 %collective-permute-start.33 = (bf16[9,16,1024]{2,1,0:T(8,128)(2,1)S(1)}, bf16[9,16,1024]{2,1,0:T(8,128)(2,1)S(1)}, u32[]{:S(2)}, u32[]{:S(2)}) collective-permute-start(bf16[9,16,1024]{2,1,0:T(8,128)(2,1)S(1)} %get-tuple-element.144.refs_6_), channel_id=1, source_target_pairs={{0,6},{1,7},{2,4},{3,5},{4,2},{5,3},{6,0},{7,1},{8,14},{9,15},{10,... | collective-permute-start | bytes 884744 | tf_op jit(solution)/shard_map/ppermute | solution.py:540
  128.4 13.3 %collective-permute-start.31 = (bf16[9,16,1024]{2,1,0:T(8,128)(2,1)S(1)}, bf16[9,16,1024]{2,1,0:T(8,128)(2,1)S(1)}, u32[]{:S(2)}, u32[]{:S(2)}) collective-permute-start(bf16[9,16,1024]{2,1,0:T(8,128)(2,1)S(1)} %get-tuple-element.150), channel_id=1, source_target_pairs={{0,8},{8,0},{16,24},{24,16},{1,9},{9,1},{17,25},{25,17},{2,10},{10... | collective-permute-start | bytes 884744 | tf_op jit(solution)/shard_map/ppermute | solution.py:534
  129.6 12.1 %collective-permute-start.32 = (bf16[9,16,1024]{2,1,0:T(8,128)(2,1)S(1)}, bf16[9,16,1024]{2,1,0:T(8,128)(2,1)S(1)}, u32[]{:S(2)}, u32[]{:S(2)}) collective-permute-start(bf16[9,16,1024]{2,1,0:T(8,128)(2,1)S(1)} %get-tuple-element.151), channel_id=1, source_target_pairs={{0,16},{8,24},{16,0},{24,8},{1,17},{9,25},{17,1},{25,9},{2,18},{10... | collective-permute-start | bytes 884744 | tf_op jit(solution)/shard_map/ppermute | solution.py:537
  134.7 7.2 %collective-permute-start.29 = (bf16[9,16,1024]{2,1,0:T(8,128)(2,1)S(1)}, bf16[9,16,1024]{2,1,0:T(8,128)(2,1)S(1)}, u32[]{:S(2)}, u32[]{:S(2)}) collective-permute-start(bf16[9,16,1024]{2,1,0:T(8,128)(2,1)S(1)} %get-tuple-element.147), channel_id=1, source_target_pairs={{0,8},{8,0},{16,24},{24,16},{1,9},{9,1},{17,25},{25,17},{2,10},{10... | collective-permute-start | bytes 884744 | tf_op jit(solution)/shard_map/ppermute | solution.py:534
  135.9 6.7 %collective-permute-start.30 = (bf16[9,16,1024]{2,1,0:T(8,128)(2,1)S(1)}, bf16[9,16,1024]{2,1,0:T(8,128)(2,1)S(1)}, u32[]{:S(2)}, u32[]{:S(2)}) collective-permute-start(bf16[9,16,1024]{2,1,0:T(8,128)(2,1)S(1)} %get-tuple-element.148), channel_id=1, source_target_pairs={{0,16},{8,24},{16,0},{24,8},{1,17},{9,25},{17,1},{25,9},{2,18},{10... | collective-permute-start | bytes 884744 | tf_op jit(solution)/shard_map/ppermute | solution.py:537
  136.6 12.9 %collective-permute-start.35 = (bf16[9,16,1024]{2,1,0:T(8,128)(2,1)S(1)}, bf16[9,16,1024]{2,1,0:T(8,128)(2,1)S(1)}, u32[]{:S(2)}, u32[]{:S(2)}) collective-permute-start(bf16[9,16,1024]{2,1,0:T(8,128)(2,1)S(1)} %get-tuple-element.152), channel_id=1, source_target_pairs={{0,4},{1,5},{2,6},{3,7},{4,0},{5,1},{6,2},{7,3},{8,12},{9,13},{10,... | collective-permute-start | bytes 884744 | tf_op jit(solution)/shard_map/ppermute | solution.py:540
  141.8 7.7 %collective-permute-start.34 = (bf16[9,16,1024]{2,1,0:T(8,128)(2,1)S(1)}, bf16[9,16,1024]{2,1,0:T(8,128)(2,1)S(1)}, u32[]{:S(2)}, u32[]{:S(2)}) collective-permute-start(bf16[9,16,1024]{2,1,0:T(8,128)(2,1)S(1)} %finish_1.1), channel_id=1, source_target_pairs={{0,2},{1,3},{2,0},{3,1},{4,6},{5,7},{6,4},{7,5},{8,10},{9,11},{10,... | collective-permute-start | bytes 884744 | tf_op jit(solution)/shard_map/ppermute | solution.py:540
  149.6 2.1 %collective-permute-start.36 = (bf16[2,9,16,1024]{3,2,1,0:T(8,128)(2,1)S(1)}, bf16[2,9,16,1024]{3,2,1,0:T(8,128)(2,1)S(1)}, u32[]{:S(2)}, u32[]{:S(2)}) collective-permute-start(bf16[2,9,16,1024]{3,2,1,0:T(8,128)(2,1)S(1)} %second_kernel.1), channel_id=1, source_target_pairs={{0,1},{1,0},{2,3},{3,2},{4,5},{5,4},{6,7},{7,6},{8,9},{9,8},{10,11... | collective-permute-start | bytes 1769480 | tf_op jit(solution)/shard_map/ppermute | solution.py:540
where the time goes:
time: 154 us
  waiting for transfers between devices  55.1 us (36%)
  starting transfers between devices  53.3 us (35%)
  Pallas kernels  37.2 us (24%)
  local copies, waits for them, and re-layouts  7.61 us (5%)
    ppermute x11, waiting for transfers between devices, along(): return lax.ppermute(v, 'exp', [(i, i ^ mask) for i in range(owners)])  32.4 us
    ppermute x11, starting transfers between devices, along(): return lax.ppermute(v, 'exp', [(i, i ^ mask) for i in range(owners)])  19.4 us
    ppermute x13, waiting for transfers between devices, over_x(): return lax.ppermute(v, 'seq', [(i, i ^ 1) for i in range(4)])  15 us
    pallas_call x22, Pallas kernels, block_call(): pl.pallas_call(kernel, name=name or getattr(body, 'func', body).__name__,...  14.8 us
    ppermute x13, starting transfers between devices, over_x(): return lax.ppermute(v, 'seq', [(i, i ^ 1) for i in range(4)])  14.3 us
    ppermute x13, starting transfers between devices, over_y(): return lax.ppermute(v, 'seq', [(i, i ^ 2) for i in range(4)])  13.3 us
    pallas_call x4, Pallas kernels, up_project(): pl.pallas_call(functools.partial(up_kernel, carry is None, features, len(...  13.2 us
    pallas_call x2, Pallas kernels, down_project(): pl.pallas_call(functools.partial(down_kernel, groups), name=name, grid=(8...  9.3 us
  transfers between devices with their start and end apart: 38, of which 22 were waited for; matrix products, arithmetic and copies ran while one was open for 0% of the time, Pallas kernels for 16%

commit v1 on v0

--- a/solution.py
+++ b/solution.py
@@ -389,11 +389,11 @@
     )(active, w_down)
 
 
-def pair_kernel(same, other, own_stream, own, far, last_stream, last, near_stream):
+def pair_kernel(same, other, own_stream, own, far_stream, far, last_stream, last, near_stream):
     owned = own_stream.shape[1]
     for side, rows in enumerate((same, other)):
         own_stream[side], own[side] = rows[0, 0:owned, :], rows[0, owned:, :]
-        far[side] = rows[1]
+        far_stream[side], far[side] = rows[1, 0:owned, :], rows[1, owned:, :]
         last_stream[side], last[side] = rows[2, 0:owned, :], rows[2, owned:, :]
         near_stream[side] = rows[3, 0:owned, :]
 
@@ -419,13 +419,8 @@
     out_x[0], out_y[0] = ry[1], rx[0]
 
 
-def join_message_kernel(own, rx, ry, out_x, out_y, *parts):
-    owned = own.shape[1] - out_x.shape[1]
-    for side in range(2):
-        rows = own[side, owned:, :]
-        out_x[side], out_y[side] = rows, rows
-        if parts:
-            parts[0][side], parts[1][side] = rows, own[side, 0:owned, :]
+def join_message_kernel(own, rx, ry, out_x, out_y):
+    out_x[0:2], out_y[0:2] = own[...], own[...]
     out_x[2], out_y[2] = ry[1], rx[0]
 
 
@@ -542,15 +537,6 @@
     rate_row = rate[None, :]
     dt_t = dt_step.T
     ids_t = expert_ids.T
-    packed = block_call(
-        pack_kernel,
-        [jax.ShapeDtypeStruct((owners, rows, channels + 128), BF16)],
-        0,
-        (ids_t, residual),
-        held=2,
-        limit=48,
-    )[0]
-    packed = lax.all_to_all(packed, "exp", split_axis=0, concat_axis=0, tiled=True)
     payload, init_t = block_call(
         state_kernel,
         [
@@ -563,6 +549,16 @@
         limit=62,
     )
     pair = over_x(payload)
+    packed = block_call(
+        pack_kernel,
+        [jax.ShapeDtypeStruct((owners, rows, channels + 128), BF16)],
+        0,
+        (ids_t, residual),
+        held=2,
+        after=(payload,),
+        limit=48,
+    )[0]
+    packed = lax.all_to_all(packed, "exp", split_axis=0, concat_axis=0, tiled=True)
     own_part, fade, token = block_call(
         intra_kernel,
         [
@@ -580,7 +576,6 @@
         [jax.ShapeDtypeStruct((state, channels), BF16)],
         1,
         (place, payload, pair),
-        after=(token,),
     )[0]
     early = over_y(joined)
     handed = (own_part, fade, c_out, init_t)
@@ -607,11 +602,10 @@
     wu = w_up.reshape(owners, channels, w_up.shape[2])
     expert_rows = jax.ShapeDtypeStruct((2, slots, channels), BF16)
     stream_rows = jax.ShapeDtypeStruct((2, rows, channels), BF16)
-    both_rows = jax.ShapeDtypeStruct((2, rows + slots, channels), BF16)
     near_a, near_b = along(near_a, 2), along(near_b, 3)
-    stream0, first, far, stream3, farthest, stream1 = block_call(
+    stream0, first, stream2, far, stream3, farthest, stream1 = block_call(
         pair_kernel,
-        [stream_rows, expert_rows, both_rows, stream_rows, expert_rows, stream_rows],
+        [stream_rows, expert_rows] * 3 + [stream_rows],
         0,
         (same, along(other, 1)),
     )
@@ -643,9 +637,9 @@
     fx0, fy0 = over_x(to_x), over_y(to_y)
     farthest_held = hold((farthest,), (far,), "hold_farthest")[0]
     farthest = along(farthest_held, 6)
-    to_x, to_y, far, stream2 = block_call(
+    to_x, to_y = block_call(
         join_message_kernel,
-        message(3) + [expert_rows, stream_rows],
+        message(3),
         0,
         (far, rx1, ry1),
         after=(fx0, fy0, farthest_held),
@@ -657,11 +651,11 @@
         join_message_kernel, message(3), 0, (farthest, rx2, ry2), after=(carry[2],), name="join_3"
     )
     rx3, ry3 = over_x(to_x), over_y(to_y)
-    held, stream1 = hold((stream3, stream1), (to_x,), "hold_streams")
-    stream3, stream1 = along(held, 6), along(stream1, 2)
-    carry = project(1, [(near, 0), (rx1, 0), (ry1, 0)], [(ry2, 2), (rx2, 2)], carry, (held,))
+    held = hold((stream1, stream2, stream3), (to_x,), "hold_streams")
+    stream1, stream2, stream3 = (along(v, 2 * g + 2) for g, v in enumerate(held))
+    carry = project(1, [(near, 0), (rx1, 0), (ry1, 0)], [(ry2, 2), (rx2, 2)], carry, held[:1])
     to_x, to_y = block_call(
-        half_message_kernel, message(1), 0, (rx3, ry3), after=(carry[2], stream1, stream3), name="half_3"
+        half_message_kernel, message(1), 0, (rx3, ry3), after=(carry[2], stream1, stream2, stream3), name="half_3"
     )
     fx3, fy3 = over_x(to_x), over_y(to_y)
     carry = project(2, [(far, 0), (rx2, 0), (ry2, 0)], [(ry3, 2), (rx3, 2)], carry)

time: 154 us -> 156 us (1.013)
  waiting for transfers between devices: 55.1 us -> 62 us
  starting transfers between devices: 53.3 us -> 48.4 us
    ppermute x13, waiting for transfers between devices: 15 us -> 27.7 us  [over_x(): return lax.ppermute(v, 'seq', [(i, i ^ 1) for i in range(4)])]
    ppermute x11 -> x12, waiting for transfers between devices: 32.4 us -> 26.7 us  [along(): return lax.ppermute(v, 'exp', [(i, i ^ mask) for i in range(owners)])]
    ppermute x13, starting transfers between devices: 14.3 us -> 12 us  [over_x(): return lax.ppermute(v, 'seq', [(i, i ^ 1) for i in range(4)])]
    ppermute x11 -> x12, starting transfers between devices: 19.4 us -> 17 us  [along(): return lax.ppermute(v, 'exp', [(i, i ^ mask) for i in range(owners)])]
  transfers between devices with their start and end apart: 38 -> 39, of which waited for: 22 -> 26; matrix products, arithmetic and copies ran while one was open for 0% -> 0% of each run, Pallas kernels for 16% -> 13%
where the time goes in v1:
time: 156 us
  waiting for transfers between devices  62 us (40%)
  starting transfers between devices  48.4 us (31%)
  Pallas kernels  37 us (24%)
  local copies, waits for them, and re-layouts  7.88 us (5%)
    ppermute x13, waiting for transfers between devices, over_x(): return lax.ppermute(v, 'seq', [(i, i ^ 1) for i in range(4)])  27.7 us
    ppermute x12, waiting for transfers between devices, along(): return lax.ppermute(v, 'exp', [(i, i ^ mask) for i in range(owners)])  26.7 us
    ppermute x12, starting transfers between devices, along(): return lax.ppermute(v, 'exp', [(i, i ^ mask) for i in range(owners)])  17 us
    pallas_call x22, Pallas kernels, block_call(): pl.pallas_call(kernel, name=name or getattr(body, 'func', body).__name__,...  14.7 us
    pallas_call x4, Pallas kernels, up_project(): pl.pallas_call(functools.partial(up_kernel, carry is None, features, len(...  13.1 us
    ppermute x13, starting transfers between devices, over_y(): return lax.ppermute(v, 'seq', [(i, i ^ 2) for i in range(4)])  13 us
    ppermute x13, starting transfers between devices, over_x(): return lax.ppermute(v, 'seq', [(i, i ^ 1) for i in range(4)])  12 us
    pallas_call x2, Pallas kernels, down_project(): pl.pallas_call(functools.partial(down_kernel, groups), name=name, grid=(8...  9.18 us
  transfers between devices with their start and end apart: 39, of which 26 were waited for; matrix products, arithmetic and copies ran while one was open for 0% of the time, Pallas kernels for 13%

profile of v1, /device:TPU:0, one launch (start us, length us, event | category | flops | bytes accessed | tf_op | source)
XLA Modules:
  0.0 155.5 jit_solution(9880372417747321152)
XLA Ops:
  0.0 4.1 %state_kernel.1 = (bf16[144,1024]{1,0:T(8,128)(2,1)}, bf16[128,1024]{1,0:T(8,128)(2,1)}) custom-call(s32[1]{0:T(128)} %bitcast.3.refs_0_, bf16[256,1024]{1,0:T(8,128)(2,1)} %refs_0_.1, bf16[256,128]{1,0:T(8,128)(2,1)} %refs_2_.3, f32[16,256]{1,0:T(8,128)} %bitcast.30, f32[1,16]{1,0:T(1,128)} %bitcast.32, f32[1024,128]{1,0:T(8,128)} %bitcast.29), custom_call_target="tpu_custom_call" | custom-call | tf_op jit(solution)/shard_map/state_kernel/pallas_call | solution.py:39
  4.1 1.0 copy-done
  5.1 1.0 copy-done.5
  6.1 0.7 copy-done.8
  6.8 1.0 pack_kernel.1
  7.9 6.3 %all-to-all-start = ((bf16[8,32,1152]{2,1,0:T(8,128)(2,1)}), bf16[8,32,1152]{2,1,0:T(8,128)(2,1)S(1)}, u32[]{:S(2)}, u32[]{:S(2)}) async-start(bf16[8,32,1152]{2,1,0:T(8,128)(2,1)} %pack_kernel.1), calls=%async_computation | async-start | bytes 1179648 | tf_op jit(solution)/shard_map/all_to_all | solution.py:561
  14.2 1.5 collective-permute-start
  15.7 8.1 %collective-permute-done.refs_2_.refs_5_ = bf16[144,1024]{1,0:T(8,128)(2,1)S(1)} collective-permute-done((bf16[144,1024]{1,0:T(8,128)(2,1)}, bf16[144,1024]{1,0:T(8,128)(2,1)S(1)}, u32[]{:S(2)}, u32[]{:S(2)}) %collective-permute-start) | collective-permute-done | bytes 294944 | tf_op jit(solution)/shard_map/ppermute | solution.py:529
  23.8 1.0 copy-done.1
  24.9 1.6 %collective-permute-start.1 = (bf16[128,1024]{1,0:T(8,128)(2,1)S(1)}, bf16[128,1024]{1,0:T(8,128)(2,1)S(1)}, u32[]{:S(2)}, u32[]{:S(2)}) collective-permute-start(bf16[128,1024]{1,0:T(8,128)(2,1)S(1)} %join_kernel.1.refs_6_), channel_id=1, source_target_pairs={{0,16},{8,24},{16,0},{24,8},{1,17},{9,25},{17,1},{25,9},{2,18},{10... | collective-permute-start | bytes 786440 | tf_op jit(solution)/shard_map/ppermute | solution.py:532
  26.5 4.7 %intra_kernel.1 = (f32[256,1024]{1,0:T(8,128)}, f32[256,1024]{1,0:T(8,128)}, f32[8,128]{1,0:T(8,128)}) custom-call(bf16[256,1024]{1,0:T(8,128)(2,1)} %refs_0_.1, bf16[256,1024]{1,0:T(8,128)(2,1)} %refs_1_.5, bf16[256,128]{1,0:T(8,128)(2,1)} %refs_2_.3, bf16[256,128]{1,0:T(8,128)(2,1)} %refs_4_.1, f32[16,256]{1,0:T(8,128)} %bitcast.31, f32[1,16]{1,0:T(1,128)} %bitcast.33, ...), custom_call_target="tpu_custom_call" | custom-call | tf_op jit(solution)/shard_map/intra_kernel/pallas_call | solution.py:39
  31.3 1.2 copy-done.2
  32.5 1.2 copy-done.3
  33.7 0.9 copy-done.6
  34.6 0.8 copy-done.7
  35.9 1.3 stream_kernel.1
  37.3 1.7 %collective-permute-start.5 = (bf16[72,1024]{1,0:T(8,128)(2,1)S(1)}, bf16[72,1024]{1,0:T(8,128)(2,1)S(1)}, u32[]{:S(2)}, u32[]{:S(2)}) collective-permute-start(bf16[72,1024]{1,0:T(8,128)(2,1)S(1)} %get-tuple-element.92), channel_id=1, source_target_pairs={{0,2},{1,3},{2,0},{3,1},{4,6},{5,7},{6,4},{7,5},{8,10},{9,11},{10,... | collective-permute-start | bytes 442376 | tf_op jit(solution)/shard_map/ppermute | solution.py:535
  39.7 1.3 collective-permute-start.10
  41.1 1.5 collective-permute-start.9
  42.7 2.4 %collective-permute-start.3 = (bf16[2,72,1024]{2,1,0:T(8,128)(2,1)S(1)}, bf16[2,72,1024]{2,1,0:T(8,128)(2,1)S(1)}, u32[]{:S(2)}, u32[]{:S(2)}) collective-permute-start(bf16[2,72,1024]{2,1,0:T(8,128)(2,1)S(1)} %get-tuple-element.91), channel_id=1, source_target_pairs={{0,4},{1,5},{2,6},{3,7},{4,0},{5,1},{6,2},{7,3},{8,12},{9,13},{10,... | collective-permute-start | bytes 884744 | tf_op jit(solution)/shard_map/ppermute | solution.py:535
  45.0 6.4 %collective-permute-done.6.refs_1_ = bf16[72,1024]{1,0:T(8,128)(2,1)S(1)} collective-permute-done((bf16[72,1024]{1,0:T(8,128)(2,1)S(1)}, bf16[72,1024]{1,0:T(8,128)(2,1)S(1)}, u32[]{:S(2)}, u32[]{:S(2)}) %collective-permute-start.6) | collective-permute-done | bytes 147488 | tf_op jit(solution)/shard_map/ppermute | solution.py:535
  51.4 0.9 collective-permute-start.8
  52.8 1.6 %collective-permute-start.11 = (bf16[1,72,1024]{2,1,0:T(8,128)(2,1)S(1)}, bf16[1,72,1024]{2,1,0:T(8,128)(2,1)S(1)}, u32[]{:S(2)}, u32[]{:S(2)}) collective-permute-start(bf16[1,72,1024]{2,1,0:T(8,128)(2,1)S(1)} %get-tuple-element.95), channel_id=1, source_target_pairs={{0,8},{8,0},{16,24},{24,16},{1,9},{9,1},{17,25},{25,17},{2,10},{10... | collective-permute-start | bytes 442376 | tf_op jit(solution)/shard_map/ppermute | solution.py:529
  54.5 1.2 collective-permute-start.12
  55.6 4.1 %collective-permute-done.3.refs_1_.refs_0_ = bf16[2,72,1024]{2,1,0:T(8,128)(2,1)S(1)} collective-permute-done((bf16[2,72,1024]{2,1,0:T(8,128)(2,1)S(1)}, bf16[2,72,1024]{2,1,0:T(8,128)(2,1)S(1)}, u32[]{:S(2)}, u32[]{:S(2)}) %collective-permute-start.3) | collective-permute-done | bytes 294944 | tf_op jit(solution)/shard_map/ppermute | solution.py:535
  59.8 1.6 %collective-permute-done.8.refs_2_ = bf16[2,72,1024]{2,1,0:T(8,128)(2,1)S(1)} collective-permute-done((bf16[2,72,1024]{2,1,0:T(8,128)(2,1)S(1)}, bf16[2,72,1024]{2,1,0:T(8,128)(2,1)S(1)}, u32[]{:S(2)}, u32[]{:S(2)}) %collective-permute-start.8) | collective-permute-done | bytes 294944 | tf_op jit(solution)/shard_map/ppermute | solution.py:532
  61.4 0.8 collective-permute-done.7.refs_1_
  62.2 2.2 %collective-permute-done.11.refs_3_.refs_4_ = bf16[1,72,1024]{2,1,0:T(8,128)(2,1)S(1)} collective-permute-done((bf16[1,72,1024]{2,1,0:T(8,128)(2,1)S(1)}, bf16[1,72,1024]{2,1,0:T(8,128)(2,1)S(1)}, u32[]{:S(2)}, u32[]{:S(2)}) %collective-permute-start.11) | collective-permute-done | bytes 147488 | tf_op jit(solution)/shard_map/ppermute | solution.py:529
  65.1 0.8 collective-permute-start.14
  65.8 1.6 %collective-permute-start.4 = (bf16[2,72,1024]{2,1,0:T(8,128)(2,1)S(1)}, bf16[2,72,1024]{2,1,0:T(8,128)(2,1)S(1)}, u32[]{:S(2)}, u32[]{:S(2)}) collective-permute-start(bf16[2,72,1024]{2,1,0:T(8,128)(2,1)S(1)} %hold_farthest.1.refs_5_), channel_id=1, source_target_pairs={{0,6},{1,7},{2,4},{3,5},{4,2},{5,3},{6,0},{7,1},{8,14},{9,15},{10,... | collective-permute-start | bytes 884744 | tf_op jit(solution)/shard_map/ppermute | solution.py:535
  67.4 3.2 %up_0.1 = (f32[288,512]{1,0:T(8,128)S(1)}, f32[288,512]{1,0:T(8,128)S(1)}, f32[288,128]{1,0:T(8,128)S(1)}) custom-call(s32[1]{0:T(128)} %bitcast.refs_0_.me, bf16[2,72,1024]{2,1,0:T(8,128)(2,1)S(1)} %get-tuple-element.94.refs_0_, bf16[2,72,1024]{2,1,0:T(8,128)(2,1)S(1)} %collective-permute-done.9.refs_0_.refs_1_, ...), custom_call_target="tpu_custom_call" | custom-call | tf_op jit(solution)/shard_map/up_0/pallas_call | solution.py:282
  70.7 4.5 %collective-permute-done.4.refs_0_ = bf16[2,72,1024]{2,1,0:T(8,128)(2,1)S(1)} collective-permute-done((bf16[2,72,1024]{2,1,0:T(8,128)(2,1)S(1)}, bf16[2,72,1024]{2,1,0:T(8,128)(2,1)S(1)}, u32[]{:S(2)}, u32[]{:S(2)}) %collective-permute-start.4) | collective-permute-done | bytes 294944 | tf_op jit(solution)/shard_map/ppermute | solution.py:535
  76.8 1.5 collective-permute-start.15
  78.3 4.5 %collective-permute-start.18 = (bf16[2,32,1024]{2,1,0:T(8,128)(2,1)S(1)}, bf16[2,32,1024]{2,1,0:T(8,128)(2,1)S(1)}, u32[]{:S(2)}, u32[]{:S(2)}) collective-permute-start(bf16[2,32,1024]{2,1,0:T(8,128)(2,1)S(1)} %get-tuple-element.109), channel_id=1, source_target_pairs={{0,4},{1,5},{2,6},{3,7},{4,0},{5,1},{6,2},{7,3},{8,12},{9,13},{10,... | collective-permute-start | bytes 393224 | tf_op jit(solution)/shard_map/ppermute | solution.py:535
  82.8 1.4 collective-permute-start.19
  84.2 3.2 %up_1.1 = (f32[288,512]{1,0:T(8,128)S(1)}, f32[288,512]{1,0:T(8,128)S(1)}, f32[288,128]{1,0:T(8,128)S(1)}) custom-call(s32[1]{0:T(128)} %bitcast.refs_0_.me, bf16[2,72,1024]{2,1,0:T(8,128)(2,1)S(1)} %near_kernel.1.refs_2_.refs_0_, ...), custom_call_target="tpu_custom_call", output_to_operand_aliasing={{0}: (9, {}), {1}: (10, {}), {2}: (11, {})} | custom-call | tf_op jit(solution)/shard_map/up_1/pallas_call | solution.py:282
  87.4 3.6 %collective-permute-done.18.refs_4_.refs_10_ = bf16[2,32,1024]{2,1,0:T(8,128)(2,1)S(1)} collective-permute-done((bf16[2,32,1024]{2,1,0:T(8,128)(2,1)S(1)}, bf16[2,32,1024]{2,1,0:T(8,128)(2,1)S(1)}, u32[]{:S(2)}, u32[]{:S(2)}) %collective-permute-start.18) | collective-permute-done | bytes 131104 | tf_op jit(solution)/shard_map/ppermute | solution.py:535
  91.5 1.3 collective-permute-start.20
  93.3 3.2 %up_2.1 = (f32[288,512]{1,0:T(8,128)S(1)}, f32[288,512]{1,0:T(8,128)S(1)}, f32[288,128]{1,0:T(8,128)S(1)}) custom-call(s32[1]{0:T(128)} %bitcast.refs_0_.me, bf16[2,72,1024]{2,1,0:T(8,128)(2,1)S(1)} %collective-permute-done.3.refs_1_.refs_0_, ...), custom_call_target="tpu_custom_call", output_to_operand_aliasing={{0}: (9, {}), {1}: (10, {}), {2}: (11, {})} | custom-call | tf_op jit(solution)/shard_map/up_2/pallas_call | solution.py:282
  96.7 1.2 collective-permute-done.21.refs_4_
  97.9 3.5 %up_3.1 = (bf16[72,512]{1,0:T(8,128)(2,1)S(1)}, bf16[216,512]{1,0:T(8,128)(2,1)S(1)}) custom-call(s32[1]{0:T(128)} %bitcast.refs_0_.me, bf16[2,72,1024]{2,1,0:T(8,128)(2,1)S(1)} %collective-permute-done.4.refs_0_, bf16[3,72,1024]{2,1,0:T(8,128)(2,1)S(1)} %collective-permute-done.15.refs_0_.refs_4_.refs_1_, ...), custom_call_target="tpu_custom_call" | custom-call | tf_op jit(solution)/shard_map/up_3/pallas_call | solution.py:282
  101.5 4.1 %down_through.1 = (bf16[9,16,1024]{2,1,0:T(8,128)(2,1)S(1)}, bf16[9,16,1024]{2,1,0:T(8,128)(2,1)S(1)}, bf16[9,16,1024]{2,1,0:T(8,128)(2,1)S(1)}, bf16[9,16,1024]{2,1,0:T(8,128)(2,1)S(1)}) custom-call(bf16[72,512]{1,0:T(8,128)(2,1)S(1)} %get-tuple-element.122.act_ref, bf16[512,8192]{1,0:T(8,128)(2,1)} %bitcast.27), custom_call_target="tpu_custom_call" | custom-call | tf_op jit(solution)/shard_map/down_through/pallas_call | solution.py:372
  106.2 0.9 collective-permute-start.23
  107.1 5.0 %down_rest.1 = (bf16[9,16,1024]{2,1,0:T(8,128)(2,1)S(1)}, bf16[9,16,1024]{2,1,0:T(8,128)(2,1)S(1)}, bf16[9,16,1024]{2,1,0:T(8,128)(2,1)S(1)}, bf16[9,16,1024]{2,...) custom-call(bf16[216,512]{1,0:T(8,128)(2,1)S(1)} %get-tuple-element., ...), custom_call_target="tpu_custom_call" | custom-call | tf_op jit(solution)/shard_map/down_rest/pallas_call | solution.py:372
  112.1 3.4 %collective-permute-done.22.refs_0_ = bf16[9,16,1024]{2,1,0:T(8,128)(2,1)S(1)} collective-permute-done((bf16[9,16,1024]{2,1,0:T(8,128)(2,1)S(1)}, bf16[9,16,1024]{2,1,0:T(8,128)(2,1)S(1)}, u32[]{:S(2)}, u32[]{:S(2)}) %collective-permute-start.22) | collective-permute-done | bytes 294944 | tf_op jit(solution)/shard_map/ppermute | solution.py:529
  116.1 1.7 %collective-permute-start.24 = (bf16[9,16,1024]{2,1,0:T(8,128)(2,1)S(1)}, bf16[9,16,1024]{2,1,0:T(8,128)(2,1)S(1)}, u32[]{:S(2)}, u32[]{:S(2)}) collective-permute-start(bf16[9,16,1024]{2,1,0:T(8,128)(2,1)S(1)} %get-tuple-element.131), channel_id=1, source_target_pairs={{0,8},{8,0},{16,24},{24,16},{1,9},{9,1},{17,25},{25,17},{2,10},{10... | collective-permute-start | bytes 884744 | tf_op jit(solution)/shard_map/ppermute | solution.py:529
  117.8 0.8 collective-permute-start.25
  118.7 1.5 collective-permute-start.29
  120.2 5.8 %collective-permute-done.24.refs_1_ = bf16[9,16,1024]{2,1,0:T(8,128)(2,1)S(1)} collective-permute-done((bf16[9,16,1024]{2,1,0:T(8,128)(2,1)S(1)}, bf16[9,16,1024]{2,1,0:T(8,128)(2,1)S(1)}, u32[]{:S(2)}, u32[]{:S(2)}) %collective-permute-start.24) | collective-permute-done | bytes 294944 | tf_op jit(solution)/shard_map/ppermute | solution.py:529
  126.0 1.7 %collective-permute-done.25.refs_2_ = bf16[9,16,1024]{2,1,0:T(8,128)(2,1)S(1)} collective-permute-done((bf16[9,16,1024]{2,1,0:T(8,128)(2,1)S(1)}, bf16[9,16,1024]{2,1,0:T(8,128)(2,1)S(1)}, u32[]{:S(2)}, u32[]{:S(2)}) %collective-permute-start.25) | collective-permute-done | bytes 294944 | tf_op jit(solution)/shard_map/ppermute | solution.py:532
  128.9 1.8 %collective-permute-start.34 = (bf16[9,16,1024]{2,1,0:T(8,128)(2,1)S(1)}, bf16[9,16,1024]{2,1,0:T(8,128)(2,1)S(1)}, u32[]{:S(2)}, u32[]{:S(2)}) collective-permute-start(bf16[9,16,1024]{2,1,0:T(8,128)(2,1)S(1)} %get-tuple-element.143.refs_6_), channel_id=1, source_target_pairs={{0,6},{1,7},{2,4},{3,5},{4,2},{5,3},{6,0},{7,1},{8,14},{9,15},{10,... | collective-permute-start | bytes 884744 | tf_op jit(solution)/shard_map/ppermute | solution.py:535
  130.6 1.7 %collective-permute-done.28.refs_0_ = bf16[9,16,1024]{2,1,0:T(8,128)(2,1)S(1)} collective-permute-done((bf16[9,16,1024]{2,1,0:T(8,128)(2,1)S(1)}, bf16[9,16,1024]{2,1,0:T(8,128)(2,1)S(1)}, u32[]{:S(2)}, u32[]{:S(2)}) %collective-permute-start.28) | collective-permute-done | bytes 294944 | tf_op jit(solution)/shard_map/ppermute | solution.py:529
  132.4 1.7 %collective-permute-done.29.refs_1_ = bf16[9,16,1024]{2,1,0:T(8,128)(2,1)S(1)} collective-permute-done((bf16[9,16,1024]{2,1,0:T(8,128)(2,1)S(1)}, bf16[9,16,1024]{2,1,0:T(8,128)(2,1)S(1)}, u32[]{:S(2)}, u32[]{:S(2)}) %collective-permute-start.29) | collective-permute-done | bytes 294944 | tf_op jit(solution)/shard_map/ppermute | solution.py:532
  135.2 2.5 %collective-permute-done.26.refs_1_ = bf16[9,16,1024]{2,1,0:T(8,128)(2,1)S(1)} collective-permute-done((bf16[9,16,1024]{2,1,0:T(8,128)(2,1)S(1)}, bf16[9,16,1024]{2,1,0:T(8,128)(2,1)S(1)}, u32[]{:S(2)}, u32[]{:S(2)}) %collective-permute-start.26) | collective-permute-done | bytes 294944 | tf_op jit(solution)/shard_map/ppermute | solution.py:529
  137.8 0.8 collective-permute-done.27.refs_2_
  138.7 1.0 collective-permute-start.30
  139.7 1.0 collective-permute-start.31
  140.7 2.4 %collective-permute-start.36 = (bf16[9,16,1024]{2,1,0:T(8,128)(2,1)S(1)}, bf16[9,16,1024]{2,1,0:T(8,128)(2,1)S(1)}, u32[]{:S(2)}, u32[]{:S(2)}) collective-permute-start(bf16[9,16,1024]{2,1,0:T(8,128)(2,1)S(1)} %get-tuple-element.151), channel_id=1, source_target_pairs={{0,4},{1,5},{2,6},{3,7},{4,0},{5,1},{6,2},{7,3},{8,12},{9,13},{10,... | collective-permute-start | bytes 884744 | tf_op jit(solution)/shard_map/ppermute | solution.py:535
  143.2 1.1 collective-permute-start.35
  144.3 1.2 collective-permute-done.30.refs_1_
  145.5 1.0 collective-permute-done.31.refs_2_
  146.5 5.0 %collective-permute-done.36.refs_2_.refs_6_ = bf16[9,16,1024]{2,1,0:T(8,128)(2,1)S(1)} collective-permute-done((bf16[9,16,1024]{2,1,0:T(8,128)(2,1)S(1)}, bf16[9,16,1024]{2,1,0:T(8,128)(2,1)S(1)}, u32[]{:S(2)}, u32[]{:S(2)}) %collective-permute-start.36) | collective-permute-done | bytes 294944 | tf_op jit(solution)/shard_map/ppermute | solution.py:535
  151.6 2.0 %collective-permute-done.37.refs_3_ = bf16[2,9,16,1024]{3,2,1,0:T(8,128)(2,1)S(1)} collective-permute-done((bf16[2,9,16,1024]{3,2,1,0:T(8,128)(2,1)S(1)}, bf16[2,9,16,1024]{3,2,1,0:T(8,128)(2,1)S(1)}, u32[]{:S(2)}, u32[]{:S(2)}) %collective-permute-start.37) | collective-permute-done | bytes 589856 | tf_op jit(solution)/shard_map/ppermute | solution.py:535
  153.6 1.9 %mix_kernel.1 = bf16[32,8192]{1,0:T(8,128)(2,1)} custom-call(s32[1]{0:T(128)} %bitcast.refs_0_.me, s32[2,32]{1,0:T(2,128)S(1)} %bitcast.17, f32[2,32]{1,0:T(2,128)S(1)} %bitcast.18, bf16[2,9,16,1024]{3,2,1,0:T(8,128)(2,1)S(1)} %collective-permute-done.37.refs_3_, bf16[9,16,1024]{2,1,0:T(8,128)(2,1)S(1)} %finish_0.1.refs_0_.refs_4_, ...), custom_call_target="tpu_custom_call" | custom-call | tf_op jit(solution)/shard_map/mix_kernel/pallas_call | solution.py:39
  (64 shorter events, 9.7 us)
Async XLA Ops:
  4.1 1.0 copy-start
  5.1 1.0 copy-start.5
  6.1 0.7 copy-start.8
  7.9 59.5 %copy-start.4 = (f32[8192]{0:T(1024)S(1)}, f32[8192]{0:T(1024)}, u32[]{:S(2)}) copy-start(f32[8192]{0:T(1024)} %param.24) | copy-start | bytes 98308
  7.9 23.4 %all-to-all-start = ((bf16[8,32,1152]{2,1,0:T(8,128)(2,1)}), bf16[8,32,1152]{2,1,0:T(8,128)(2,1)S(1)}, u32[]{:S(2)}, u32[]{:S(2)}) async-start(bf16[8,32,1152]{2,1,0:T(8,128)(2,1)} %pack_kernel.1), calls=%async_computation | async-start | bytes 1179648 | tf_op jit(solution)/shard_map/all_to_all | solution.py:561
  14.2 9.6 %collective-permute-start = (bf16[144,1024]{1,0:T(8,128)(2,1)}, bf16[144,1024]{1,0:T(8,128)(2,1)S(1)}, u32[]{:S(2)}, u32[]{:S(2)}) collective-permute-start(bf16[144,1024]{1,0:T(8,128)(2,1)} %get-tuple-element.79.refs_2_.refs_1_), channel_id=1, source_target_pairs={{0,8},{8,0},{16,24},{24,16},{1,9},{9,1},{17,25},{25,17},{2,10},{10... | collective-permute-start | bytes 884744 | tf_op jit(solution)/shard_map/ppermute | solution.py:529
  23.8 1.0 copy-start.1
  24.9 10.9 %collective-permute-start.1 = (bf16[128,1024]{1,0:T(8,128)(2,1)S(1)}, bf16[128,1024]{1,0:T(8,128)(2,1)S(1)}, u32[]{:S(2)}, u32[]{:S(2)}) collective-permute-start(bf16[128,1024]{1,0:T(8,128)(2,1)S(1)} %join_kernel.1.refs_6_), channel_id=1, source_target_pairs={{0,16},{8,24},{16,0},{24,8},{1,17},{9,25},{17,1},{25,9},{2,18},{10... | collective-permute-start | bytes 786440 | tf_op jit(solution)/shard_map/ppermute | solution.py:532
  31.2 1.2 copy-start.2
  32.5 1.2 copy-start.3
  33.7 0.9 copy-start.6
  34.6 0.8 copy-start.7
  37.2 2.4 %collective-permute-start.2 = (bf16[4,104,1024]{2,1,0:T(8,128)(2,1)S(1)}, bf16[4,104,1024]{2,1,0:T(8,128)(2,1)S(1)}, u32[]{:S(2)}, u32[]{:S(2)}) collective-permute-start(bf16[4,104,1024]{2,1,0:T(8,128)(2,1)S(1)} %get-tuple-element.89), channel_id=1, source_target_pairs={{0,1},{1,0},{2,3},{3,2},{4,5},{5,4},{6,7},{7,6},{8,9},{9,8},{10,11... | collective-permute-start | bytes 2555912 | tf_op jit(solution)/shard_map/ppermute | solution.py:535
  37.3 7.7 %collective-permute-start.5 = (bf16[72,1024]{1,0:T(8,128)(2,1)S(1)}, bf16[72,1024]{1,0:T(8,128)(2,1)S(1)}, u32[]{:S(2)}, u32[]{:S(2)}) collective-permute-start(bf16[72,1024]{1,0:T(8,128)(2,1)S(1)} %get-tuple-element.92), channel_id=1, source_target_pairs={{0,2},{1,3},{2,0},{3,1},{4,6},{5,7},{6,4},{7,5},{8,10},{9,11},{10,... | collective-permute-start | bytes 442376 | tf_op jit(solution)/shard_map/ppermute | solution.py:535
  39.7 13.1 %collective-permute-start.10 = (bf16[2,72,1024]{2,1,0:T(8,128)(2,1)S(1)}, bf16[2,72,1024]{2,1,0:T(8,128)(2,1)S(1)}, u32[]{:S(2)}, u32[]{:S(2)}) collective-permute-start(bf16[2,72,1024]{2,1,0:T(8,128)(2,1)S(1)} %get-tuple-element.94.refs_0_), channel_id=1, source_target_pairs={{0,16},{8,24},{16,0},{24,8},{1,17},{9,25},{17,1},{25,9},{2,18},{10... | collective-permute-start | bytes 884744 | tf_op jit(solution)/shard_map/ppermute | solution.py:532
  41.1 11.7 %collective-permute-start.9 = (bf16[2,72,1024]{2,1,0:T(8,128)(2,1)S(1)}, bf16[2,72,1024]{2,1,0:T(8,128)(2,1)S(1)}, u32[]{:S(2)}, u32[]{:S(2)}) collective-permute-start(bf16[2,72,1024]{2,1,0:T(8,128)(2,1)S(1)} %get-tuple-element.94.refs_0_), channel_id=1, source_target_pairs={{0,8},{8,0},{16,24},{24,16},{1,9},{9,1},{17,25},{25,17},{2,10},{10... | collective-permute-start | bytes 884744 | tf_op jit(solution)/shard_map/ppermute | solution.py:529
  42.5 8.8 %collective-permute-start.6 = (bf16[72,1024]{1,0:T(8,128)(2,1)S(1)}, bf16[72,1024]{1,0:T(8,128)(2,1)S(1)}, u32[]{:S(2)}, u32[]{:S(2)}) collective-permute-start(bf16[72,1024]{1,0:T(8,128)(2,1)S(1)} %get-tuple-element.93), channel_id=1, source_target_pairs={{0,3},{1,2},{2,1},{3,0},{4,7},{5,6},{6,5},{7,4},{8,11},{9,10},{10,... | collective-permute-start | bytes 442376 | tf_op jit(solution)/shard_map/ppermute | solution.py:535
  42.7 17.1 %collective-permute-start.3 = (bf16[2,72,1024]{2,1,0:T(8,128)(2,1)S(1)}, bf16[2,72,1024]{2,1,0:T(8,128)(2,1)S(1)}, u32[]{:S(2)}, u32[]{:S(2)}) collective-permute-start(bf16[2,72,1024]{2,1,0:T(8,128)(2,1)S(1)} %get-tuple-element.91), channel_id=1, source_target_pairs={{0,4},{1,5},{2,6},{3,7},{4,0},{5,1},{6,2},{7,3},{8,12},{9,13},{10,... | collective-permute-start | bytes 884744 | tf_op jit(solution)/shard_map/ppermute | solution.py:535
  51.4 10.0 %collective-permute-start.8 = (bf16[2,72,1024]{2,1,0:T(8,128)(2,1)S(1)}, bf16[2,72,1024]{2,1,0:T(8,128)(2,1)S(1)}, u32[]{:S(2)}, u32[]{:S(2)}) collective-permute-start(bf16[2,72,1024]{2,1,0:T(8,128)(2,1)S(1)} %near_kernel.1.refs_2_.refs_0_), channel_id=1, source_target_pairs={{0,16},{8,24},{16,0},{24,8},{1,17},{9,25},{17,1},{25,9},{2,18},{10... | collective-permute-start | bytes 884744 | tf_op jit(solution)/shard_map/ppermute | solution.py:532
  52.3 9.9 %collective-permute-start.7 = (bf16[2,72,1024]{2,1,0:T(8,128)(2,1)S(1)}, bf16[2,72,1024]{2,1,0:T(8,128)(2,1)S(1)}, u32[]{:S(2)}, u32[]{:S(2)}) collective-permute-start(bf16[2,72,1024]{2,1,0:T(8,128)(2,1)S(1)} %near_kernel.1.refs_2_.refs_0_), channel_id=1, source_target_pairs={{0,8},{8,0},{16,24},{24,16},{1,9},{9,1},{17,25},{25,17},{2,10},{10... | collective-permute-start | bytes 884744 | tf_op jit(solution)/shard_map/ppermute | solution.py:529
  52.8 11.6 %collective-permute-start.11 = (bf16[1,72,1024]{2,1,0:T(8,128)(2,1)S(1)}, bf16[1,72,1024]{2,1,0:T(8,128)(2,1)S(1)}, u32[]{:S(2)}, u32[]{:S(2)}) collective-permute-start(bf16[1,72,1024]{2,1,0:T(8,128)(2,1)S(1)} %get-tuple-element.95), channel_id=1, source_target_pairs={{0,8},{8,0},{16,24},{24,16},{1,9},{9,1},{17,25},{25,17},{2,10},{10... | collective-permute-start | bytes 442376 | tf_op jit(solution)/shard_map/ppermute | solution.py:529
  54.5 10.0 %collective-permute-start.12 = (bf16[1,72,1024]{2,1,0:T(8,128)(2,1)S(1)}, bf16[1,72,1024]{2,1,0:T(8,128)(2,1)S(1)}, u32[]{:S(2)}, u32[]{:S(2)}) collective-permute-start(bf16[1,72,1024]{2,1,0:T(8,128)(2,1)S(1)} %get-tuple-element.96), channel_id=1, source_target_pairs={{0,16},{8,24},{16,0},{24,8},{1,17},{9,25},{17,1},{25,9},{2,18},{10... | collective-permute-start | bytes 442376 | tf_op jit(solution)/shard_map/ppermute | solution.py:532
  64.5 11.3 %collective-permute-start.13 = (bf16[3,72,1024]{2,1,0:T(8,128)(2,1)S(1)}, bf16[3,72,1024]{2,1,0:T(8,128)(2,1)S(1)}, u32[]{:S(2)}, u32[]{:S(2)}) collective-permute-start(bf16[3,72,1024]{2,1,0:T(8,128)(2,1)S(1)} %get-tuple-element.97), channel_id=1, source_target_pairs={{0,8},{8,0},{16,24},{24,16},{1,9},{9,1},{17,25},{25,17},{2,10},{10... | collective-permute-start | bytes 1327112 | tf_op jit(solution)/shard_map/ppermute | solution.py:529
  65.1 11.0 %collective-permute-start.14 = (bf16[3,72,1024]{2,1,0:T(8,128)(2,1)S(1)}, bf16[3,72,1024]{2,1,0:T(8,128)(2,1)S(1)}, u32[]{:S(2)}, u32[]{:S(2)}) collective-permute-start(bf16[3,72,1024]{2,1,0:T(8,128)(2,1)S(1)} %get-tuple-element.98), channel_id=1, source_target_pairs={{0,16},{8,24},{16,0},{24,8},{1,17},{9,25},{17,1},{25,9},{2,18},{10... | collective-permute-start | bytes 1327112 | tf_op jit(solution)/shard_map/ppermute | solution.py:532
  65.8 9.3 %collective-permute-start.4 = (bf16[2,72,1024]{2,1,0:T(8,128)(2,1)S(1)}, bf16[2,72,1024]{2,1,0:T(8,128)(2,1)S(1)}, u32[]{:S(2)}, u32[]{:S(2)}) collective-permute-start(bf16[2,72,1024]{2,1,0:T(8,128)(2,1)S(1)} %hold_farthest.1.refs_5_), channel_id=1, source_target_pairs={{0,6},{1,7},{2,4},{3,5},{4,2},{5,3},{6,0},{7,1},{8,14},{9,15},{10,... | collective-permute-start | bytes 884744 | tf_op jit(solution)/shard_map/ppermute | solution.py:535
  76.1 15.4 %collective-permute-start.16 = (bf16[3,72,1024]{2,1,0:T(8,128)(2,1)S(1)}, bf16[3,72,1024]{2,1,0:T(8,128)(2,1)S(1)}, u32[]{:S(2)}, u32[]{:S(2)}) collective-permute-start(bf16[3,72,1024]{2,1,0:T(8,128)(2,1)S(1)} %get-tuple-element.101), channel_id=1, source_target_pairs={{0,16},{8,24},{16,0},{24,8},{1,17},{9,25},{17,1},{25,9},{2,18},{10... | collective-permute-start | bytes 1327112 | tf_op jit(solution)/shard_map/ppermute | solution.py:532
  76.8 14.7 %collective-permute-start.15 = (bf16[3,72,1024]{2,1,0:T(8,128)(2,1)S(1)}, bf16[3,72,1024]{2,1,0:T(8,128)(2,1)S(1)}, u32[]{:S(2)}, u32[]{:S(2)}) collective-permute-start(bf16[3,72,1024]{2,1,0:T(8,128)(2,1)S(1)} %get-tuple-element.100.refs_3_), channel_id=1, source_target_pairs={{0,8},{8,0},{16,24},{24,16},{1,9},{9,1},{17,25},{25,17},{2,10},{10... | collective-permute-start | bytes 1327112 | tf_op jit(solution)/shard_map/ppermute | solution.py:529
  78.3 12.6 %collective-permute-start.18 = (bf16[2,32,1024]{2,1,0:T(8,128)(2,1)S(1)}, bf16[2,32,1024]{2,1,0:T(8,128)(2,1)S(1)}, u32[]{:S(2)}, u32[]{:S(2)}) collective-permute-start(bf16[2,32,1024]{2,1,0:T(8,128)(2,1)S(1)} %get-tuple-element.109), channel_id=1, source_target_pairs={{0,4},{1,5},{2,6},{3,7},{4,0},{5,1},{6,2},{7,3},{8,12},{9,13},{10,... | collective-permute-start | bytes 393224 | tf_op jit(solution)/shard_map/ppermute | solution.py:535
  82.8 8.1 %collective-permute-start.19 = (bf16[2,32,1024]{2,1,0:T(8,128)(2,1)S(1)}, bf16[2,32,1024]{2,1,0:T(8,128)(2,1)S(1)}, u32[]{:S(2)}, u32[]{:S(2)}) collective-permute-start(bf16[2,32,1024]{2,1,0:T(8,128)(2,1)S(1)} %get-tuple-element.110), channel_id=1, source_target_pairs={{0,6},{1,7},{2,4},{3,5},{4,2},{5,3},{6,0},{7,1},{8,14},{9,15},{10,... | collective-permute-start | bytes 393224 | tf_op jit(solution)/shard_map/ppermute | solution.py:535
  84.2 7.3 %collective-permute-start.17 = (bf16[2,32,1024]{2,1,0:T(8,128)(2,1)S(1)}, bf16[2,32,1024]{2,1,0:T(8,128)(2,1)S(1)}, u32[]{:S(2)}, u32[]{:S(2)}) collective-permute-start(bf16[2,32,1024]{2,1,0:T(8,128)(2,1)S(1)} %get-tuple-element.107.refs_11_), channel_id=1, source_target_pairs={{0,2},{1,3},{2,0},{3,1},{4,6},{5,7},{6,4},{7,5},{8,10},{9,11},{10,... | collective-permute-start | bytes 393224 | tf_op jit(solution)/shard_map/ppermute | solution.py:535
  91.5 5.2 %collective-permute-start.20 = (bf16[1,72,1024]{2,1,0:T(8,128)(2,1)S(1)}, bf16[1,72,1024]{2,1,0:T(8,128)(2,1)S(1)}, u32[]{:S(2)}, u32[]{:S(2)}) collective-permute-start(bf16[1,72,1024]{2,1,0:T(8,128)(2,1)S(1)} %get-tuple-element.111), channel_id=1, source_target_pairs={{0,16},{8,24},{16,0},{24,8},{1,17},{9,25},{17,1},{25,9},{2,18},{10... | collective-permute-start | bytes 442376 | tf_op jit(solution)/shard_map/ppermute | solution.py:532
  92.8 5.1 %collective-permute-start.21 = (bf16[1,72,1024]{2,1,0:T(8,128)(2,1)S(1)}, bf16[1,72,1024]{2,1,0:T(8,128)(2,1)S(1)}, u32[]{:S(2)}, u32[]{:S(2)}) collective-permute-start(bf16[1,72,1024]{2,1,0:T(8,128)(2,1)S(1)} %get-tuple-element.112), channel_id=1, source_target_pairs={{0,8},{8,0},{16,24},{24,16},{1,9},{9,1},{17,25},{25,17},{2,10},{10... | collective-permute-start | bytes 442376 | tf_op jit(solution)/shard_map/ppermute | solution.py:529
  105.6 9.9 %collective-permute-start.22 = (bf16[9,16,1024]{2,1,0:T(8,128)(2,1)S(1)}, bf16[9,16,1024]{2,1,0:T(8,128)(2,1)S(1)}, u32[]{:S(2)}, u32[]{:S(2)}) collective-permute-start(bf16[9,16,1024]{2,1,0:T(8,128)(2,1)S(1)} %get-tuple-element.123), channel_id=1, source_target_pairs={{0,8},{8,0},{16,24},{24,16},{1,9},{9,1},{17,25},{25,17},{2,10},{10... | collective-permute-start | bytes 884744 | tf_op jit(solution)/shard_map/ppermute | solution.py:529
  106.2 9.7 %collective-permute-start.23 = (bf16[9,16,1024]{2,1,0:T(8,128)(2,1)S(1)}, bf16[9,16,1024]{2,1,0:T(8,128)(2,1)S(1)}, u32[]{:S(2)}, u32[]{:S(2)}) collective-permute-start(bf16[9,16,1024]{2,1,0:T(8,128)(2,1)S(1)} %get-tuple-element.124), channel_id=1, source_target_pairs={{0,16},{8,24},{16,0},{24,8},{1,17},{9,25},{17,1},{25,9},{2,18},{10... | collective-permute-start | bytes 884744 | tf_op jit(solution)/shard_map/ppermute | solution.py:532
  107.1 46.6 %copy-start.9 = (s32[32,2]{0,1:T(2,128)S(1)}, s32[32,2]{0,1:T(2,128)}, u32[]{:S(2)}) copy-start(s32[32,2]{0,1:T(2,128)} %param.25) | copy-start | bytes 772
  107.1 46.6 %copy-start.10 = (f32[32,2]{0,1:T(2,128)S(1)}, f32[32,2]{0,1:T(2,128)}, u32[]{:S(2)}) copy-start(f32[32,2]{0,1:T(2,128)} %param.26) | copy-start | bytes 772
  116.1 9.9 %collective-permute-start.24 = (bf16[9,16,1024]{2,1,0:T(8,128)(2,1)S(1)}, bf16[9,16,1024]{2,1,0:T(8,128)(2,1)S(1)}, u32[]{:S(2)}, u32[]{:S(2)}) collective-permute-start(bf16[9,16,1024]{2,1,0:T(8,128)(2,1)S(1)} %get-tuple-element.131), channel_id=1, source_target_pairs={{0,8},{8,0},{16,24},{24,16},{1,9},{9,1},{17,25},{25,17},{2,10},{10... | collective-permute-start | bytes 884744 | tf_op jit(solution)/shard_map/ppermute | solution.py:529
  117.8 9.9 %collective-permute-start.25 = (bf16[9,16,1024]{2,1,0:T(8,128)(2,1)S(1)}, bf16[9,16,1024]{2,1,0:T(8,128)(2,1)S(1)}, u32[]{:S(2)}, u32[]{:S(2)}) collective-permute-start(bf16[9,16,1024]{2,1,0:T(8,128)(2,1)S(1)} %get-tuple-element.132), channel_id=1, source_target_pairs={{0,16},{8,24},{16,0},{24,8},{1,17},{9,25},{17,1},{25,9},{2,18},{10... | collective-permute-start | bytes 884744 | tf_op jit(solution)/shard_map/ppermute | solution.py:532
  118.6 13.8 %collective-permute-start.28 = (bf16[9,16,1024]{2,1,0:T(8,128)(2,1)S(1)}, bf16[9,16,1024]{2,1,0:T(8,128)(2,1)S(1)}, u32[]{:S(2)}, u32[]{:S(2)}) collective-permute-start(bf16[9,16,1024]{2,1,0:T(8,128)(2,1)S(1)} %get-tuple-element.137), channel_id=1, source_target_pairs={{0,8},{8,0},{16,24},{24,16},{1,9},{9,1},{17,25},{25,17},{2,10},{10... | collective-permute-start | bytes 884744 | tf_op jit(solution)/shard_map/ppermute | solution.py:529
  118.7 15.3 %collective-permute-start.29 = (bf16[9,16,1024]{2,1,0:T(8,128)(2,1)S(1)}, bf16[9,16,1024]{2,1,0:T(8,128)(2,1)S(1)}, u32[]{:S(2)}, u32[]{:S(2)}) collective-permute-start(bf16[9,16,1024]{2,1,0:T(8,128)(2,1)S(1)} %get-tuple-element.138), channel_id=1, source_target_pairs={{0,16},{8,24},{16,0},{24,8},{1,17},{9,25},{17,1},{25,9},{2,18},{10... | collective-permute-start | bytes 884744 | tf_op jit(solution)/shard_map/ppermute | solution.py:532
  127.8 9.9 %collective-permute-start.26 = (bf16[9,16,1024]{2,1,0:T(8,128)(2,1)S(1)}, bf16[9,16,1024]{2,1,0:T(8,128)(2,1)S(1)}, u32[]{:S(2)}, u32[]{:S(2)}) collective-permute-start(bf16[9,16,1024]{2,1,0:T(8,128)(2,1)S(1)} %get-tuple-element.135), channel_id=1, source_target_pairs={{0,8},{8,0},{16,24},{24,16},{1,9},{9,1},{17,25},{25,17},{2,10},{10... | collective-permute-start | bytes 884744 | tf_op jit(solution)/shard_map/ppermute | solution.py:529
  128.3 10.2 %collective-permute-start.27 = (bf16[9,16,1024]{2,1,0:T(8,128)(2,1)S(1)}, bf16[9,16,1024]{2,1,0:T(8,128)(2,1)S(1)}, u32[]{:S(2)}, u32[]{:S(2)}) collective-permute-start(bf16[9,16,1024]{2,1,0:T(8,128)(2,1)S(1)} %get-tuple-element.136), channel_id=1, source_target_pairs={{0,16},{8,24},{16,0},{24,8},{1,17},{9,25},{17,1},{25,9},{2,18},{10... | collective-permute-start | bytes 884744 | tf_op jit(solution)/shard_map/ppermute | solution.py:532
  128.9 11.9 %collective-permute-start.34 = (bf16[9,16,1024]{2,1,0:T(8,128)(2,1)S(1)}, bf16[9,16,1024]{2,1,0:T(8,128)(2,1)S(1)}, u32[]{:S(2)}, u32[]{:S(2)}) collective-permute-start(bf16[9,16,1024]{2,1,0:T(8,128)(2,1)S(1)} %get-tuple-element.143.refs_6_), channel_id=1, source_target_pairs={{0,6},{1,7},{2,4},{3,5},{4,2},{5,3},{6,0},{7,1},{8,14},{9,15},{10,... | collective-permute-start | bytes 884744 | tf_op jit(solution)/shard_map/ppermute | solution.py:535
  134.2 8.9 %collective-permute-start.32 = (bf16[9,16,1024]{2,1,0:T(8,128)(2,1)S(1)}, bf16[9,16,1024]{2,1,0:T(8,128)(2,1)S(1)}, u32[]{:S(2)}, u32[]{:S(2)}) collective-permute-start(bf16[9,16,1024]{2,1,0:T(8,128)(2,1)S(1)} %get-tuple-element.149), channel_id=1, source_target_pairs={{0,8},{8,0},{16,24},{24,16},{1,9},{9,1},{17,25},{25,17},{2,10},{10... | collective-permute-start | bytes 884744 | tf_op jit(solution)/shard_map/ppermute | solution.py:529
  134.6 8.4 %collective-permute-start.33 = (bf16[9,16,1024]{2,1,0:T(8,128)(2,1)S(1)}, bf16[9,16,1024]{2,1,0:T(8,128)(2,1)S(1)}, u32[]{:S(2)}, u32[]{:S(2)}) collective-permute-start(bf16[9,16,1024]{2,1,0:T(8,128)(2,1)S(1)} %get-tuple-element.150), channel_id=1, source_target_pairs={{0,16},{8,24},{16,0},{24,8},{1,17},{9,25},{17,1},{25,9},{2,18},{10... | collective-permute-start | bytes 884744 | tf_op jit(solution)/shard_map/ppermute | solution.py:532
  138.7 6.8 %collective-permute-start.30 = (bf16[9,16,1024]{2,1,0:T(8,128)(2,1)S(1)}, bf16[9,16,1024]{2,1,0:T(8,128)(2,1)S(1)}, u32[]{:S(2)}, u32[]{:S(2)}) collective-permute-start(bf16[9,16,1024]{2,1,0:T(8,128)(2,1)S(1)} %get-tuple-element.146), channel_id=1, source_target_pairs={{0,8},{8,0},{16,24},{24,16},{1,9},{9,1},{17,25},{25,17},{2,10},{10... | collective-permute-start | bytes 884744 | tf_op jit(solution)/shard_map/ppermute | solution.py:529
  139.7 6.7 %collective-permute-start.31 = (bf16[9,16,1024]{2,1,0:T(8,128)(2,1)S(1)}, bf16[9,16,1024]{2,1,0:T(8,128)(2,1)S(1)}, u32[]{:S(2)}, u32[]{:S(2)}) collective-permute-start(bf16[9,16,1024]{2,1,0:T(8,128)(2,1)S(1)} %get-tuple-element.147), channel_id=1, source_target_pairs={{0,16},{8,24},{16,0},{24,8},{1,17},{9,25},{17,1},{25,9},{2,18},{10... | collective-permute-start | bytes 884744 | tf_op jit(solution)/shard_map/ppermute | solution.py:532
  140.7 10.8 %collective-permute-start.36 = (bf16[9,16,1024]{2,1,0:T(8,128)(2,1)S(1)}, bf16[9,16,1024]{2,1,0:T(8,128)(2,1)S(1)}, u32[]{:S(2)}, u32[]{:S(2)}) collective-permute-start(bf16[9,16,1024]{2,1,0:T(8,128)(2,1)S(1)} %get-tuple-element.151), channel_id=1, source_target_pairs={{0,4},{1,5},{2,6},{3,7},{4,0},{5,1},{6,2},{7,3},{8,12},{9,13},{10,... | collective-permute-start | bytes 884744 | tf_op jit(solution)/shard_map/ppermute | solution.py:535
  143.2 8.3 %collective-permute-start.35 = (bf16[9,16,1024]{2,1,0:T(8,128)(2,1)S(1)}, bf16[9,16,1024]{2,1,0:T(8,128)(2,1)S(1)}, u32[]{:S(2)}, u32[]{:S(2)}) collective-permute-start(bf16[9,16,1024]{2,1,0:T(8,128)(2,1)S(1)} %finish_1.1), channel_id=1, source_target_pairs={{0,2},{1,3},{2,0},{3,1},{4,6},{5,7},{6,4},{7,5},{8,10},{9,11},{10,... | collective-permute-start | bytes 884744 | tf_op jit(solution)/shard_map/ppermute | solution.py:535
  151.6 2.1 %collective-permute-start.37 = (bf16[2,9,16,1024]{3,2,1,0:T(8,128)(2,1)S(1)}, bf16[2,9,16,1024]{3,2,1,0:T(8,128)(2,1)S(1)}, u32[]{:S(2)}, u32[]{:S(2)}) collective-permute-start(bf16[2,9,16,1024]{3,2,1,0:T(8,128)(2,1)S(1)} %second_kernel.1), channel_id=1, source_target_pairs={{0,1},{1,0},{2,3},{3,2},{4,5},{5,4},{6,7},{7,6},{8,9},{9,8},{10,11... | collective-permute-start | bytes 1769480 | tf_op jit(solution)/shard_map/ppermute | solution.py:535

commit v2 on v1

--- a/solution.py
+++ b/solution.py
@@ -197,9 +197,10 @@
     tokens, channels = mixer.shape
     residual = res_ref[:, :, 0:channels].astype(F32).reshape(tokens, channels)
     stream = (residual + mixer).astype(BF16)
-    owned = sel_ref.shape[1] - near_a_ref.shape[0]
-    near_a_ref[...] = dot(sel_ref[2, owned:, :], stream).astype(BF16)
-    near_b_ref[...] = dot(sel_ref[3, owned:, :], stream).astype(BF16)
+    owned = stream.shape[0] // sel_ref.shape[0]
+    slots = sel_ref.shape[1] - owned
+    near_a_ref[0:slots, :] = dot(sel_ref[2, owned:, :], stream).astype(BF16)
+    near_b_ref[0:slots, :] = dot(sel_ref[3, owned:, :], stream).astype(BF16)
     for at, k in enumerate((0, 2, 3, 1)):
         same_ref[at] = dot(sel_ref[2 * k], stream).astype(BF16)
         other_ref[at] = dot(sel_ref[2 * k + 1], stream).astype(BF16)
@@ -390,16 +391,17 @@
 
 
 def pair_kernel(same, other, own_stream, own, far_stream, far, last_stream, last, near_stream):
-    owned = own_stream.shape[1]
+    owned = same.shape[1] - own.shape[1]
     for side, rows in enumerate((same, other)):
-        own_stream[side], own[side] = rows[0, 0:owned, :], rows[0, owned:, :]
-        far_stream[side], far[side] = rows[1, 0:owned, :], rows[1, owned:, :]
-        last_stream[side], last[side] = rows[2, 0:owned, :], rows[2, owned:, :]
-        near_stream[side] = rows[3, 0:owned, :]
+        own_stream[side, 0:owned, :], own[side] = rows[0, 0:owned, :], rows[0, owned:, :]
+        far_stream[side, 0:owned, :], far[side] = rows[1, 0:owned, :], rows[1, owned:, :]
+        last_stream[side, 0:owned, :], last[side] = rows[2, 0:owned, :], rows[2, owned:, :]
+        near_stream[side, 0:owned, :] = rows[3, 0:owned, :]
 
 
 def near_kernel(same, other, rows):
-    rows[0], rows[1] = same[...], other[...]
+    slots = rows.shape[1]
+    rows[0], rows[1] = same[0:slots, :], other[0:slots, :]
 
 
 def second_kernel(*refs):
@@ -489,7 +491,7 @@
         high = coef.astype(BF16)
         low = (coef - high.astype(F32)).astype(BF16)
         data = jnp.concatenate(rows_of(k) + last, axis=0).astype(BF16)
-        stream = streams[m // 2][m % 2].astype(F32)
+        stream = streams[m // 2][m % 2, 0:rows, :].astype(F32)
         out_ref[:, pl.ds(pl.multiple_of(k * tile, 128), tile)] = (
             stream + (dot(high, data) + dot(low, data))
         ).astype(BF16)
@@ -537,6 +539,15 @@
     rate_row = rate[None, :]
     dt_t = dt_step.T
     ids_t = expert_ids.T
+    packed = block_call(
+        pack_kernel,
+        [jax.ShapeDtypeStruct((owners, rows, channels + 128), BF16)],
+        0,
+        (ids_t, residual),
+        held=2,
+        limit=48,
+    )[0]
+    packed = lax.all_to_all(packed, "exp", split_axis=0, concat_axis=0, tiled=True)
     payload, init_t = block_call(
         state_kernel,
         [
@@ -549,16 +560,6 @@
         limit=62,
     )
     pair = over_x(payload)
-    packed = block_call(
-        pack_kernel,
-        [jax.ShapeDtypeStruct((owners, rows, channels + 128), BF16)],
-        0,
-        (ids_t, residual),
-        held=2,
-        after=(payload,),
-        limit=48,
-    )[0]
-    packed = lax.all_to_all(packed, "exp", split_axis=0, concat_axis=0, tiled=True)
     own_part, fade, token = block_call(
         intra_kernel,
         [
@@ -576,6 +577,7 @@
         [jax.ShapeDtypeStruct((state, channels), BF16)],
         1,
         (place, payload, pair),
+        after=(token,),
     )[0]
     early = over_y(joined)
     handed = (own_part, fade, c_out, init_t)
@@ -589,7 +591,7 @@
     )
     groups = owners // 2
     lanes = jax.ShapeDtypeStruct((groups, rows + slots, channels), BF16)
-    one = jax.ShapeDtypeStruct((slots, channels), BF16)
+    one = jax.ShapeDtypeStruct((slots + 8, channels), BF16)
     near_a, near_b, same, other = block_call(
         stream_kernel,
         [one, one, lanes, lanes],
@@ -601,7 +603,7 @@
     wg = w_gate.reshape(owners, channels, w_gate.shape[2])
     wu = w_up.reshape(owners, channels, w_up.shape[2])
     expert_rows = jax.ShapeDtypeStruct((2, slots, channels), BF16)
-    stream_rows = jax.ShapeDtypeStruct((2, rows, channels), BF16)
+    stream_rows = jax.ShapeDtypeStruct((2, 40, channels), BF16)
     near_a, near_b = along(near_a, 2), along(near_b, 3)
     stream0, first, stream2, far, stream3, farthest, stream1 = block_call(
         pair_kernel,
@@ -655,10 +657,10 @@
     stream1, stream2, stream3 = (along(v, 2 * g + 2) for g, v in enumerate(held))
     carry = project(1, [(near, 0), (rx1, 0), (ry1, 0)], [(ry2, 2), (rx2, 2)], carry, held[:1])
     to_x, to_y = block_call(
-        half_message_kernel, message(1), 0, (rx3, ry3), after=(carry[2], stream1, stream2, stream3), name="half_3"
+        half_message_kernel, message(1), 0, (rx3, ry3), after=(carry[2],), name="half_3"
     )
     fx3, fy3 = over_x(to_x), over_y(to_y)
-    carry = project(2, [(far, 0), (rx2, 0), (ry2, 0)], [(ry3, 2), (rx3, 2)], carry)
+    carry = project(2, [(far, 0), (rx2, 0), (ry2, 0)], [(ry3, 2), (rx3, 2)], carry, (stream1, stream2, stream3))
     active_far, active = project(
         3, [(farthest, 0), (rx3, 0), (ry3, 0)], [(fy3, 0), (fx3, 0)], carry
     )

time: 156 us -> 156 us (level)
  waiting for transfers between devices: 62 us -> 52.2 us
  starting transfers between devices: 48.4 us -> 57.7 us
    ppermute x13, waiting for transfers between devices: 27.7 us -> 18.8 us  [over_x(): return lax.ppermute(v, 'seq', [(i, i ^ 1) for i in range(4)])]
    ppermute x13, starting transfers between devices: 12 us -> 16.3 us  [over_x(): return lax.ppermute(v, 'seq', [(i, i ^ 1) for i in range(4)])]
    ppermute x12, starting transfers between devices: 17 us -> 21 us  [along(): return lax.ppermute(v, 'exp', [(i, i ^ mask) for i in range(owners)])]
    ppermute x12, waiting for transfers between devices: 26.7 us -> 24.9 us  [along(): return lax.ppermute(v, 'exp', [(i, i ^ mask) for i in range(owners)])]
  transfers between devices with their start and end apart: 39 -> 39, of which waited for: 26 -> 23; matrix products, arithmetic and copies ran while one was open for 0% -> 0% of each run, Pallas kernels for 13% -> 16%
where the time goes in v2:
time: 156 us; the launch traced here: 155 us
  starting transfers between devices  57.7 us (37%)
  waiting for transfers between devices  52.2 us (33%)
  Pallas kernels  37.3 us (24%)
  local copies, waits for them, and re-layouts  7.61 us (5%)
    ppermute x12, waiting for transfers between devices, along(): return lax.ppermute(v, 'exp', [(i, i ^ mask) for i in range(owners)])  24.9 us
    ppermute x12, starting transfers between devices, along(): return lax.ppermute(v, 'exp', [(i, i ^ mask) for i in range(owners)])  21 us
    ppermute x13, waiting for transfers between devices, over_x(): return lax.ppermute(v, 'seq', [(i, i ^ 1) for i in range(4)])  18.8 us
    ppermute x13, starting transfers between devices, over_x(): return lax.ppermute(v, 'seq', [(i, i ^ 1) for i in range(4)])  16.3 us
    pallas_call x22, Pallas kernels, block_call(): pl.pallas_call(kernel, name=name or getattr(body, 'func', body).__name__,...  14.8 us
    ppermute x13, starting transfers between devices, over_y(): return lax.ppermute(v, 'seq', [(i, i ^ 2) for i in range(4)])  14.2 us
    pallas_call x4, Pallas kernels, up_project(): pl.pallas_call(functools.partial(up_kernel, carry is None, features, len(...  13.2 us
    pallas_call x2, Pallas kernels, down_project(): pl.pallas_call(functools.partial(down_kernel, groups), name=name, grid=(8...  9.3 us
  transfers between devices with their start and end apart: 39, of which 23 were waited for; matrix products, arithmetic and copies ran while one was open for 0% of the time, Pallas kernels for 16%

profile of v2, /device:TPU:0, one launch (start us, length us, event | category | flops | bytes accessed | tf_op | source)
XLA Modules:
  0.0 155.0 jit_solution(15846315782385842151)
XLA Ops:
  0.0 1.0 copy-done.3
  1.7 1.0 pack_kernel.1
  2.8 6.3 %all-to-all-start = ((bf16[8,32,1152]{2,1,0:T(8,128)(2,1)}), bf16[8,32,1152]{2,1,0:T(8,128)(2,1)S(1)}, u32[]{:S(2)}, u32[]{:S(2)}) async-start(bf16[8,32,1152]{2,1,0:T(8,128)(2,1)} %pack_kernel.1), calls=%async_computation | async-start | bytes 1179648 | tf_op jit(solution)/shard_map/all_to_all | solution.py:550
  9.1 4.1 %state_kernel.1 = (bf16[144,1024]{1,0:T(8,128)(2,1)}, bf16[128,1024]{1,0:T(8,128)(2,1)}) custom-call(s32[1]{0:T(128)} %bitcast.3.refs_0_, bf16[256,1024]{1,0:T(8,128)(2,1)} %refs_1_.5, bf16[256,128]{1,0:T(8,128)(2,1)} %refs_2_.3, f32[16,256]{1,0:T(8,128)} %bitcast.30, f32[1,16]{1,0:T(1,128)} %bitcast.32, f32[1024,128]{1,0:T(8,128)} %bitcast.29), custom_call_target="tpu_custom_call" | custom-call | tf_op jit(solution)/shard_map/state_kernel/pallas_call | solution.py:39
  13.2 1.6 %collective-permute-start = (bf16[144,1024]{1,0:T(8,128)(2,1)}, bf16[144,1024]{1,0:T(8,128)(2,1)S(1)}, u32[]{:S(2)}, u32[]{:S(2)}) collective-permute-start(bf16[144,1024]{1,0:T(8,128)(2,1)} %get-tuple-element.83.refs_1_), channel_id=1, source_target_pairs={{0,8},{8,0},{16,24},{24,16},{1,9},{9,1},{17,25},{25,17},{2,10},{10... | collective-permute-start | bytes 884744 | tf_op jit(solution)/shard_map/ppermute | solution.py:531
  14.8 4.7 %intra_kernel.1 = (f32[256,1024]{1,0:T(8,128)}, f32[256,1024]{1,0:T(8,128)}, f32[8,128]{1,0:T(8,128)}) custom-call(bf16[256,1024]{1,0:T(8,128)(2,1)} %refs_1_.5, bf16[256,1024]{1,0:T(8,128)(2,1)} %refs_1_.4, bf16[256,128]{1,0:T(8,128)(2,1)} %refs_2_.3, bf16[256,128]{1,0:T(8,128)(2,1)} %refs_4_.1, f32[16,256]{1,0:T(8,128)} %bitcast.31, f32[1,16]{1,0:T(1,128)} %bitcast.33, ...), custom_call_target="tpu_custom_call" | custom-call | tf_op jit(solution)/shard_map/intra_kernel/pallas_call | solution.py:39
  19.5 3.4 %collective-permute-done.refs_2_.refs_5_ = bf16[144,1024]{1,0:T(8,128)(2,1)S(1)} collective-permute-done((bf16[144,1024]{1,0:T(8,128)(2,1)}, bf16[144,1024]{1,0:T(8,128)(2,1)S(1)}, u32[]{:S(2)}, u32[]{:S(2)}) %collective-permute-start) | collective-permute-done | bytes 294944 | tf_op jit(solution)/shard_map/ppermute | solution.py:531
  22.9 1.0 copy-done.4
  24.7 1.6 %collective-permute-start.1 = (bf16[128,1024]{1,0:T(8,128)(2,1)S(1)}, bf16[128,1024]{1,0:T(8,128)(2,1)S(1)}, u32[]{:S(2)}, u32[]{:S(2)}) collective-permute-start(bf16[128,1024]{1,0:T(8,128)(2,1)S(1)} %join_kernel.1.refs_6_), channel_id=1, source_target_pairs={{0,16},{8,24},{16,0},{24,8},{1,17},{9,25},{17,1},{25,9},{2,18},{10... | collective-permute-start | bytes 786440 | tf_op jit(solution)/shard_map/ppermute | solution.py:534
  26.3 1.2 copy-done
  27.5 1.2 copy-done.1
  28.8 0.9 copy-done.5
  29.7 0.8 copy-done.6
  30.9 1.8 %collective-permute-done.1.refs_6_ = bf16[128,1024]{1,0:T(8,128)(2,1)S(1)} collective-permute-done((bf16[128,1024]{1,0:T(8,128)(2,1)S(1)}, bf16[128,1024]{1,0:T(8,128)(2,1)S(1)}, u32[]{:S(2)}, u32[]{:S(2)}) %collective-permute-start.1) | collective-permute-done | bytes 262176 | tf_op jit(solution)/shard_map/ppermute | solution.py:534
  32.7 1.3 stream_kernel.1
  34.1 1.3 collective-permute-start.5
  36.6 1.6 %collective-permute-start.10 = (bf16[2,72,1024]{2,1,0:T(8,128)(2,1)S(1)}, bf16[2,72,1024]{2,1,0:T(8,128)(2,1)S(1)}, u32[]{:S(2)}, u32[]{:S(2)}) collective-permute-start(bf16[2,72,1024]{2,1,0:T(8,128)(2,1)S(1)} %get-tuple-element.96.refs_0_), channel_id=1, source_target_pairs={{0,16},{8,24},{16,0},{24,8},{1,17},{9,25},{17,1},{25,9},{2,18},{10... | collective-permute-start | bytes 884744 | tf_op jit(solution)/shard_map/ppermute | solution.py:534
  38.2 1.5 collective-permute-start.9
  39.6 2.2 %collective-permute-start.3 = (bf16[2,72,1024]{2,1,0:T(8,128)(2,1)S(1)}, bf16[2,72,1024]{2,1,0:T(8,128)(2,1)S(1)}, u32[]{:S(2)}, u32[]{:S(2)}) collective-permute-start(bf16[2,72,1024]{2,1,0:T(8,128)(2,1)S(1)} %get-tuple-element.93), channel_id=1, source_target_pairs={{0,4},{1,5},{2,6},{3,7},{4,0},{5,1},{6,2},{7,3},{8,12},{9,13},{10,... | collective-permute-start | bytes 884744 | tf_op jit(solution)/shard_map/ppermute | solution.py:537
  41.8 5.2 %collective-permute-done.6.refs_1_ = bf16[80,1024]{1,0:T(8,128)(2,1)S(1)} collective-permute-done((bf16[80,1024]{1,0:T(8,128)(2,1)S(1)}, bf16[80,1024]{1,0:T(8,128)(2,1)S(1)}, u32[]{:S(2)}, u32[]{:S(2)}) %collective-permute-start.6) | collective-permute-done | bytes 163872 | tf_op jit(solution)/shard_map/ppermute | solution.py:537
  47.0 2.6 %collective-permute-start.8 = (bf16[2,72,1024]{2,1,0:T(8,128)(2,1)S(1)}, bf16[2,72,1024]{2,1,0:T(8,128)(2,1)S(1)}, u32[]{:S(2)}, u32[]{:S(2)}) collective-permute-start(bf16[2,72,1024]{2,1,0:T(8,128)(2,1)S(1)} %near_kernel.1.refs_2_.refs_0_), channel_id=1, source_target_pairs={{0,16},{8,24},{16,0},{24,8},{1,17},{9,25},{17,1},{25,9},{2,18},{10... | collective-permute-start | bytes 884744 | tf_op jit(solution)/shard_map/ppermute | solution.py:534
  49.6 2.3 %collective-permute-start.7 = (bf16[2,72,1024]{2,1,0:T(8,128)(2,1)S(1)}, bf16[2,72,1024]{2,1,0:T(8,128)(2,1)S(1)}, u32[]{:S(2)}, u32[]{:S(2)}) collective-permute-start(bf16[2,72,1024]{2,1,0:T(8,128)(2,1)S(1)} %near_kernel.1.refs_2_.refs_0_), channel_id=1, source_target_pairs={{0,8},{8,0},{16,24},{24,16},{1,9},{9,1},{17,25},{25,17},{2,10},{10... | collective-permute-start | bytes 884744 | tf_op jit(solution)/shard_map/ppermute | solution.py:531
  52.2 3.2 %collective-permute-done.3.refs_1_.refs_0_ = bf16[2,72,1024]{2,1,0:T(8,128)(2,1)S(1)} collective-permute-done((bf16[2,72,1024]{2,1,0:T(8,128)(2,1)S(1)}, bf16[2,72,1024]{2,1,0:T(8,128)(2,1)S(1)}, u32[]{:S(2)}, u32[]{:S(2)}) %collective-permute-start.3) | collective-permute-done | bytes 294944 | tf_op jit(solution)/shard_map/ppermute | solution.py:537
  55.4 2.1 %collective-permute-done.8.refs_2_ = bf16[2,72,1024]{2,1,0:T(8,128)(2,1)S(1)} collective-permute-done((bf16[2,72,1024]{2,1,0:T(8,128)(2,1)S(1)}, bf16[2,72,1024]{2,1,0:T(8,128)(2,1)S(1)}, u32[]{:S(2)}, u32[]{:S(2)}) %collective-permute-start.8) | collective-permute-done | bytes 294944 | tf_op jit(solution)/shard_map/ppermute | solution.py:534
  57.5 2.3 %collective-permute-done.7.refs_1_ = bf16[2,72,1024]{2,1,0:T(8,128)(2,1)S(1)} collective-permute-done((bf16[2,72,1024]{2,1,0:T(8,128)(2,1)S(1)}, bf16[2,72,1024]{2,1,0:T(8,128)(2,1)S(1)}, u32[]{:S(2)}, u32[]{:S(2)}) %collective-permute-start.7) | collective-permute-done | bytes 294944 | tf_op jit(solution)/shard_map/ppermute | solution.py:531
  59.7 2.9 %collective-permute-done.11.refs_3_.refs_4_ = bf16[1,72,1024]{2,1,0:T(8,128)(2,1)S(1)} collective-permute-done((bf16[1,72,1024]{2,1,0:T(8,128)(2,1)S(1)}, bf16[1,72,1024]{2,1,0:T(8,128)(2,1)S(1)}, u32[]{:S(2)}, u32[]{:S(2)}) %collective-permute-start.11) | collective-permute-done | bytes 147488 | tf_op jit(solution)/shard_map/ppermute | solution.py:531
  62.7 1.8 %collective-permute-start.13 = (bf16[3,72,1024]{2,1,0:T(8,128)(2,1)S(1)}, bf16[3,72,1024]{2,1,0:T(8,128)(2,1)S(1)}, u32[]{:S(2)}, u32[]{:S(2)}) collective-permute-start(bf16[3,72,1024]{2,1,0:T(8,128)(2,1)S(1)} %get-tuple-element.99), channel_id=1, source_target_pairs={{0,8},{8,0},{16,24},{24,16},{1,9},{9,1},{17,25},{25,17},{2,10},{10... | collective-permute-start | bytes 1327112 | tf_op jit(solution)/shard_map/ppermute | solution.py:531
  64.8 1.5 collective-permute-start.4
  66.4 3.3 %up_0.1 = (f32[288,512]{1,0:T(8,128)S(1)}, f32[288,512]{1,0:T(8,128)S(1)}, f32[288,128]{1,0:T(8,128)S(1)}) custom-call(s32[1]{0:T(128)} %bitcast.refs_0_.me, bf16[2,72,1024]{2,1,0:T(8,128)(2,1)S(1)} %get-tuple-element.96.refs_0_, bf16[2,72,1024]{2,1,0:T(8,128)(2,1)S(1)} %collective-permute-done.9.refs_0_.refs_1_, ...), custom_call_target="tpu_custom_call" | custom-call | tf_op jit(solution)/shard_map/up_0/pallas_call | solution.py:283
  69.6 5.2 %collective-permute-done.4.refs_0_ = bf16[2,72,1024]{2,1,0:T(8,128)(2,1)S(1)} collective-permute-done((bf16[2,72,1024]{2,1,0:T(8,128)(2,1)S(1)}, bf16[2,72,1024]{2,1,0:T(8,128)(2,1)S(1)}, u32[]{:S(2)}, u32[]{:S(2)}) %collective-permute-start.4) | collective-permute-done | bytes 294944 | tf_op jit(solution)/shard_map/ppermute | solution.py:537
  74.9 0.9 collective-permute-done.14.refs_2_.refs_3_
  75.8 0.7 collective-permute-start.16
  77.1 2.6 %collective-permute-start.20 = (bf16[2,40,1024]{2,1,0:T(8,128)(2,1)S(1)}, bf16[2,40,1024]{2,1,0:T(8,128)(2,1)S(1)}, u32[]{:S(2)}, u32[]{:S(2)}) collective-permute-start(bf16[2,40,1024]{2,1,0:T(8,128)(2,1)S(1)} %get-tuple-element.115), channel_id=1, source_target_pairs={{0,4},{1,5},{2,6},{3,7},{4,0},{5,1},{6,2},{7,3},{8,12},{9,13},{10,... | collective-permute-start | bytes 491528 | tf_op jit(solution)/shard_map/ppermute | solution.py:537
  79.6 2.3 %collective-permute-start.21 = (bf16[2,40,1024]{2,1,0:T(8,128)(2,1)S(1)}, bf16[2,40,1024]{2,1,0:T(8,128)(2,1)S(1)}, u32[]{:S(2)}, u32[]{:S(2)}) collective-permute-start(bf16[2,40,1024]{2,1,0:T(8,128)(2,1)S(1)} %get-tuple-element.116), channel_id=1, source_target_pairs={{0,6},{1,7},{2,4},{3,5},{4,2},{5,3},{6,0},{7,1},{8,14},{9,15},{10,... | collective-permute-start | bytes 491528 | tf_op jit(solution)/shard_map/ppermute | solution.py:537
  81.9 3.2 %up_1.1 = (f32[288,512]{1,0:T(8,128)S(1)}, f32[288,512]{1,0:T(8,128)S(1)}, f32[288,128]{1,0:T(8,128)S(1)}) custom-call(s32[1]{0:T(128)} %bitcast.refs_0_.me, bf16[2,72,1024]{2,1,0:T(8,128)(2,1)S(1)} %near_kernel.1.refs_2_.refs_0_, ...), custom_call_target="tpu_custom_call", output_to_operand_aliasing={{0}: (9, {}), {1}: (10, {}), {2}: (11, {})} | custom-call | tf_op jit(solution)/shard_map/up_1/pallas_call | solution.py:283
  85.1 1.1 collective-permute-done.16.refs_1_.refs_3_.refs_2_
  87.0 1.1 collective-permute-start.17
  88.1 0.9 collective-permute-start.18
  89.0 1.1 collective-permute-done.19.refs_11_.refs_9_
  90.1 3.2 %up_2.1 = (f32[288,512]{1,0:T(8,128)S(1)}, f32[288,512]{1,0:T(8,128)S(1)}, f32[288,128]{1,0:T(8,128)S(1)}) custom-call(s32[1]{0:T(128)} %bitcast.refs_0_.me, bf16[2,72,1024]{2,1,0:T(8,128)(2,1)S(1)} %collective-permute-done.3.refs_1_.refs_0_, ...), custom_call_target="tpu_custom_call", output_to_operand_aliasing={{0}: (9, {}), {1}: (10, {}), {2}: (11, {})} | custom-call | tf_op jit(solution)/shard_map/up_2/pallas_call | solution.py:283
  93.3 3.5 %up_3.1 = (bf16[72,512]{1,0:T(8,128)(2,1)S(1)}, bf16[216,512]{1,0:T(8,128)(2,1)S(1)}) custom-call(s32[1]{0:T(128)} %bitcast.refs_0_.me, bf16[2,72,1024]{2,1,0:T(8,128)(2,1)S(1)} %collective-permute-done.4.refs_0_, bf16[3,72,1024]{2,1,0:T(8,128)(2,1)S(1)} %collective-permute-done.15.refs_0_.refs_4_.refs_1_, ...), custom_call_target="tpu_custom_call" | custom-call | tf_op jit(solution)/shard_map/up_3/pallas_call | solution.py:283
  96.9 4.2 %down_through.1 = (bf16[9,16,1024]{2,1,0:T(8,128)(2,1)S(1)}, bf16[9,16,1024]{2,1,0:T(8,128)(2,1)S(1)}, bf16[9,16,1024]{2,1,0:T(8,128)(2,1)S(1)}, bf16[9,16,1024]{2,1,0:T(8,128)(2,1)S(1)}) custom-call(bf16[72,512]{1,0:T(8,128)(2,1)S(1)} %get-tuple-element.124.act_ref, bf16[512,8192]{1,0:T(8,128)(2,1)} %bitcast.27), custom_call_target="tpu_custom_call" | custom-call | tf_op jit(solution)/shard_map/down_through/pallas_call | solution.py:373
  101.1 1.4 collective-permute-start.22
  102.5 1.0 collective-permute-start.23
  103.5 5.1 %down_rest.1 = (bf16[9,16,1024]{2,1,0:T(8,128)(2,1)S(1)}, bf16[9,16,1024]{2,1,0:T(8,128)(2,1)S(1)}, bf16[9,16,1024]{2,1,0:T(8,128)(2,1)S(1)}, bf16[9,16,1024]{2,...) custom-call(bf16[216,512]{1,0:T(8,128)(2,1)S(1)} %get-tuple-element., ...), custom_call_target="tpu_custom_call" | custom-call | tf_op jit(solution)/shard_map/down_rest/pallas_call | solution.py:373
  109.4 0.8 collective-permute-start.24
  110.1 1.0 collective-permute-start.25
  111.2 1.3 collective-permute-start.28
  112.5 1.0 collective-permute-start.29
  113.5 5.9 %collective-permute-done.24.refs_1_ = bf16[9,16,1024]{2,1,0:T(8,128)(2,1)S(1)} collective-permute-done((bf16[9,16,1024]{2,1,0:T(8,128)(2,1)S(1)}, bf16[9,16,1024]{2,1,0:T(8,128)(2,1)S(1)}, u32[]{:S(2)}, u32[]{:S(2)}) %collective-permute-start.24) | collective-permute-done | bytes 294944 | tf_op jit(solution)/shard_map/ppermute | solution.py:531
  120.2 1.4 collective-permute-start.26
  121.6 1.0 collective-permute-start.27
  122.6 2.5 %collective-permute-start.34 = (bf16[9,16,1024]{2,1,0:T(8,128)(2,1)S(1)}, bf16[9,16,1024]{2,1,0:T(8,128)(2,1)S(1)}, u32[]{:S(2)}, u32[]{:S(2)}) collective-permute-start(bf16[9,16,1024]{2,1,0:T(8,128)(2,1)S(1)} %get-tuple-element.145.refs_6_), channel_id=1, source_target_pairs={{0,6},{1,7},{2,4},{3,5},{4,2},{5,3},{6,0},{7,1},{8,14},{9,15},{10,... | collective-permute-start | bytes 884744 | tf_op jit(solution)/shard_map/ppermute | solution.py:537
  126.6 1.4 collective-permute-start.32
  128.0 1.0 collective-permute-start.33
  129.0 3.1 %collective-permute-done.26.refs_1_ = bf16[9,16,1024]{2,1,0:T(8,128)(2,1)S(1)} collective-permute-done((bf16[9,16,1024]{2,1,0:T(8,128)(2,1)S(1)}, bf16[9,16,1024]{2,1,0:T(8,128)(2,1)S(1)}, u32[]{:S(2)}, u32[]{:S(2)}) %collective-permute-start.26) | collective-permute-done | bytes 294944 | tf_op jit(solution)/shard_map/ppermute | solution.py:531
  132.9 1.4 collective-permute-start.30
  134.2 1.0 collective-permute-start.31
  135.2 5.1 %collective-permute-start.36 = (bf16[9,16,1024]{2,1,0:T(8,128)(2,1)S(1)}, bf16[9,16,1024]{2,1,0:T(8,128)(2,1)S(1)}, u32[]{:S(2)}, u32[]{:S(2)}) collective-permute-start(bf16[9,16,1024]{2,1,0:T(8,128)(2,1)S(1)} %get-tuple-element.153), channel_id=1, source_target_pairs={{0,4},{1,5},{2,6},{3,7},{4,0},{5,1},{6,2},{7,3},{8,12},{9,13},{10,... | collective-permute-start | bytes 884744 | tf_op jit(solution)/shard_map/ppermute | solution.py:537
  140.5 2.8 %collective-permute-start.35 = (bf16[9,16,1024]{2,1,0:T(8,128)(2,1)S(1)}, bf16[9,16,1024]{2,1,0:T(8,128)(2,1)S(1)}, u32[]{:S(2)}, u32[]{:S(2)}) collective-permute-start(bf16[9,16,1024]{2,1,0:T(8,128)(2,1)S(1)} %finish_1.1), channel_id=1, source_target_pairs={{0,2},{1,3},{2,0},{3,1},{4,6},{5,7},{6,4},{7,5},{8,10},{9,11},{10,... | collective-permute-start | bytes 884744 | tf_op jit(solution)/shard_map/ppermute | solution.py:537
  143.4 5.0 %collective-permute-done.36.refs_2_.refs_6_ = bf16[9,16,1024]{2,1,0:T(8,128)(2,1)S(1)} collective-permute-done((bf16[9,16,1024]{2,1,0:T(8,128)(2,1)S(1)}, bf16[9,16,1024]{2,1,0:T(8,128)(2,1)S(1)}, u32[]{:S(2)}, u32[]{:S(2)}) %collective-permute-start.36) | collective-permute-done | bytes 294944 | tf_op jit(solution)/shard_map/ppermute | solution.py:537
  148.4 2.7 %collective-permute-done.35.refs_1_.refs_5_ = bf16[9,16,1024]{2,1,0:T(8,128)(2,1)S(1)} collective-permute-done((bf16[9,16,1024]{2,1,0:T(8,128)(2,1)S(1)}, bf16[9,16,1024]{2,1,0:T(8,128)(2,1)S(1)}, u32[]{:S(2)}, u32[]{:S(2)}) %collective-permute-start.35) | collective-permute-done | bytes 294944 | tf_op jit(solution)/shard_map/ppermute | solution.py:537
  151.1 2.0 %collective-permute-done.37.refs_3_ = bf16[2,9,16,1024]{3,2,1,0:T(8,128)(2,1)S(1)} collective-permute-done((bf16[2,9,16,1024]{3,2,1,0:T(8,128)(2,1)S(1)}, bf16[2,9,16,1024]{3,2,1,0:T(8,128)(2,1)S(1)}, u32[]{:S(2)}, u32[]{:S(2)}) %collective-permute-start.37) | collective-permute-done | bytes 589856 | tf_op jit(solution)/shard_map/ppermute | solution.py:537
  153.1 1.9 %mix_kernel.1 = bf16[32,8192]{1,0:T(8,128)(2,1)} custom-call(s32[1]{0:T(128)} %bitcast.refs_0_.me, s32[2,32]{1,0:T(2,128)S(1)} %bitcast.17, f32[2,32]{1,0:T(2,128)S(1)} %bitcast.18, bf16[2,9,16,1024]{3,2,1,0:T(8,128)(2,1)S(1)} %collective-permute-done.37.refs_3_, bf16[9,16,1024]{2,1,0:T(8,128)(2,1)S(1)} %finish_0.1.refs_0_.refs_4_, ...), custom_call_target="tpu_custom_call" | custom-call | tf_op jit(solution)/shard_map/mix_kernel/pallas_call | solution.py:39
  (64 shorter events, 9.3 us)
Async XLA Ops:
  0.0 1.0 copy-start.3
  1.0 0.7 copy-start.8
  2.8 63.6 %copy-start.2 = (f32[8192]{0:T(1024)S(1)}, f32[8192]{0:T(1024)}, u32[]{:S(2)}) copy-start(f32[8192]{0:T(1024)} %param.24) | copy-start | bytes 98308
  2.8 23.5 %all-to-all-start = ((bf16[8,32,1152]{2,1,0:T(8,128)(2,1)}), bf16[8,32,1152]{2,1,0:T(8,128)(2,1)S(1)}, u32[]{:S(2)}, u32[]{:S(2)}) async-start(bf16[8,32,1152]{2,1,0:T(8,128)(2,1)} %pack_kernel.1), calls=%async_computation | async-start | bytes 1179648 | tf_op jit(solution)/shard_map/all_to_all | solution.py:550
  13.2 9.7 %collective-permute-start = (bf16[144,1024]{1,0:T(8,128)(2,1)}, bf16[144,1024]{1,0:T(8,128)(2,1)S(1)}, u32[]{:S(2)}, u32[]{:S(2)}) collective-permute-start(bf16[144,1024]{1,0:T(8,128)(2,1)} %get-tuple-element.83.refs_1_), channel_id=1, source_target_pairs={{0,8},{8,0},{16,24},{24,16},{1,9},{9,1},{17,25},{25,17},{2,10},{10... | collective-permute-start | bytes 884744 | tf_op jit(solution)/shard_map/ppermute | solution.py:531
  22.9 1.0 copy-start.4
  23.9 0.7 copy-start.7
  24.7 8.0 %collective-permute-start.1 = (bf16[128,1024]{1,0:T(8,128)(2,1)S(1)}, bf16[128,1024]{1,0:T(8,128)(2,1)S(1)}, u32[]{:S(2)}, u32[]{:S(2)}) collective-permute-start(bf16[128,1024]{1,0:T(8,128)(2,1)S(1)} %join_kernel.1.refs_6_), channel_id=1, source_target_pairs={{0,16},{8,24},{16,0},{24,8},{1,17},{9,25},{17,1},{25,9},{2,18},{10... | collective-permute-start | bytes 786440 | tf_op jit(solution)/shard_map/ppermute | solution.py:534
  26.3 1.2 copy-start
  27.5 1.2 copy-start.1
  28.8 0.9 copy-start.5
  29.7 0.8 copy-start.6
  34.0 2.4 %collective-permute-start.2 = (bf16[4,104,1024]{2,1,0:T(8,128)(2,1)S(1)}, bf16[4,104,1024]{2,1,0:T(8,128)(2,1)S(1)}, u32[]{:S(2)}, u32[]{:S(2)}) collective-permute-start(bf16[4,104,1024]{2,1,0:T(8,128)(2,1)S(1)} %get-tuple-element.91), channel_id=1, source_target_pairs={{0,1},{1,0},{2,3},{3,2},{4,5},{5,4},{6,7},{7,6},{8,9},{9,8},{10,11... | collective-permute-start | bytes 2555912 | tf_op jit(solution)/shard_map/ppermute | solution.py:537
  34.1 7.7 %collective-permute-start.5 = (bf16[80,1024]{1,0:T(8,128)(2,1)S(1)}, bf16[80,1024]{1,0:T(8,128)(2,1)S(1)}, u32[]{:S(2)}, u32[]{:S(2)}) collective-permute-start(bf16[80,1024]{1,0:T(8,128)(2,1)S(1)} %get-tuple-element.94), channel_id=1, source_target_pairs={{0,2},{1,3},{2,0},{3,1},{4,6},{5,7},{6,4},{7,5},{8,10},{9,11},{10,... | collective-permute-start | bytes 491528 | tf_op jit(solution)/shard_map/ppermute | solution.py:537
  35.4 11.6 %collective-permute-start.6 = (bf16[80,1024]{1,0:T(8,128)(2,1)S(1)}, bf16[80,1024]{1,0:T(8,128)(2,1)S(1)}, u32[]{:S(2)}, u32[]{:S(2)}) collective-permute-start(bf16[80,1024]{1,0:T(8,128)(2,1)S(1)} %get-tuple-element.95), channel_id=1, source_target_pairs={{0,3},{1,2},{2,1},{3,0},{4,7},{5,6},{6,5},{7,4},{8,11},{9,10},{10,... | collective-permute-start | bytes 491528 | tf_op jit(solution)/shard_map/ppermute | solution.py:537
  36.6 15.4 %collective-permute-start.10 = (bf16[2,72,1024]{2,1,0:T(8,128)(2,1)S(1)}, bf16[2,72,1024]{2,1,0:T(8,128)(2,1)S(1)}, u32[]{:S(2)}, u32[]{:S(2)}) collective-permute-start(bf16[2,72,1024]{2,1,0:T(8,128)(2,1)S(1)} %get-tuple-element.96.refs_0_), channel_id=1, source_target_pairs={{0,16},{8,24},{16,0},{24,8},{1,17},{9,25},{17,1},{25,9},{2,18},{10... | collective-permute-start | bytes 884744 | tf_op jit(solution)/shard_map/ppermute | solution.py:534
  38.2 13.8 %collective-permute-start.9 = (bf16[2,72,1024]{2,1,0:T(8,128)(2,1)S(1)}, bf16[2,72,1024]{2,1,0:T(8,128)(2,1)S(1)}, u32[]{:S(2)}, u32[]{:S(2)}) collective-permute-start(bf16[2,72,1024]{2,1,0:T(8,128)(2,1)S(1)} %get-tuple-element.96.refs_0_), channel_id=1, source_target_pairs={{0,8},{8,0},{16,24},{24,16},{1,9},{9,1},{17,25},{25,17},{2,10},{10... | collective-permute-start | bytes 884744 | tf_op jit(solution)/shard_map/ppermute | solution.py:531
  39.6 15.8 %collective-permute-start.3 = (bf16[2,72,1024]{2,1,0:T(8,128)(2,1)S(1)}, bf16[2,72,1024]{2,1,0:T(8,128)(2,1)S(1)}, u32[]{:S(2)}, u32[]{:S(2)}) collective-permute-start(bf16[2,72,1024]{2,1,0:T(8,128)(2,1)S(1)} %get-tuple-element.93), channel_id=1, source_target_pairs={{0,4},{1,5},{2,6},{3,7},{4,0},{5,1},{6,2},{7,3},{8,12},{9,13},{10,... | collective-permute-start | bytes 884744 | tf_op jit(solution)/shard_map/ppermute | solution.py:537
  47.0 10.4 %collective-permute-start.8 = (bf16[2,72,1024]{2,1,0:T(8,128)(2,1)S(1)}, bf16[2,72,1024]{2,1,0:T(8,128)(2,1)S(1)}, u32[]{:S(2)}, u32[]{:S(2)}) collective-permute-start(bf16[2,72,1024]{2,1,0:T(8,128)(2,1)S(1)} %near_kernel.1.refs_2_.refs_0_), channel_id=1, source_target_pairs={{0,16},{8,24},{16,0},{24,8},{1,17},{9,25},{17,1},{25,9},{2,18},{10... | collective-permute-start | bytes 884744 | tf_op jit(solution)/shard_map/ppermute | solution.py:534
  49.6 10.1 %collective-permute-start.7 = (bf16[2,72,1024]{2,1,0:T(8,128)(2,1)S(1)}, bf16[2,72,1024]{2,1,0:T(8,128)(2,1)S(1)}, u32[]{:S(2)}, u32[]{:S(2)}) collective-permute-start(bf16[2,72,1024]{2,1,0:T(8,128)(2,1)S(1)} %near_kernel.1.refs_2_.refs_0_), channel_id=1, source_target_pairs={{0,8},{8,0},{16,24},{24,16},{1,9},{9,1},{17,25},{25,17},{2,10},{10... | collective-permute-start | bytes 884744 | tf_op jit(solution)/shard_map/ppermute | solution.py:531
  52.0 10.6 %collective-permute-start.11 = (bf16[1,72,1024]{2,1,0:T(8,128)(2,1)S(1)}, bf16[1,72,1024]{2,1,0:T(8,128)(2,1)S(1)}, u32[]{:S(2)}, u32[]{:S(2)}) collective-permute-start(bf16[1,72,1024]{2,1,0:T(8,128)(2,1)S(1)} %get-tuple-element.97), channel_id=1, source_target_pairs={{0,8},{8,0},{16,24},{24,16},{1,9},{9,1},{17,25},{25,17},{2,10},{10... | collective-permute-start | bytes 442376 | tf_op jit(solution)/shard_map/ppermute | solution.py:531
  52.1 10.5 %collective-permute-start.12 = (bf16[1,72,1024]{2,1,0:T(8,128)(2,1)S(1)}, bf16[1,72,1024]{2,1,0:T(8,128)(2,1)S(1)}, u32[]{:S(2)}, u32[]{:S(2)}) collective-permute-start(bf16[1,72,1024]{2,1,0:T(8,128)(2,1)S(1)} %get-tuple-element.98), channel_id=1, source_target_pairs={{0,16},{8,24},{16,0},{24,8},{1,17},{9,25},{17,1},{25,9},{2,18},{10... | collective-permute-start | bytes 442376 | tf_op jit(solution)/shard_map/ppermute | solution.py:534
  62.7 12.2 %collective-permute-start.13 = (bf16[3,72,1024]{2,1,0:T(8,128)(2,1)S(1)}, bf16[3,72,1024]{2,1,0:T(8,128)(2,1)S(1)}, u32[]{:S(2)}, u32[]{:S(2)}) collective-permute-start(bf16[3,72,1024]{2,1,0:T(8,128)(2,1)S(1)} %get-tuple-element.99), channel_id=1, source_target_pairs={{0,8},{8,0},{16,24},{24,16},{1,9},{9,1},{17,25},{25,17},{2,10},{10... | collective-permute-start | bytes 1327112 | tf_op jit(solution)/shard_map/ppermute | solution.py:531
  64.5 11.3 %collective-permute-start.14 = (bf16[3,72,1024]{2,1,0:T(8,128)(2,1)S(1)}, bf16[3,72,1024]{2,1,0:T(8,128)(2,1)S(1)}, u32[]{:S(2)}, u32[]{:S(2)}) collective-permute-start(bf16[3,72,1024]{2,1,0:T(8,128)(2,1)S(1)} %get-tuple-element.100), channel_id=1, source_target_pairs={{0,16},{8,24},{16,0},{24,8},{1,17},{9,25},{17,1},{25,9},{2,18},{10... | collective-permute-start | bytes 1327112 | tf_op jit(solution)/shard_map/ppermute | solution.py:534
  64.8 10.1 %collective-permute-start.4 = (bf16[2,72,1024]{2,1,0:T(8,128)(2,1)S(1)}, bf16[2,72,1024]{2,1,0:T(8,128)(2,1)S(1)}, u32[]{:S(2)}, u32[]{:S(2)}) collective-permute-start(bf16[2,72,1024]{2,1,0:T(8,128)(2,1)S(1)} %hold_farthest.1.refs_5_), channel_id=1, source_target_pairs={{0,6},{1,7},{2,4},{3,5},{4,2},{5,3},{6,0},{7,1},{8,14},{9,15},{10,... | collective-permute-start | bytes 884744 | tf_op jit(solution)/shard_map/ppermute | solution.py:537
  75.8 10.4 %collective-permute-start.16 = (bf16[3,72,1024]{2,1,0:T(8,128)(2,1)S(1)}, bf16[3,72,1024]{2,1,0:T(8,128)(2,1)S(1)}, u32[]{:S(2)}, u32[]{:S(2)}) collective-permute-start(bf16[3,72,1024]{2,1,0:T(8,128)(2,1)S(1)} %get-tuple-element.103), channel_id=1, source_target_pairs={{0,16},{8,24},{16,0},{24,8},{1,17},{9,25},{17,1},{25,9},{2,18},{10... | collective-permute-start | bytes 1327112 | tf_op jit(solution)/shard_map/ppermute | solution.py:534
  76.5 10.4 %collective-permute-start.15 = (bf16[3,72,1024]{2,1,0:T(8,128)(2,1)S(1)}, bf16[3,72,1024]{2,1,0:T(8,128)(2,1)S(1)}, u32[]{:S(2)}, u32[]{:S(2)}) collective-permute-start(bf16[3,72,1024]{2,1,0:T(8,128)(2,1)S(1)} %get-tuple-element.102.refs_3_), channel_id=1, source_target_pairs={{0,8},{8,0},{16,24},{24,16},{1,9},{9,1},{17,25},{25,17},{2,10},{10... | collective-permute-start | bytes 1327112 | tf_op jit(solution)/shard_map/ppermute | solution.py:531
  77.1 11.9 %collective-permute-start.20 = (bf16[2,40,1024]{2,1,0:T(8,128)(2,1)S(1)}, bf16[2,40,1024]{2,1,0:T(8,128)(2,1)S(1)}, u32[]{:S(2)}, u32[]{:S(2)}) collective-permute-start(bf16[2,40,1024]{2,1,0:T(8,128)(2,1)S(1)} %get-tuple-element.115), channel_id=1, source_target_pairs={{0,4},{1,5},{2,6},{3,7},{4,0},{5,1},{6,2},{7,3},{8,12},{9,13},{10,... | collective-permute-start | bytes 491528 | tf_op jit(solution)/shard_map/ppermute | solution.py:537
  79.6 9.4 %collective-permute-start.21 = (bf16[2,40,1024]{2,1,0:T(8,128)(2,1)S(1)}, bf16[2,40,1024]{2,1,0:T(8,128)(2,1)S(1)}, u32[]{:S(2)}, u32[]{:S(2)}) collective-permute-start(bf16[2,40,1024]{2,1,0:T(8,128)(2,1)S(1)} %get-tuple-element.116), channel_id=1, source_target_pairs={{0,6},{1,7},{2,4},{3,5},{4,2},{5,3},{6,0},{7,1},{8,14},{9,15},{10,... | collective-permute-start | bytes 491528 | tf_op jit(solution)/shard_map/ppermute | solution.py:537
  81.9 8.2 %collective-permute-start.19 = (bf16[2,40,1024]{2,1,0:T(8,128)(2,1)S(1)}, bf16[2,40,1024]{2,1,0:T(8,128)(2,1)S(1)}, u32[]{:S(2)}, u32[]{:S(2)}) collective-permute-start(bf16[2,40,1024]{2,1,0:T(8,128)(2,1)S(1)} %get-tuple-element.109.refs_11_), channel_id=1, source_target_pairs={{0,2},{1,3},{2,0},{3,1},{4,6},{5,7},{6,4},{7,5},{8,10},{9,11},{10,... | collective-permute-start | bytes 491528 | tf_op jit(solution)/shard_map/ppermute | solution.py:537
  87.0 6.3 %collective-permute-start.17 = (bf16[1,72,1024]{2,1,0:T(8,128)(2,1)S(1)}, bf16[1,72,1024]{2,1,0:T(8,128)(2,1)S(1)}, u32[]{:S(2)}, u32[]{:S(2)}) collective-permute-start(bf16[1,72,1024]{2,1,0:T(8,128)(2,1)S(1)} %get-tuple-element.111), channel_id=1, source_target_pairs={{0,16},{8,24},{16,0},{24,8},{1,17},{9,25},{17,1},{25,9},{2,18},{10... | collective-permute-start | bytes 442376 | tf_op jit(solution)/shard_map/ppermute | solution.py:534
  88.1 5.3 %collective-permute-start.18 = (bf16[1,72,1024]{2,1,0:T(8,128)(2,1)S(1)}, bf16[1,72,1024]{2,1,0:T(8,128)(2,1)S(1)}, u32[]{:S(2)}, u32[]{:S(2)}) collective-permute-start(bf16[1,72,1024]{2,1,0:T(8,128)(2,1)S(1)} %get-tuple-element.112), channel_id=1, source_target_pairs={{0,8},{8,0},{16,24},{24,16},{1,9},{9,1},{17,25},{25,17},{2,10},{10... | collective-permute-start | bytes 442376 | tf_op jit(solution)/shard_map/ppermute | solution.py:531
  101.1 7.5 %collective-permute-start.22 = (bf16[9,16,1024]{2,1,0:T(8,128)(2,1)S(1)}, bf16[9,16,1024]{2,1,0:T(8,128)(2,1)S(1)}, u32[]{:S(2)}, u32[]{:S(2)}) collective-permute-start(bf16[9,16,1024]{2,1,0:T(8,128)(2,1)S(1)} %get-tuple-element.125), channel_id=1, source_target_pairs={{0,8},{8,0},{16,24},{24,16},{1,9},{9,1},{17,25},{25,17},{2,10},{10... | collective-permute-start | bytes 884744 | tf_op jit(solution)/shard_map/ppermute | solution.py:531
  102.5 6.7 %collective-permute-start.23 = (bf16[9,16,1024]{2,1,0:T(8,128)(2,1)S(1)}, bf16[9,16,1024]{2,1,0:T(8,128)(2,1)S(1)}, u32[]{:S(2)}, u32[]{:S(2)}) collective-permute-start(bf16[9,16,1024]{2,1,0:T(8,128)(2,1)S(1)} %get-tuple-element.126), channel_id=1, source_target_pairs={{0,16},{8,24},{16,0},{24,8},{1,17},{9,25},{17,1},{25,9},{2,18},{10... | collective-permute-start | bytes 884744 | tf_op jit(solution)/shard_map/ppermute | solution.py:534
  103.5 49.7 %copy-start.9 = (s32[32,2]{0,1:T(2,128)S(1)}, s32[32,2]{0,1:T(2,128)}, u32[]{:S(2)}) copy-start(s32[32,2]{0,1:T(2,128)} %param.25) | copy-start | bytes 772
  103.5 49.7 %copy-start.10 = (f32[32,2]{0,1:T(2,128)S(1)}, f32[32,2]{0,1:T(2,128)}, u32[]{:S(2)}) copy-start(f32[32,2]{0,1:T(2,128)} %param.26) | copy-start | bytes 772
  109.4 10.0 %collective-permute-start.24 = (bf16[9,16,1024]{2,1,0:T(8,128)(2,1)S(1)}, bf16[9,16,1024]{2,1,0:T(8,128)(2,1)S(1)}, u32[]{:S(2)}, u32[]{:S(2)}) collective-permute-start(bf16[9,16,1024]{2,1,0:T(8,128)(2,1)S(1)} %get-tuple-element.133), channel_id=1, source_target_pairs={{0,8},{8,0},{16,24},{24,16},{1,9},{9,1},{17,25},{25,17},{2,10},{10... | collective-permute-start | bytes 884744 | tf_op jit(solution)/shard_map/ppermute | solution.py:531
  110.1 9.9 %collective-permute-start.25 = (bf16[9,16,1024]{2,1,0:T(8,128)(2,1)S(1)}, bf16[9,16,1024]{2,1,0:T(8,128)(2,1)S(1)}, u32[]{:S(2)}, u32[]{:S(2)}) collective-permute-start(bf16[9,16,1024]{2,1,0:T(8,128)(2,1)S(1)} %get-tuple-element.134), channel_id=1, source_target_pairs={{0,16},{8,24},{16,0},{24,8},{1,17},{9,25},{17,1},{25,9},{2,18},{10... | collective-permute-start | bytes 884744 | tf_op jit(solution)/shard_map/ppermute | solution.py:534
  111.2 14.5 %collective-permute-start.28 = (bf16[9,16,1024]{2,1,0:T(8,128)(2,1)S(1)}, bf16[9,16,1024]{2,1,0:T(8,128)(2,1)S(1)}, u32[]{:S(2)}, u32[]{:S(2)}) collective-permute-start(bf16[9,16,1024]{2,1,0:T(8,128)(2,1)S(1)} %get-tuple-element.139), channel_id=1, source_target_pairs={{0,8},{8,0},{16,24},{24,16},{1,9},{9,1},{17,25},{25,17},{2,10},{10... | collective-permute-start | bytes 884744 | tf_op jit(solution)/shard_map/ppermute | solution.py:531
  112.5 13.9 %collective-permute-start.29 = (bf16[9,16,1024]{2,1,0:T(8,128)(2,1)S(1)}, bf16[9,16,1024]{2,1,0:T(8,128)(2,1)S(1)}, u32[]{:S(2)}, u32[]{:S(2)}) collective-permute-start(bf16[9,16,1024]{2,1,0:T(8,128)(2,1)S(1)} %get-tuple-element.140), channel_id=1, source_target_pairs={{0,16},{8,24},{16,0},{24,8},{1,17},{9,25},{17,1},{25,9},{2,18},{10... | collective-permute-start | bytes 884744 | tf_op jit(solution)/shard_map/ppermute | solution.py:534
  120.2 11.8 %collective-permute-start.26 = (bf16[9,16,1024]{2,1,0:T(8,128)(2,1)S(1)}, bf16[9,16,1024]{2,1,0:T(8,128)(2,1)S(1)}, u32[]{:S(2)}, u32[]{:S(2)}) collective-permute-start(bf16[9,16,1024]{2,1,0:T(8,128)(2,1)S(1)} %get-tuple-element.137), channel_id=1, source_target_pairs={{0,8},{8,0},{16,24},{24,16},{1,9},{9,1},{17,25},{25,17},{2,10},{10... | collective-permute-start | bytes 884744 | tf_op jit(solution)/shard_map/ppermute | solution.py:531
  121.6 11.1 %collective-permute-start.27 = (bf16[9,16,1024]{2,1,0:T(8,128)(2,1)S(1)}, bf16[9,16,1024]{2,1,0:T(8,128)(2,1)S(1)}, u32[]{:S(2)}, u32[]{:S(2)}) collective-permute-start(bf16[9,16,1024]{2,1,0:T(8,128)(2,1)S(1)} %get-tuple-element.138), channel_id=1, source_target_pairs={{0,16},{8,24},{16,0},{24,8},{1,17},{9,25},{17,1},{25,9},{2,18},{10... | collective-permute-start | bytes 884744 | tf_op jit(solution)/shard_map/ppermute | solution.py:534
  122.6 12.6 %collective-permute-start.34 = (bf16[9,16,1024]{2,1,0:T(8,128)(2,1)S(1)}, bf16[9,16,1024]{2,1,0:T(8,128)(2,1)S(1)}, u32[]{:S(2)}, u32[]{:S(2)}) collective-permute-start(bf16[9,16,1024]{2,1,0:T(8,128)(2,1)S(1)} %get-tuple-element.145.refs_6_), channel_id=1, source_target_pairs={{0,6},{1,7},{2,4},{3,5},{4,2},{5,3},{6,0},{7,1},{8,14},{9,15},{10,... | collective-permute-start | bytes 884744 | tf_op jit(solution)/shard_map/ppermute | solution.py:537
  126.6 13.8 %collective-permute-start.32 = (bf16[9,16,1024]{2,1,0:T(8,128)(2,1)S(1)}, bf16[9,16,1024]{2,1,0:T(8,128)(2,1)S(1)}, u32[]{:S(2)}, u32[]{:S(2)}) collective-permute-start(bf16[9,16,1024]{2,1,0:T(8,128)(2,1)S(1)} %get-tuple-element.151), channel_id=1, source_target_pairs={{0,8},{8,0},{16,24},{24,16},{1,9},{9,1},{17,25},{25,17},{2,10},{10... | collective-permute-start | bytes 884744 | tf_op jit(solution)/shard_map/ppermute | solution.py:531
  128.0 12.4 %collective-permute-start.33 = (bf16[9,16,1024]{2,1,0:T(8,128)(2,1)S(1)}, bf16[9,16,1024]{2,1,0:T(8,128)(2,1)S(1)}, u32[]{:S(2)}, u32[]{:S(2)}) collective-permute-start(bf16[9,16,1024]{2,1,0:T(8,128)(2,1)S(1)} %get-tuple-element.152), channel_id=1, source_target_pairs={{0,16},{8,24},{16,0},{24,8},{1,17},{9,25},{17,1},{25,9},{2,18},{10... | collective-permute-start | bytes 884744 | tf_op jit(solution)/shard_map/ppermute | solution.py:534
  132.9 10.4 %collective-permute-start.30 = (bf16[9,16,1024]{2,1,0:T(8,128)(2,1)S(1)}, bf16[9,16,1024]{2,1,0:T(8,128)(2,1)S(1)}, u32[]{:S(2)}, u32[]{:S(2)}) collective-permute-start(bf16[9,16,1024]{2,1,0:T(8,128)(2,1)S(1)} %get-tuple-element.148), channel_id=1, source_target_pairs={{0,8},{8,0},{16,24},{24,16},{1,9},{9,1},{17,25},{25,17},{2,10},{10... | collective-permute-start | bytes 884744 | tf_op jit(solution)/shard_map/ppermute | solution.py:531
  134.2 9.0 %collective-permute-start.31 = (bf16[9,16,1024]{2,1,0:T(8,128)(2,1)S(1)}, bf16[9,16,1024]{2,1,0:T(8,128)(2,1)S(1)}, u32[]{:S(2)}, u32[]{:S(2)}) collective-permute-start(bf16[9,16,1024]{2,1,0:T(8,128)(2,1)S(1)} %get-tuple-element.149), channel_id=1, source_target_pairs={{0,16},{8,24},{16,0},{24,8},{1,17},{9,25},{17,1},{25,9},{2,18},{10... | collective-permute-start | bytes 884744 | tf_op jit(solution)/shard_map/ppermute | solution.py:534
  135.2 13.1 %collective-permute-start.36 = (bf16[9,16,1024]{2,1,0:T(8,128)(2,1)S(1)}, bf16[9,16,1024]{2,1,0:T(8,128)(2,1)S(1)}, u32[]{:S(2)}, u32[]{:S(2)}) collective-permute-start(bf16[9,16,1024]{2,1,0:T(8,128)(2,1)S(1)} %get-tuple-element.153), channel_id=1, source_target_pairs={{0,4},{1,5},{2,6},{3,7},{4,0},{5,1},{6,2},{7,3},{8,12},{9,13},{10,... | collective-permute-start | bytes 884744 | tf_op jit(solution)/shard_map/ppermute | solution.py:537
  140.5 10.5 %collective-permute-start.35 = (bf16[9,16,1024]{2,1,0:T(8,128)(2,1)S(1)}, bf16[9,16,1024]{2,1,0:T(8,128)(2,1)S(1)}, u32[]{:S(2)}, u32[]{:S(2)}) collective-permute-start(bf16[9,16,1024]{2,1,0:T(8,128)(2,1)S(1)} %finish_1.1), channel_id=1, source_target_pairs={{0,2},{1,3},{2,0},{3,1},{4,6},{5,7},{6,4},{7,5},{8,10},{9,11},{10,... | collective-permute-start | bytes 884744 | tf_op jit(solution)/shard_map/ppermute | solution.py:537
  151.1 2.1 %collective-permute-start.37 = (bf16[2,9,16,1024]{3,2,1,0:T(8,128)(2,1)S(1)}, bf16[2,9,16,1024]{3,2,1,0:T(8,128)(2,1)S(1)}, u32[]{:S(2)}, u32[]{:S(2)}) collective-permute-start(bf16[2,9,16,1024]{3,2,1,0:T(8,128)(2,1)S(1)} %second_kernel.1), channel_id=1, source_target_pairs={{0,1},{1,0},{2,3},{3,2},{4,5},{5,4},{6,7},{7,6},{8,9},{9,8},{10,11... | collective-permute-start | bytes 1769480 | tf_op jit(solution)/shard_map/ppermute | solution.py:537

commit v3 on v2

--- a/solution.py
+++ b/solution.py
@@ -197,10 +197,9 @@
     tokens, channels = mixer.shape
     residual = res_ref[:, :, 0:channels].astype(F32).reshape(tokens, channels)
     stream = (residual + mixer).astype(BF16)
-    owned = stream.shape[0] // sel_ref.shape[0]
-    slots = sel_ref.shape[1] - owned
-    near_a_ref[0:slots, :] = dot(sel_ref[2, owned:, :], stream).astype(BF16)
-    near_b_ref[0:slots, :] = dot(sel_ref[3, owned:, :], stream).astype(BF16)
+    owned = sel_ref.shape[1] - near_a_ref.shape[0]
+    near_a_ref[...] = dot(sel_ref[2, owned:, :], stream).astype(BF16)
+    near_b_ref[...] = dot(sel_ref[3, owned:, :], stream).astype(BF16)
     for at, k in enumerate((0, 2, 3, 1)):
         same_ref[at] = dot(sel_ref[2 * k], stream).astype(BF16)
         other_ref[at] = dot(sel_ref[2 * k + 1], stream).astype(BF16)
@@ -400,8 +399,7 @@
 
 
 def near_kernel(same, other, rows):
-    slots = rows.shape[1]
-    rows[0], rows[1] = same[0:slots, :], other[0:slots, :]
+    rows[0], rows[1] = same[...], other[...]
 
 
 def second_kernel(*refs):
@@ -591,7 +589,7 @@
     )
     groups = owners // 2
     lanes = jax.ShapeDtypeStruct((groups, rows + slots, channels), BF16)
-    one = jax.ShapeDtypeStruct((slots + 8, channels), BF16)
+    one = jax.ShapeDtypeStruct((slots, channels), BF16)
     near_a, near_b, same, other = block_call(
         stream_kernel,
         [one, one, lanes, lanes],

time: 156 us -> 153 us (0.981)
  starting transfers between devices: 57.7 us -> 55.4 us
    ppermute x13, starting transfers between devices: 16.3 us -> 12.4 us  [over_x(): return lax.ppermute(v, 'seq', [(i, i ^ 1) for i in range(4)])]
    ppermute x13, starting transfers between devices: 14.2 us -> 17.9 us  [over_y(): return lax.ppermute(v, 'seq', [(i, i ^ 2) for i in range(4)])]
    ppermute x13, waiting for transfers between devices: 18.8 us -> 15.9 us  [over_x(): return lax.ppermute(v, 'seq', [(i, i ^ 1) for i in range(4)])]
    ppermute x12, starting transfers between devices: 21 us -> 18.7 us  [along(): return lax.ppermute(v, 'exp', [(i, i ^ mask) for i in range(owners)])]
    ppermute x12, waiting for transfers between devices: 24.9 us -> 26.9 us  [along(): return lax.ppermute(v, 'exp', [(i, i ^ mask) for i in range(owners)])]
  transfers between devices with their start and end apart: 39 -> 39, of which waited for: 23 -> 22; matrix products, arithmetic and copies ran while one was open for 0% -> 0% of each run, Pallas kernels for 16% -> 16%
where the time goes in v3:
time: 153 us; the launch traced here: 152 us
  starting transfers between devices  55.4 us (36%)
  waiting for transfers between devices  51.9 us (34%)
  Pallas kernels  37.3 us (24%)
  local copies, waits for them, and re-layouts  7.61 us (5%)
    ppermute x12, waiting for transfers between devices, along(): return lax.ppermute(v, 'exp', [(i, i ^ mask) for i in range(owners)])  26.9 us
    ppermute x12, starting transfers between devices, along(): return lax.ppermute(v, 'exp', [(i, i ^ mask) for i in range(owners)])  18.7 us
    ppermute x13, starting transfers between devices, over_y(): return lax.ppermute(v, 'seq', [(i, i ^ 2) for i in range(4)])  17.9 us
    ppermute x13, waiting for transfers between devices, over_x(): return lax.ppermute(v, 'seq', [(i, i ^ 1) for i in range(4)])  15.9 us
    pallas_call x22, Pallas kernels, block_call(): pl.pallas_call(kernel, name=name or getattr(body, 'func', body).__name__,...  14.8 us
    pallas_call x4, Pallas kernels, up_project(): pl.pallas_call(functools.partial(up_kernel, carry is None, features, len(...  13.2 us
    ppermute x13, starting transfers between devices, over_x(): return lax.ppermute(v, 'seq', [(i, i ^ 1) for i in range(4)])  12.4 us
    pallas_call x2, Pallas kernels, down_project(): pl.pallas_call(functools.partial(down_kernel, groups), name=name, grid=(8...  9.3 us
  transfers between devices with their start and end apart: 39, of which 22 were waited for; matrix products, arithmetic and copies ran while one was open for 0% of the time, Pallas kernels for 16%

profile of v3, /device:TPU:0, one launch (start us, length us, event | category | flops | bytes accessed | tf_op | source)
XLA Modules:
  0.0 152.4 jit_solution(17516794028378670270)
XLA Ops:
  0.0 1.0 copy-done.3
  1.7 1.0 pack_kernel.1
  2.8 6.3 %all-to-all-start = ((bf16[8,32,1152]{2,1,0:T(8,128)(2,1)}), bf16[8,32,1152]{2,1,0:T(8,128)(2,1)S(1)}, u32[]{:S(2)}, u32[]{:S(2)}) async-start(bf16[8,32,1152]{2,1,0:T(8,128)(2,1)} %pack_kernel.1), calls=%async_computation | async-start | bytes 1179648 | tf_op jit(solution)/shard_map/all_to_all | solution.py:548
  9.1 4.1 %state_kernel.1 = (bf16[144,1024]{1,0:T(8,128)(2,1)}, bf16[128,1024]{1,0:T(8,128)(2,1)}) custom-call(s32[1]{0:T(128)} %bitcast.3.refs_0_, bf16[256,1024]{1,0:T(8,128)(2,1)} %refs_1_.5, bf16[256,128]{1,0:T(8,128)(2,1)} %refs_2_.3, f32[16,256]{1,0:T(8,128)} %bitcast.30, f32[1,16]{1,0:T(1,128)} %bitcast.32, f32[1024,128]{1,0:T(8,128)} %bitcast.29), custom_call_target="tpu_custom_call" | custom-call | tf_op jit(solution)/shard_map/state_kernel/pallas_call | solution.py:39
  13.2 1.6 %collective-permute-start = (bf16[144,1024]{1,0:T(8,128)(2,1)}, bf16[144,1024]{1,0:T(8,128)(2,1)S(1)}, u32[]{:S(2)}, u32[]{:S(2)}) collective-permute-start(bf16[144,1024]{1,0:T(8,128)(2,1)} %get-tuple-element.83.refs_1_), channel_id=1, source_target_pairs={{0,8},{8,0},{16,24},{24,16},{1,9},{9,1},{17,25},{25,17},{2,10},{10... | collective-permute-start | bytes 884744 | tf_op jit(solution)/shard_map/ppermute | solution.py:529
  14.8 4.7 %intra_kernel.1 = (f32[256,1024]{1,0:T(8,128)}, f32[256,1024]{1,0:T(8,128)}, f32[8,128]{1,0:T(8,128)}) custom-call(bf16[256,1024]{1,0:T(8,128)(2,1)} %refs_1_.5, bf16[256,1024]{1,0:T(8,128)(2,1)} %refs_1_.4, bf16[256,128]{1,0:T(8,128)(2,1)} %refs_2_.3, bf16[256,128]{1,0:T(8,128)(2,1)} %refs_4_.1, f32[16,256]{1,0:T(8,128)} %bitcast.31, f32[1,16]{1,0:T(1,128)} %bitcast.33, ...), custom_call_target="tpu_custom_call" | custom-call | tf_op jit(solution)/shard_map/intra_kernel/pallas_call | solution.py:39
  19.5 3.4 %collective-permute-done.refs_2_.refs_5_ = bf16[144,1024]{1,0:T(8,128)(2,1)S(1)} collective-permute-done((bf16[144,1024]{1,0:T(8,128)(2,1)}, bf16[144,1024]{1,0:T(8,128)(2,1)S(1)}, u32[]{:S(2)}, u32[]{:S(2)}) %collective-permute-start) | collective-permute-done | bytes 294944 | tf_op jit(solution)/shard_map/ppermute | solution.py:529
  22.9 1.0 copy-done.4
  23.9 0.7 copy-done.7
  24.7 1.6 %collective-permute-start.1 = (bf16[128,1024]{1,0:T(8,128)(2,1)S(1)}, bf16[128,1024]{1,0:T(8,128)(2,1)S(1)}, u32[]{:S(2)}, u32[]{:S(2)}) collective-permute-start(bf16[128,1024]{1,0:T(8,128)(2,1)S(1)} %join_kernel.1.refs_6_), channel_id=1, source_target_pairs={{0,16},{8,24},{16,0},{24,8},{1,17},{9,25},{17,1},{25,9},{2,18},{10... | collective-permute-start | bytes 786440 | tf_op jit(solution)/shard_map/ppermute | solution.py:532
  26.3 1.2 copy-done
  27.5 1.2 copy-done.1
  28.8 0.9 copy-done.5
  29.7 0.8 copy-done.6
  30.9 1.8 %collective-permute-done.1.refs_6_ = bf16[128,1024]{1,0:T(8,128)(2,1)S(1)} collective-permute-done((bf16[128,1024]{1,0:T(8,128)(2,1)S(1)}, bf16[128,1024]{1,0:T(8,128)(2,1)S(1)}, u32[]{:S(2)}, u32[]{:S(2)}) %collective-permute-start.1) | collective-permute-done | bytes 262176 | tf_op jit(solution)/shard_map/ppermute | solution.py:532
  32.7 1.3 stream_kernel.1
  34.1 1.3 collective-permute-start.5
  35.4 1.0 collective-permute-done.2.refs_1_
  36.6 1.6 %collective-permute-start.10 = (bf16[2,72,1024]{2,1,0:T(8,128)(2,1)S(1)}, bf16[2,72,1024]{2,1,0:T(8,128)(2,1)S(1)}, u32[]{:S(2)}, u32[]{:S(2)}) collective-permute-start(bf16[2,72,1024]{2,1,0:T(8,128)(2,1)S(1)} %get-tuple-element.96.refs_0_), channel_id=1, source_target_pairs={{0,16},{8,24},{16,0},{24,8},{1,17},{9,25},{17,1},{25,9},{2,18},{10... | collective-permute-start | bytes 884744 | tf_op jit(solution)/shard_map/ppermute | solution.py:532
  38.2 1.5 collective-permute-start.9
  40.1 2.4 %collective-permute-start.3 = (bf16[2,72,1024]{2,1,0:T(8,128)(2,1)S(1)}, bf16[2,72,1024]{2,1,0:T(8,128)(2,1)S(1)}, u32[]{:S(2)}, u32[]{:S(2)}) collective-permute-start(bf16[2,72,1024]{2,1,0:T(8,128)(2,1)S(1)} %get-tuple-element.93), channel_id=1, source_target_pairs={{0,4},{1,5},{2,6},{3,7},{4,0},{5,1},{6,2},{7,3},{8,12},{9,13},{10,... | collective-permute-start | bytes 884744 | tf_op jit(solution)/shard_map/ppermute | solution.py:535
  42.5 6.0 %collective-permute-done.6.refs_1_ = bf16[72,1024]{1,0:T(8,128)(2,1)S(1)} collective-permute-done((bf16[72,1024]{1,0:T(8,128)(2,1)S(1)}, bf16[72,1024]{1,0:T(8,128)(2,1)S(1)}, u32[]{:S(2)}, u32[]{:S(2)}) %collective-permute-start.6) | collective-permute-done | bytes 147488 | tf_op jit(solution)/shard_map/ppermute | solution.py:535
  49.7 1.5 %collective-permute-start.11 = (bf16[1,72,1024]{2,1,0:T(8,128)(2,1)S(1)}, bf16[1,72,1024]{2,1,0:T(8,128)(2,1)S(1)}, u32[]{:S(2)}, u32[]{:S(2)}) collective-permute-start(bf16[1,72,1024]{2,1,0:T(8,128)(2,1)S(1)} %get-tuple-element.97), channel_id=1, source_target_pairs={{0,8},{8,0},{16,24},{24,16},{1,9},{9,1},{17,25},{25,17},{2,10},{10... | collective-permute-start | bytes 442376 | tf_op jit(solution)/shard_map/ppermute | solution.py:529
  51.3 1.5 collective-permute-start.12
  52.8 4.5 %collective-permute-done.3.refs_1_.refs_0_ = bf16[2,72,1024]{2,1,0:T(8,128)(2,1)S(1)} collective-permute-done((bf16[2,72,1024]{2,1,0:T(8,128)(2,1)S(1)}, bf16[2,72,1024]{2,1,0:T(8,128)(2,1)S(1)}, u32[]{:S(2)}, u32[]{:S(2)}) %collective-permute-start.3) | collective-permute-done | bytes 294944 | tf_op jit(solution)/shard_map/ppermute | solution.py:535
  57.2 1.2 collective-permute-done.8.refs_2_
  59.1 1.8 %collective-permute-done.11.refs_3_.refs_4_ = bf16[1,72,1024]{2,1,0:T(8,128)(2,1)S(1)} collective-permute-done((bf16[1,72,1024]{2,1,0:T(8,128)(2,1)S(1)}, bf16[1,72,1024]{2,1,0:T(8,128)(2,1)S(1)}, u32[]{:S(2)}, u32[]{:S(2)}) %collective-permute-start.11) | collective-permute-done | bytes 147488 | tf_op jit(solution)/shard_map/ppermute | solution.py:529
  61.5 1.5 collective-permute-start.14
  63.0 1.8 %collective-permute-start.4 = (bf16[2,72,1024]{2,1,0:T(8,128)(2,1)S(1)}, bf16[2,72,1024]{2,1,0:T(8,128)(2,1)S(1)}, u32[]{:S(2)}, u32[]{:S(2)}) collective-permute-start(bf16[2,72,1024]{2,1,0:T(8,128)(2,1)S(1)} %hold_farthest.1.refs_5_), channel_id=1, source_target_pairs={{0,6},{1,7},{2,4},{3,5},{4,2},{5,3},{6,0},{7,1},{8,14},{9,15},{10,... | collective-permute-start | bytes 884744 | tf_op jit(solution)/shard_map/ppermute | solution.py:535
  64.8 3.3 %up_0.1 = (f32[288,512]{1,0:T(8,128)S(1)}, f32[288,512]{1,0:T(8,128)S(1)}, f32[288,128]{1,0:T(8,128)S(1)}) custom-call(s32[1]{0:T(128)} %bitcast.refs_0_.me, bf16[2,72,1024]{2,1,0:T(8,128)(2,1)S(1)} %get-tuple-element.96.refs_0_, bf16[2,72,1024]{2,1,0:T(8,128)(2,1)S(1)} %collective-permute-done.9.refs_0_.refs_1_, ...), custom_call_target="tpu_custom_call" | custom-call | tf_op jit(solution)/shard_map/up_0/pallas_call | solution.py:282
  68.1 3.9 %collective-permute-done.4.refs_0_ = bf16[2,72,1024]{2,1,0:T(8,128)(2,1)S(1)} collective-permute-done((bf16[2,72,1024]{2,1,0:T(8,128)(2,1)S(1)}, bf16[2,72,1024]{2,1,0:T(8,128)(2,1)S(1)}, u32[]{:S(2)}, u32[]{:S(2)}) %collective-permute-start.4) | collective-permute-done | bytes 294944 | tf_op jit(solution)/shard_map/ppermute | solution.py:535
  72.2 1.5 collective-permute-start.16
  73.7 1.6 %collective-permute-start.15 = (bf16[3,72,1024]{2,1,0:T(8,128)(2,1)S(1)}, bf16[3,72,1024]{2,1,0:T(8,128)(2,1)S(1)}, u32[]{:S(2)}, u32[]{:S(2)}) collective-permute-start(bf16[3,72,1024]{2,1,0:T(8,128)(2,1)S(1)} %get-tuple-element.102.refs_3_), channel_id=1, source_target_pairs={{0,8},{8,0},{16,24},{24,16},{1,9},{9,1},{17,25},{25,17},{2,10},{10... | collective-permute-start | bytes 1327112 | tf_op jit(solution)/shard_map/ppermute | solution.py:529
  75.3 4.2 %collective-permute-start.20 = (bf16[2,40,1024]{2,1,0:T(8,128)(2,1)S(1)}, bf16[2,40,1024]{2,1,0:T(8,128)(2,1)S(1)}, u32[]{:S(2)}, u32[]{:S(2)}) collective-permute-start(bf16[2,40,1024]{2,1,0:T(8,128)(2,1)S(1)} %get-tuple-element.115), channel_id=1, source_target_pairs={{0,4},{1,5},{2,6},{3,7},{4,0},{5,1},{6,2},{7,3},{8,12},{9,13},{10,... | collective-permute-start | bytes 491528 | tf_op jit(solution)/shard_map/ppermute | solution.py:535
  79.5 2.0 %collective-permute-start.21 = (bf16[2,40,1024]{2,1,0:T(8,128)(2,1)S(1)}, bf16[2,40,1024]{2,1,0:T(8,128)(2,1)S(1)}, u32[]{:S(2)}, u32[]{:S(2)}) collective-permute-start(bf16[2,40,1024]{2,1,0:T(8,128)(2,1)S(1)} %get-tuple-element.116), channel_id=1, source_target_pairs={{0,6},{1,7},{2,4},{3,5},{4,2},{5,3},{6,0},{7,1},{8,14},{9,15},{10,... | collective-permute-start | bytes 491528 | tf_op jit(solution)/shard_map/ppermute | solution.py:535
  81.5 3.2 %up_1.1 = (f32[288,512]{1,0:T(8,128)S(1)}, f32[288,512]{1,0:T(8,128)S(1)}, f32[288,128]{1,0:T(8,128)S(1)}) custom-call(s32[1]{0:T(128)} %bitcast.refs_0_.me, bf16[2,72,1024]{2,1,0:T(8,128)(2,1)S(1)} %near_kernel.1.refs_2_.refs_0_, ...), custom_call_target="tpu_custom_call", output_to_operand_aliasing={{0}: (9, {}), {1}: (10, {}), {2}: (11, {})} | custom-call | tf_op jit(solution)/shard_map/up_1/pallas_call | solution.py:282
  84.7 1.3 collective-permute-start.17
  86.0 0.7 collective-permute-start.18
  86.8 3.2 %collective-permute-done.20.refs_12_.refs_10_ = bf16[2,40,1024]{2,1,0:T(8,128)(2,1)S(1)} collective-permute-done((bf16[2,40,1024]{2,1,0:T(8,128)(2,1)S(1)}, bf16[2,40,1024]{2,1,0:T(8,128)(2,1)S(1)}, u32[]{:S(2)}, u32[]{:S(2)}) %collective-permute-start.20) | collective-permute-done | bytes 163872 | tf_op jit(solution)/shard_map/ppermute | solution.py:535
  90.0 3.2 %up_2.1 = (f32[288,512]{1,0:T(8,128)S(1)}, f32[288,512]{1,0:T(8,128)S(1)}, f32[288,128]{1,0:T(8,128)S(1)}) custom-call(s32[1]{0:T(128)} %bitcast.refs_0_.me, bf16[2,72,1024]{2,1,0:T(8,128)(2,1)S(1)} %collective-permute-done.3.refs_1_.refs_0_, ...), custom_call_target="tpu_custom_call", output_to_operand_aliasing={{0}: (9, {}), {1}: (10, {}), {2}: (11, {})} | custom-call | tf_op jit(solution)/shard_map/up_2/pallas_call | solution.py:282
  93.2 3.5 %up_3.1 = (bf16[72,512]{1,0:T(8,128)(2,1)S(1)}, bf16[216,512]{1,0:T(8,128)(2,1)S(1)}) custom-call(s32[1]{0:T(128)} %bitcast.refs_0_.me, bf16[2,72,1024]{2,1,0:T(8,128)(2,1)S(1)} %collective-permute-done.4.refs_0_, bf16[3,72,1024]{2,1,0:T(8,128)(2,1)S(1)} %collective-permute-done.15.refs_0_.refs_4_.refs_1_, ...), custom_call_target="tpu_custom_call" | custom-call | tf_op jit(solution)/shard_map/up_3/pallas_call | solution.py:282
  96.7 4.2 %down_through.1 = (bf16[9,16,1024]{2,1,0:T(8,128)(2,1)S(1)}, bf16[9,16,1024]{2,1,0:T(8,128)(2,1)S(1)}, bf16[9,16,1024]{2,1,0:T(8,128)(2,1)S(1)}, bf16[9,16,1024]{2,1,0:T(8,128)(2,1)S(1)}) custom-call(bf16[72,512]{1,0:T(8,128)(2,1)S(1)} %get-tuple-element.124.act_ref, bf16[512,8192]{1,0:T(8,128)(2,1)} %bitcast.27), custom_call_target="tpu_custom_call" | custom-call | tf_op jit(solution)/shard_map/down_through/pallas_call | solution.py:372
  101.4 1.4 collective-permute-start.23
  102.9 5.1 %down_rest.1 = (bf16[9,16,1024]{2,1,0:T(8,128)(2,1)S(1)}, bf16[9,16,1024]{2,1,0:T(8,128)(2,1)S(1)}, bf16[9,16,1024]{2,1,0:T(8,128)(2,1)S(1)}, bf16[9,16,1024]{2,...) custom-call(bf16[216,512]{1,0:T(8,128)(2,1)S(1)} %get-tuple-element., ...), custom_call_target="tpu_custom_call" | custom-call | tf_op jit(solution)/shard_map/down_rest/pallas_call | solution.py:372
  108.0 2.0 %collective-permute-done.22.refs_0_ = bf16[9,16,1024]{2,1,0:T(8,128)(2,1)S(1)} collective-permute-done((bf16[9,16,1024]{2,1,0:T(8,128)(2,1)S(1)}, bf16[9,16,1024]{2,1,0:T(8,128)(2,1)S(1)}, u32[]{:S(2)}, u32[]{:S(2)}) %collective-permute-start.22) | collective-permute-done | bytes 294944 | tf_op jit(solution)/shard_map/ppermute | solution.py:529
  110.2 2.4 %collective-permute-start.24 = (bf16[9,16,1024]{2,1,0:T(8,128)(2,1)S(1)}, bf16[9,16,1024]{2,1,0:T(8,128)(2,1)S(1)}, u32[]{:S(2)}, u32[]{:S(2)}) collective-permute-start(bf16[9,16,1024]{2,1,0:T(8,128)(2,1)S(1)} %get-tuple-element.133), channel_id=1, source_target_pairs={{0,8},{8,0},{16,24},{24,16},{1,9},{9,1},{17,25},{25,17},{2,10},{10... | collective-permute-start | bytes 884744 | tf_op jit(solution)/shard_map/ppermute | solution.py:529
  112.6 1.8 %collective-permute-start.25 = (bf16[9,16,1024]{2,1,0:T(8,128)(2,1)S(1)}, bf16[9,16,1024]{2,1,0:T(8,128)(2,1)S(1)}, u32[]{:S(2)}, u32[]{:S(2)}) collective-permute-start(bf16[9,16,1024]{2,1,0:T(8,128)(2,1)S(1)} %get-tuple-element.134), channel_id=1, source_target_pairs={{0,16},{8,24},{16,0},{24,8},{1,17},{9,25},{17,1},{25,9},{2,18},{10... | collective-permute-start | bytes 884744 | tf_op jit(solution)/shard_map/ppermute | solution.py:532
  114.7 5.8 %collective-permute-done.24.refs_1_ = bf16[9,16,1024]{2,1,0:T(8,128)(2,1)S(1)} collective-permute-done((bf16[9,16,1024]{2,1,0:T(8,128)(2,1)S(1)}, bf16[9,16,1024]{2,1,0:T(8,128)(2,1)S(1)}, u32[]{:S(2)}, u32[]{:S(2)}) %collective-permute-start.24) | collective-permute-done | bytes 294944 | tf_op jit(solution)/shard_map/ppermute | solution.py:529
  120.5 1.9 %collective-permute-done.25.refs_2_ = bf16[9,16,1024]{2,1,0:T(8,128)(2,1)S(1)} collective-permute-done((bf16[9,16,1024]{2,1,0:T(8,128)(2,1)S(1)}, bf16[9,16,1024]{2,1,0:T(8,128)(2,1)S(1)}, u32[]{:S(2)}, u32[]{:S(2)}) %collective-permute-start.25) | collective-permute-done | bytes 294944 | tf_op jit(solution)/shard_map/ppermute | solution.py:532
  122.8 1.8 %collective-permute-start.27 = (bf16[9,16,1024]{2,1,0:T(8,128)(2,1)S(1)}, bf16[9,16,1024]{2,1,0:T(8,128)(2,1)S(1)}, u32[]{:S(2)}, u32[]{:S(2)}) collective-permute-start(bf16[9,16,1024]{2,1,0:T(8,128)(2,1)S(1)} %get-tuple-element.138), channel_id=1, source_target_pairs={{0,16},{8,24},{16,0},{24,8},{1,17},{9,25},{17,1},{25,9},{2,18},{10... | collective-permute-start | bytes 884744 | tf_op jit(solution)/shard_map/ppermute | solution.py:532
  124.6 2.0 %collective-permute-start.34 = (bf16[9,16,1024]{2,1,0:T(8,128)(2,1)S(1)}, bf16[9,16,1024]{2,1,0:T(8,128)(2,1)S(1)}, u32[]{:S(2)}, u32[]{:S(2)}) collective-permute-start(bf16[9,16,1024]{2,1,0:T(8,128)(2,1)S(1)} %get-tuple-element.145.refs_6_), channel_id=1, source_target_pairs={{0,6},{1,7},{2,4},{3,5},{4,2},{5,3},{6,0},{7,1},{8,14},{9,15},{10,... | collective-permute-start | bytes 884744 | tf_op jit(solution)/shard_map/ppermute | solution.py:535
  126.9 1.9 %collective-permute-done.29.refs_1_ = bf16[9,16,1024]{2,1,0:T(8,128)(2,1)S(1)} collective-permute-done((bf16[9,16,1024]{2,1,0:T(8,128)(2,1)S(1)}, bf16[9,16,1024]{2,1,0:T(8,128)(2,1)S(1)}, u32[]{:S(2)}, u32[]{:S(2)}) %collective-permute-start.29) | collective-permute-done | bytes 294944 | tf_op jit(solution)/shard_map/ppermute | solution.py:532
  129.2 1.8 %collective-permute-start.33 = (bf16[9,16,1024]{2,1,0:T(8,128)(2,1)S(1)}, bf16[9,16,1024]{2,1,0:T(8,128)(2,1)S(1)}, u32[]{:S(2)}, u32[]{:S(2)}) collective-permute-start(bf16[9,16,1024]{2,1,0:T(8,128)(2,1)S(1)} %get-tuple-element.152), channel_id=1, source_target_pairs={{0,16},{8,24},{16,0},{24,8},{1,17},{9,25},{17,1},{25,9},{2,18},{10... | collective-permute-start | bytes 884744 | tf_op jit(solution)/shard_map/ppermute | solution.py:532
  131.0 2.0 %collective-permute-done.26.refs_1_ = bf16[9,16,1024]{2,1,0:T(8,128)(2,1)S(1)} collective-permute-done((bf16[9,16,1024]{2,1,0:T(8,128)(2,1)S(1)}, bf16[9,16,1024]{2,1,0:T(8,128)(2,1)S(1)}, u32[]{:S(2)}, u32[]{:S(2)}) %collective-permute-start.26) | collective-permute-done | bytes 294944 | tf_op jit(solution)/shard_map/ppermute | solution.py:529
  133.0 1.2 collective-permute-done.27.refs_2_
  134.3 0.9 collective-permute-start.30
  135.2 1.3 collective-permute-start.31
  136.5 3.1 %collective-permute-start.36 = (bf16[9,16,1024]{2,1,0:T(8,128)(2,1)S(1)}, bf16[9,16,1024]{2,1,0:T(8,128)(2,1)S(1)}, u32[]{:S(2)}, u32[]{:S(2)}) collective-permute-start(bf16[9,16,1024]{2,1,0:T(8,128)(2,1)S(1)} %get-tuple-element.153), channel_id=1, source_target_pairs={{0,4},{1,5},{2,6},{3,7},{4,0},{5,1},{6,2},{7,3},{8,12},{9,13},{10,... | collective-permute-start | bytes 884744 | tf_op jit(solution)/shard_map/ppermute | solution.py:535
  139.7 1.4 collective-permute-start.35
  141.1 0.8 collective-permute-done.31.refs_2_
  142.1 5.5 %collective-permute-done.36.refs_2_.refs_6_ = bf16[9,16,1024]{2,1,0:T(8,128)(2,1)S(1)} collective-permute-done((bf16[9,16,1024]{2,1,0:T(8,128)(2,1)S(1)}, bf16[9,16,1024]{2,1,0:T(8,128)(2,1)S(1)}, u32[]{:S(2)}, u32[]{:S(2)}) %collective-permute-start.36) | collective-permute-done | bytes 294944 | tf_op jit(solution)/shard_map/ppermute | solution.py:535
  147.6 0.7 collective-permute-done.35.refs_1_.refs_5_
  148.5 2.0 %collective-permute-done.37.refs_3_ = bf16[2,9,16,1024]{3,2,1,0:T(8,128)(2,1)S(1)} collective-permute-done((bf16[2,9,16,1024]{3,2,1,0:T(8,128)(2,1)S(1)}, bf16[2,9,16,1024]{3,2,1,0:T(8,128)(2,1)S(1)}, u32[]{:S(2)}, u32[]{:S(2)}) %collective-permute-start.37) | collective-permute-done | bytes 589856 | tf_op jit(solution)/shard_map/ppermute | solution.py:535
  150.5 1.9 %mix_kernel.1 = bf16[32,8192]{1,0:T(8,128)(2,1)} custom-call(s32[1]{0:T(128)} %bitcast.refs_0_.me, s32[2,32]{1,0:T(2,128)S(1)} %bitcast.17, f32[2,32]{1,0:T(2,128)S(1)} %bitcast.18, bf16[2,9,16,1024]{3,2,1,0:T(8,128)(2,1)S(1)} %collective-permute-done.37.refs_3_, bf16[9,16,1024]{2,1,0:T(8,128)(2,1)S(1)} %finish_0.1.refs_0_.refs_4_, ...), custom_call_target="tpu_custom_call" | custom-call | tf_op jit(solution)/shard_map/mix_kernel/pallas_call | solution.py:39
  (64 shorter events, 7.0 us)
Async XLA Ops:
  0.0 1.0 copy-start.3
  1.0 0.7 copy-start.8
  2.8 62.0 %copy-start.2 = (f32[8192]{0:T(1024)S(1)}, f32[8192]{0:T(1024)}, u32[]{:S(2)}) copy-start(f32[8192]{0:T(1024)} %param.24) | copy-start | bytes 98308
  2.8 23.5 %all-to-all-start = ((bf16[8,32,1152]{2,1,0:T(8,128)(2,1)}), bf16[8,32,1152]{2,1,0:T(8,128)(2,1)S(1)}, u32[]{:S(2)}, u32[]{:S(2)}) async-start(bf16[8,32,1152]{2,1,0:T(8,128)(2,1)} %pack_kernel.1), calls=%async_computation | async-start | bytes 1179648 | tf_op jit(solution)/shard_map/all_to_all | solution.py:548
  13.2 9.7 %collective-permute-start = (bf16[144,1024]{1,0:T(8,128)(2,1)}, bf16[144,1024]{1,0:T(8,128)(2,1)S(1)}, u32[]{:S(2)}, u32[]{:S(2)}) collective-permute-start(bf16[144,1024]{1,0:T(8,128)(2,1)} %get-tuple-element.83.refs_1_), channel_id=1, source_target_pairs={{0,8},{8,0},{16,24},{24,16},{1,9},{9,1},{17,25},{25,17},{2,10},{10... | collective-permute-start | bytes 884744 | tf_op jit(solution)/shard_map/ppermute | solution.py:529
  22.9 1.0 copy-start.4
  23.9 0.7 copy-start.7
  24.7 8.0 %collective-permute-start.1 = (bf16[128,1024]{1,0:T(8,128)(2,1)S(1)}, bf16[128,1024]{1,0:T(8,128)(2,1)S(1)}, u32[]{:S(2)}, u32[]{:S(2)}) collective-permute-start(bf16[128,1024]{1,0:T(8,128)(2,1)S(1)} %join_kernel.1.refs_6_), channel_id=1, source_target_pairs={{0,16},{8,24},{16,0},{24,8},{1,17},{9,25},{17,1},{25,9},{2,18},{10... | collective-permute-start | bytes 786440 | tf_op jit(solution)/shard_map/ppermute | solution.py:532
  26.3 1.2 copy-start
  27.5 1.2 copy-start.1
  28.8 0.9 copy-start.5
  29.7 0.8 copy-start.6
  34.0 2.4 %collective-permute-start.2 = (bf16[4,104,1024]{2,1,0:T(8,128)(2,1)S(1)}, bf16[4,104,1024]{2,1,0:T(8,128)(2,1)S(1)}, u32[]{:S(2)}, u32[]{:S(2)}) collective-permute-start(bf16[4,104,1024]{2,1,0:T(8,128)(2,1)S(1)} %get-tuple-element.91), channel_id=1, source_target_pairs={{0,1},{1,0},{2,3},{3,2},{4,5},{5,4},{6,7},{7,6},{8,9},{9,8},{10,11... | collective-permute-start | bytes 2555912 | tf_op jit(solution)/shard_map/ppermute | solution.py:535
  34.1 8.3 %collective-permute-start.5 = (bf16[72,1024]{1,0:T(8,128)(2,1)S(1)}, bf16[72,1024]{1,0:T(8,128)(2,1)S(1)}, u32[]{:S(2)}, u32[]{:S(2)}) collective-permute-start(bf16[72,1024]{1,0:T(8,128)(2,1)S(1)} %get-tuple-element.94), channel_id=1, source_target_pairs={{0,2},{1,3},{2,0},{3,1},{4,6},{5,7},{6,4},{7,5},{8,10},{9,11},{10,... | collective-permute-start | bytes 442376 | tf_op jit(solution)/shard_map/ppermute | solution.py:535
  36.6 13.1 %collective-permute-start.10 = (bf16[2,72,1024]{2,1,0:T(8,128)(2,1)S(1)}, bf16[2,72,1024]{2,1,0:T(8,128)(2,1)S(1)}, u32[]{:S(2)}, u32[]{:S(2)}) collective-permute-start(bf16[2,72,1024]{2,1,0:T(8,128)(2,1)S(1)} %get-tuple-element.96.refs_0_), channel_id=1, source_target_pairs={{0,16},{8,24},{16,0},{24,8},{1,17},{9,25},{17,1},{25,9},{2,18},{10... | collective-permute-start | bytes 884744 | tf_op jit(solution)/shard_map/ppermute | solution.py:532
  38.2 11.5 %collective-permute-start.9 = (bf16[2,72,1024]{2,1,0:T(8,128)(2,1)S(1)}, bf16[2,72,1024]{2,1,0:T(8,128)(2,1)S(1)}, u32[]{:S(2)}, u32[]{:S(2)}) collective-permute-start(bf16[2,72,1024]{2,1,0:T(8,128)(2,1)S(1)} %get-tuple-element.96.refs_0_), channel_id=1, source_target_pairs={{0,8},{8,0},{16,24},{24,16},{1,9},{9,1},{17,25},{25,17},{2,10},{10... | collective-permute-start | bytes 884744 | tf_op jit(solution)/shard_map/ppermute | solution.py:529
  39.6 8.9 %collective-permute-start.6 = (bf16[72,1024]{1,0:T(8,128)(2,1)S(1)}, bf16[72,1024]{1,0:T(8,128)(2,1)S(1)}, u32[]{:S(2)}, u32[]{:S(2)}) collective-permute-start(bf16[72,1024]{1,0:T(8,128)(2,1)S(1)} %get-tuple-element.95), channel_id=1, source_target_pairs={{0,3},{1,2},{2,1},{3,0},{4,7},{5,6},{6,5},{7,4},{8,11},{9,10},{10,... | collective-permute-start | bytes 442376 | tf_op jit(solution)/shard_map/ppermute | solution.py:535
  40.1 17.1 %collective-permute-start.3 = (bf16[2,72,1024]{2,1,0:T(8,128)(2,1)S(1)}, bf16[2,72,1024]{2,1,0:T(8,128)(2,1)S(1)}, u32[]{:S(2)}, u32[]{:S(2)}) collective-permute-start(bf16[2,72,1024]{2,1,0:T(8,128)(2,1)S(1)} %get-tuple-element.93), channel_id=1, source_target_pairs={{0,4},{1,5},{2,6},{3,7},{4,0},{5,1},{6,2},{7,3},{8,12},{9,13},{10,... | collective-permute-start | bytes 884744 | tf_op jit(solution)/shard_map/ppermute | solution.py:535
  48.5 9.9 %collective-permute-start.8 = (bf16[2,72,1024]{2,1,0:T(8,128)(2,1)S(1)}, bf16[2,72,1024]{2,1,0:T(8,128)(2,1)S(1)}, u32[]{:S(2)}, u32[]{:S(2)}) collective-permute-start(bf16[2,72,1024]{2,1,0:T(8,128)(2,1)S(1)} %near_kernel.1.refs_2_.refs_0_), channel_id=1, source_target_pairs={{0,16},{8,24},{16,0},{24,8},{1,17},{9,25},{17,1},{25,9},{2,18},{10... | collective-permute-start | bytes 884744 | tf_op jit(solution)/shard_map/ppermute | solution.py:532
  49.1 9.9 %collective-permute-start.7 = (bf16[2,72,1024]{2,1,0:T(8,128)(2,1)S(1)}, bf16[2,72,1024]{2,1,0:T(8,128)(2,1)S(1)}, u32[]{:S(2)}, u32[]{:S(2)}) collective-permute-start(bf16[2,72,1024]{2,1,0:T(8,128)(2,1)S(1)} %near_kernel.1.refs_2_.refs_0_), channel_id=1, source_target_pairs={{0,8},{8,0},{16,24},{24,16},{1,9},{9,1},{17,25},{25,17},{2,10},{10... | collective-permute-start | bytes 884744 | tf_op jit(solution)/shard_map/ppermute | solution.py:529
  49.7 11.1 %collective-permute-start.11 = (bf16[1,72,1024]{2,1,0:T(8,128)(2,1)S(1)}, bf16[1,72,1024]{2,1,0:T(8,128)(2,1)S(1)}, u32[]{:S(2)}, u32[]{:S(2)}) collective-permute-start(bf16[1,72,1024]{2,1,0:T(8,128)(2,1)S(1)} %get-tuple-element.97), channel_id=1, source_target_pairs={{0,8},{8,0},{16,24},{24,16},{1,9},{9,1},{17,25},{25,17},{2,10},{10... | collective-permute-start | bytes 442376 | tf_op jit(solution)/shard_map/ppermute | solution.py:529
  51.3 9.6 %collective-permute-start.12 = (bf16[1,72,1024]{2,1,0:T(8,128)(2,1)S(1)}, bf16[1,72,1024]{2,1,0:T(8,128)(2,1)S(1)}, u32[]{:S(2)}, u32[]{:S(2)}) collective-permute-start(bf16[1,72,1024]{2,1,0:T(8,128)(2,1)S(1)} %get-tuple-element.98), channel_id=1, source_target_pairs={{0,16},{8,24},{16,0},{24,8},{1,17},{9,25},{17,1},{25,9},{2,18},{10... | collective-permute-start | bytes 442376 | tf_op jit(solution)/shard_map/ppermute | solution.py:532
  60.9 11.1 %collective-permute-start.13 = (bf16[3,72,1024]{2,1,0:T(8,128)(2,1)S(1)}, bf16[3,72,1024]{2,1,0:T(8,128)(2,1)S(1)}, u32[]{:S(2)}, u32[]{:S(2)}) collective-permute-start(bf16[3,72,1024]{2,1,0:T(8,128)(2,1)S(1)} %get-tuple-element.99), channel_id=1, source_target_pairs={{0,8},{8,0},{16,24},{24,16},{1,9},{9,1},{17,25},{25,17},{2,10},{10... | collective-permute-start | bytes 1327112 | tf_op jit(solution)/shard_map/ppermute | solution.py:529
  61.5 10.6 %collective-permute-start.14 = (bf16[3,72,1024]{2,1,0:T(8,128)(2,1)S(1)}, bf16[3,72,1024]{2,1,0:T(8,128)(2,1)S(1)}, u32[]{:S(2)}, u32[]{:S(2)}) collective-permute-start(bf16[3,72,1024]{2,1,0:T(8,128)(2,1)S(1)} %get-tuple-element.100), channel_id=1, source_target_pairs={{0,16},{8,24},{16,0},{24,8},{1,17},{9,25},{17,1},{25,9},{2,18},{10... | collective-permute-start | bytes 1327112 | tf_op jit(solution)/shard_map/ppermute | solution.py:532
  63.0 9.0 %collective-permute-start.4 = (bf16[2,72,1024]{2,1,0:T(8,128)(2,1)S(1)}, bf16[2,72,1024]{2,1,0:T(8,128)(2,1)S(1)}, u32[]{:S(2)}, u32[]{:S(2)}) collective-permute-start(bf16[2,72,1024]{2,1,0:T(8,128)(2,1)S(1)} %hold_farthest.1.refs_5_), channel_id=1, source_target_pairs={{0,6},{1,7},{2,4},{3,5},{4,2},{5,3},{6,0},{7,1},{8,14},{9,15},{10,... | collective-permute-start | bytes 884744 | tf_op jit(solution)/shard_map/ppermute | solution.py:535
  72.2 12.5 %collective-permute-start.16 = (bf16[3,72,1024]{2,1,0:T(8,128)(2,1)S(1)}, bf16[3,72,1024]{2,1,0:T(8,128)(2,1)S(1)}, u32[]{:S(2)}, u32[]{:S(2)}) collective-permute-start(bf16[3,72,1024]{2,1,0:T(8,128)(2,1)S(1)} %get-tuple-element.103), channel_id=1, source_target_pairs={{0,16},{8,24},{16,0},{24,8},{1,17},{9,25},{17,1},{25,9},{2,18},{10... | collective-permute-start | bytes 1327112 | tf_op jit(solution)/shard_map/ppermute | solution.py:532
  73.7 11.0 %collective-permute-start.15 = (bf16[3,72,1024]{2,1,0:T(8,128)(2,1)S(1)}, bf16[3,72,1024]{2,1,0:T(8,128)(2,1)S(1)}, u32[]{:S(2)}, u32[]{:S(2)}) collective-permute-start(bf16[3,72,1024]{2,1,0:T(8,128)(2,1)S(1)} %get-tuple-element.102.refs_3_), channel_id=1, source_target_pairs={{0,8},{8,0},{16,24},{24,16},{1,9},{9,1},{17,25},{25,17},{2,10},{10... | collective-permute-start | bytes 1327112 | tf_op jit(solution)/shard_map/ppermute | solution.py:529
  75.3 14.7 %collective-permute-start.20 = (bf16[2,40,1024]{2,1,0:T(8,128)(2,1)S(1)}, bf16[2,40,1024]{2,1,0:T(8,128)(2,1)S(1)}, u32[]{:S(2)}, u32[]{:S(2)}) collective-permute-start(bf16[2,40,1024]{2,1,0:T(8,128)(2,1)S(1)} %get-tuple-element.115), channel_id=1, source_target_pairs={{0,4},{1,5},{2,6},{3,7},{4,0},{5,1},{6,2},{7,3},{8,12},{9,13},{10,... | collective-permute-start | bytes 491528 | tf_op jit(solution)/shard_map/ppermute | solution.py:535
  79.5 10.5 %collective-permute-start.21 = (bf16[2,40,1024]{2,1,0:T(8,128)(2,1)S(1)}, bf16[2,40,1024]{2,1,0:T(8,128)(2,1)S(1)}, u32[]{:S(2)}, u32[]{:S(2)}) collective-permute-start(bf16[2,40,1024]{2,1,0:T(8,128)(2,1)S(1)} %get-tuple-element.116), channel_id=1, source_target_pairs={{0,6},{1,7},{2,4},{3,5},{4,2},{5,3},{6,0},{7,1},{8,14},{9,15},{10,... | collective-permute-start | bytes 491528 | tf_op jit(solution)/shard_map/ppermute | solution.py:535
  81.5 8.5 %collective-permute-start.19 = (bf16[2,40,1024]{2,1,0:T(8,128)(2,1)S(1)}, bf16[2,40,1024]{2,1,0:T(8,128)(2,1)S(1)}, u32[]{:S(2)}, u32[]{:S(2)}) collective-permute-start(bf16[2,40,1024]{2,1,0:T(8,128)(2,1)S(1)} %get-tuple-element.109.refs_11_), channel_id=1, source_target_pairs={{0,2},{1,3},{2,0},{3,1},{4,6},{5,7},{6,4},{7,5},{8,10},{9,11},{10,... | collective-permute-start | bytes 491528 | tf_op jit(solution)/shard_map/ppermute | solution.py:535
  84.7 8.5 %collective-permute-start.17 = (bf16[1,72,1024]{2,1,0:T(8,128)(2,1)S(1)}, bf16[1,72,1024]{2,1,0:T(8,128)(2,1)S(1)}, u32[]{:S(2)}, u32[]{:S(2)}) collective-permute-start(bf16[1,72,1024]{2,1,0:T(8,128)(2,1)S(1)} %get-tuple-element.111), channel_id=1, source_target_pairs={{0,16},{8,24},{16,0},{24,8},{1,17},{9,25},{17,1},{25,9},{2,18},{10... | collective-permute-start | bytes 442376 | tf_op jit(solution)/shard_map/ppermute | solution.py:532
  86.0 7.1 %collective-permute-start.18 = (bf16[1,72,1024]{2,1,0:T(8,128)(2,1)S(1)}, bf16[1,72,1024]{2,1,0:T(8,128)(2,1)S(1)}, u32[]{:S(2)}, u32[]{:S(2)}) collective-permute-start(bf16[1,72,1024]{2,1,0:T(8,128)(2,1)S(1)} %get-tuple-element.112), channel_id=1, source_target_pairs={{0,8},{8,0},{16,24},{24,16},{1,9},{9,1},{17,25},{25,17},{2,10},{10... | collective-permute-start | bytes 442376 | tf_op jit(solution)/shard_map/ppermute | solution.py:529
  100.9 9.1 %collective-permute-start.22 = (bf16[9,16,1024]{2,1,0:T(8,128)(2,1)S(1)}, bf16[9,16,1024]{2,1,0:T(8,128)(2,1)S(1)}, u32[]{:S(2)}, u32[]{:S(2)}) collective-permute-start(bf16[9,16,1024]{2,1,0:T(8,128)(2,1)S(1)} %get-tuple-element.125), channel_id=1, source_target_pairs={{0,8},{8,0},{16,24},{24,16},{1,9},{9,1},{17,25},{25,17},{2,10},{10... | collective-permute-start | bytes 884744 | tf_op jit(solution)/shard_map/ppermute | solution.py:529
  101.4 8.6 %collective-permute-start.23 = (bf16[9,16,1024]{2,1,0:T(8,128)(2,1)S(1)}, bf16[9,16,1024]{2,1,0:T(8,128)(2,1)S(1)}, u32[]{:S(2)}, u32[]{:S(2)}) collective-permute-start(bf16[9,16,1024]{2,1,0:T(8,128)(2,1)S(1)} %get-tuple-element.126), channel_id=1, source_target_pairs={{0,16},{8,24},{16,0},{24,8},{1,17},{9,25},{17,1},{25,9},{2,18},{10... | collective-permute-start | bytes 884744 | tf_op jit(solution)/shard_map/ppermute | solution.py:532
  102.9 47.6 %copy-start.9 = (s32[32,2]{0,1:T(2,128)S(1)}, s32[32,2]{0,1:T(2,128)}, u32[]{:S(2)}) copy-start(s32[32,2]{0,1:T(2,128)} %param.25) | copy-start | bytes 772
  102.9 47.6 %copy-start.10 = (f32[32,2]{0,1:T(2,128)S(1)}, f32[32,2]{0,1:T(2,128)}, u32[]{:S(2)}) copy-start(f32[32,2]{0,1:T(2,128)} %param.26) | copy-start | bytes 772
  110.2 10.3 %collective-permute-start.24 = (bf16[9,16,1024]{2,1,0:T(8,128)(2,1)S(1)}, bf16[9,16,1024]{2,1,0:T(8,128)(2,1)S(1)}, u32[]{:S(2)}, u32[]{:S(2)}) collective-permute-start(bf16[9,16,1024]{2,1,0:T(8,128)(2,1)S(1)} %get-tuple-element.133), channel_id=1, source_target_pairs={{0,8},{8,0},{16,24},{24,16},{1,9},{9,1},{17,25},{25,17},{2,10},{10... | collective-permute-start | bytes 884744 | tf_op jit(solution)/shard_map/ppermute | solution.py:529
  112.6 9.9 %collective-permute-start.25 = (bf16[9,16,1024]{2,1,0:T(8,128)(2,1)S(1)}, bf16[9,16,1024]{2,1,0:T(8,128)(2,1)S(1)}, u32[]{:S(2)}, u32[]{:S(2)}) collective-permute-start(bf16[9,16,1024]{2,1,0:T(8,128)(2,1)S(1)} %get-tuple-element.134), channel_id=1, source_target_pairs={{0,16},{8,24},{16,0},{24,8},{1,17},{9,25},{17,1},{25,9},{2,18},{10... | collective-permute-start | bytes 884744 | tf_op jit(solution)/shard_map/ppermute | solution.py:532
  114.4 12.4 %collective-permute-start.28 = (bf16[9,16,1024]{2,1,0:T(8,128)(2,1)S(1)}, bf16[9,16,1024]{2,1,0:T(8,128)(2,1)S(1)}, u32[]{:S(2)}, u32[]{:S(2)}) collective-permute-start(bf16[9,16,1024]{2,1,0:T(8,128)(2,1)S(1)} %get-tuple-element.139), channel_id=1, source_target_pairs={{0,8},{8,0},{16,24},{24,16},{1,9},{9,1},{17,25},{25,17},{2,10},{10... | collective-permute-start | bytes 884744 | tf_op jit(solution)/shard_map/ppermute | solution.py:529
  114.5 14.3 %collective-permute-start.29 = (bf16[9,16,1024]{2,1,0:T(8,128)(2,1)S(1)}, bf16[9,16,1024]{2,1,0:T(8,128)(2,1)S(1)}, u32[]{:S(2)}, u32[]{:S(2)}) collective-permute-start(bf16[9,16,1024]{2,1,0:T(8,128)(2,1)S(1)} %get-tuple-element.140), channel_id=1, source_target_pairs={{0,16},{8,24},{16,0},{24,8},{1,17},{9,25},{17,1},{25,9},{2,18},{10... | collective-permute-start | bytes 884744 | tf_op jit(solution)/shard_map/ppermute | solution.py:532
  122.6 10.4 %collective-permute-start.26 = (bf16[9,16,1024]{2,1,0:T(8,128)(2,1)S(1)}, bf16[9,16,1024]{2,1,0:T(8,128)(2,1)S(1)}, u32[]{:S(2)}, u32[]{:S(2)}) collective-permute-start(bf16[9,16,1024]{2,1,0:T(8,128)(2,1)S(1)} %get-tuple-element.137), channel_id=1, source_target_pairs={{0,8},{8,0},{16,24},{24,16},{1,9},{9,1},{17,25},{25,17},{2,10},{10... | collective-permute-start | bytes 884744 | tf_op jit(solution)/shard_map/ppermute | solution.py:529
  122.8 11.3 %collective-permute-start.27 = (bf16[9,16,1024]{2,1,0:T(8,128)(2,1)S(1)}, bf16[9,16,1024]{2,1,0:T(8,128)(2,1)S(1)}, u32[]{:S(2)}, u32[]{:S(2)}) collective-permute-start(bf16[9,16,1024]{2,1,0:T(8,128)(2,1)S(1)} %get-tuple-element.138), channel_id=1, source_target_pairs={{0,16},{8,24},{16,0},{24,8},{1,17},{9,25},{17,1},{25,9},{2,18},{10... | collective-permute-start | bytes 884744 | tf_op jit(solution)/shard_map/ppermute | solution.py:532
  124.6 11.9 %collective-permute-start.34 = (bf16[9,16,1024]{2,1,0:T(8,128)(2,1)S(1)}, bf16[9,16,1024]{2,1,0:T(8,128)(2,1)S(1)}, u32[]{:S(2)}, u32[]{:S(2)}) collective-permute-start(bf16[9,16,1024]{2,1,0:T(8,128)(2,1)S(1)} %get-tuple-element.145.refs_6_), channel_id=1, source_target_pairs={{0,6},{1,7},{2,4},{3,5},{4,2},{5,3},{6,0},{7,1},{8,14},{9,15},{10,... | collective-permute-start | bytes 884744 | tf_op jit(solution)/shard_map/ppermute | solution.py:535
  129.0 10.6 %collective-permute-start.32 = (bf16[9,16,1024]{2,1,0:T(8,128)(2,1)S(1)}, bf16[9,16,1024]{2,1,0:T(8,128)(2,1)S(1)}, u32[]{:S(2)}, u32[]{:S(2)}) collective-permute-start(bf16[9,16,1024]{2,1,0:T(8,128)(2,1)S(1)} %get-tuple-element.151), channel_id=1, source_target_pairs={{0,8},{8,0},{16,24},{24,16},{1,9},{9,1},{17,25},{25,17},{2,10},{10... | collective-permute-start | bytes 884744 | tf_op jit(solution)/shard_map/ppermute | solution.py:529
  129.2 10.4 %collective-permute-start.33 = (bf16[9,16,1024]{2,1,0:T(8,128)(2,1)S(1)}, bf16[9,16,1024]{2,1,0:T(8,128)(2,1)S(1)}, u32[]{:S(2)}, u32[]{:S(2)}) collective-permute-start(bf16[9,16,1024]{2,1,0:T(8,128)(2,1)S(1)} %get-tuple-element.152), channel_id=1, source_target_pairs={{0,16},{8,24},{16,0},{24,8},{1,17},{9,25},{17,1},{25,9},{2,18},{10... | collective-permute-start | bytes 884744 | tf_op jit(solution)/shard_map/ppermute | solution.py:532
  134.3 6.8 %collective-permute-start.30 = (bf16[9,16,1024]{2,1,0:T(8,128)(2,1)S(1)}, bf16[9,16,1024]{2,1,0:T(8,128)(2,1)S(1)}, u32[]{:S(2)}, u32[]{:S(2)}) collective-permute-start(bf16[9,16,1024]{2,1,0:T(8,128)(2,1)S(1)} %get-tuple-element.148), channel_id=1, source_target_pairs={{0,8},{8,0},{16,24},{24,16},{1,9},{9,1},{17,25},{25,17},{2,10},{10... | collective-permute-start | bytes 884744 | tf_op jit(solution)/shard_map/ppermute | solution.py:529
  135.2 6.7 %collective-permute-start.31 = (bf16[9,16,1024]{2,1,0:T(8,128)(2,1)S(1)}, bf16[9,16,1024]{2,1,0:T(8,128)(2,1)S(1)}, u32[]{:S(2)}, u32[]{:S(2)}) collective-permute-start(bf16[9,16,1024]{2,1,0:T(8,128)(2,1)S(1)} %get-tuple-element.149), channel_id=1, source_target_pairs={{0,16},{8,24},{16,0},{24,8},{1,17},{9,25},{17,1},{25,9},{2,18},{10... | collective-permute-start | bytes 884744 | tf_op jit(solution)/shard_map/ppermute | solution.py:532
  136.5 11.1 %collective-permute-start.36 = (bf16[9,16,1024]{2,1,0:T(8,128)(2,1)S(1)}, bf16[9,16,1024]{2,1,0:T(8,128)(2,1)S(1)}, u32[]{:S(2)}, u32[]{:S(2)}) collective-permute-start(bf16[9,16,1024]{2,1,0:T(8,128)(2,1)S(1)} %get-tuple-element.153), channel_id=1, source_target_pairs={{0,4},{1,5},{2,6},{3,7},{4,0},{5,1},{6,2},{7,3},{8,12},{9,13},{10,... | collective-permute-start | bytes 884744 | tf_op jit(solution)/shard_map/ppermute | solution.py:535
  139.7 8.6 %collective-permute-start.35 = (bf16[9,16,1024]{2,1,0:T(8,128)(2,1)S(1)}, bf16[9,16,1024]{2,1,0:T(8,128)(2,1)S(1)}, u32[]{:S(2)}, u32[]{:S(2)}) collective-permute-start(bf16[9,16,1024]{2,1,0:T(8,128)(2,1)S(1)} %finish_1.1), channel_id=1, source_target_pairs={{0,2},{1,3},{2,0},{3,1},{4,6},{5,7},{6,4},{7,5},{8,10},{9,11},{10,... | collective-permute-start | bytes 884744 | tf_op jit(solution)/shard_map/ppermute | solution.py:535
  148.4 2.1 %collective-permute-start.37 = (bf16[2,9,16,1024]{3,2,1,0:T(8,128)(2,1)S(1)}, bf16[2,9,16,1024]{3,2,1,0:T(8,128)(2,1)S(1)}, u32[]{:S(2)}, u32[]{:S(2)}) collective-permute-start(bf16[2,9,16,1024]{3,2,1,0:T(8,128)(2,1)S(1)} %second_kernel.1), channel_id=1, source_target_pairs={{0,1},{1,0},{2,3},{3,2},{4,5},{5,4},{6,7},{7,6},{8,9},{9,8},{10,11... | collective-permute-start | bytes 1769480 | tf_op jit(solution)/shard_map/ppermute | solution.py:535

commit v4 on v3

--- a/solution.py
+++ b/solution.py
@@ -658,9 +658,13 @@
         half_message_kernel, message(1), 0, (rx3, ry3), after=(carry[2],), name="half_3"
     )
     fx3, fy3 = over_x(to_x), over_y(to_y)
-    carry = project(2, [(far, 0), (rx2, 0), (ry2, 0)], [(ry3, 2), (rx3, 2)], carry, (stream1, stream2, stream3))
+    carry = project(2, [(far, 0), (rx2, 0), (ry2, 0)], [(ry3, 2), (rx3, 2)], carry)
     active_far, active = project(
-        3, [(farthest, 0), (rx3, 0), (ry3, 0)], [(fy3, 0), (fx3, 0)], carry
+        3,
+        [(farthest, 0), (rx3, 0), (ry3, 0)],
+        [(fy3, 0), (fx3, 0)],
+        carry,
+        (stream1, stream2, stream3),
     )
 
     wd = w_down.reshape(w_down.shape[1], features)

time: 153 us -> 153 us (level)
  starting transfers between devices: 55.4 us -> 52 us
  waiting for transfers between devices: 51.9 us -> 54.8 us
    ppermute x13, starting transfers between devices: 17.9 us -> 12.7 us  [over_y(): return lax.ppermute(v, 'seq', [(i, i ^ 2) for i in range(4)])]
    ppermute x13, waiting for transfers between devices: 15.9 us -> 20.7 us  [over_x(): return lax.ppermute(v, 'seq', [(i, i ^ 1) for i in range(4)])]
    ppermute x12, starting transfers between devices: 18.7 us -> 20.5 us  [along(): return lax.ppermute(v, 'exp', [(i, i ^ mask) for i in range(owners)])]
    ppermute x12, waiting for transfers between devices: 26.9 us -> 25.3 us  [along(): return lax.ppermute(v, 'exp', [(i, i ^ mask) for i in range(owners)])]
where the time goes in v4:
time: 153 us; the launch traced here: 152 us
  waiting for transfers between devices  54.8 us (36%)
  starting transfers between devices  52 us (34%)
  Pallas kernels  37.2 us (24%)
  local copies, waits for them, and re-layouts  7.61 us (5%)
    ppermute x12, waiting for transfers between devices, along(): return lax.ppermute(v, 'exp', [(i, i ^ mask) for i in range(owners)])  25.3 us
    ppermute x13, waiting for transfers between devices, over_x(): return lax.ppermute(v, 'seq', [(i, i ^ 1) for i in range(4)])  20.7 us
    ppermute x12, starting transfers between devices, along(): return lax.ppermute(v, 'exp', [(i, i ^ mask) for i in range(owners)])  20.5 us
    pallas_call x22, Pallas kernels, block_call(): pl.pallas_call(kernel, name=name or getattr(body, 'func', body).__name__,...  14.8 us
    pallas_call x4, Pallas kernels, up_project(): pl.pallas_call(functools.partial(up_kernel, carry is None, features, len(...  13.2 us
    ppermute x13, starting transfers between devices, over_y(): return lax.ppermute(v, 'seq', [(i, i ^ 2) for i in range(4)])  12.7 us
    ppermute x13, starting transfers between devices, over_x(): return lax.ppermute(v, 'seq', [(i, i ^ 1) for i in range(4)])  12.4 us
    pallas_call x2, Pallas kernels, down_project(): pl.pallas_call(functools.partial(down_kernel, groups), name=name, grid=(8...  9.3 us
  transfers between devices with their start and end apart: 39, of which 22 were waited for; matrix products, arithmetic and copies ran while one was open for 0% of the time, Pallas kernels for 16%

profile of v4, /device:TPU:0, one launch (start us, length us, event | category | flops | bytes accessed | tf_op | source)
XLA Modules:
  0.0 152.0 jit_solution(11625122162245089034)
XLA Ops:
  0.0 1.0 copy-done.3
  1.0 0.7 copy-done.8
  1.7 1.0 pack_kernel.1
  2.8 6.3 %all-to-all-start = ((bf16[8,32,1152]{2,1,0:T(8,128)(2,1)}), bf16[8,32,1152]{2,1,0:T(8,128)(2,1)S(1)}, u32[]{:S(2)}, u32[]{:S(2)}) async-start(bf16[8,32,1152]{2,1,0:T(8,128)(2,1)} %pack_kernel.1), calls=%async_computation | async-start | bytes 1179648 | tf_op jit(solution)/shard_map/all_to_all | solution.py:548
  9.1 4.1 %state_kernel.1 = (bf16[144,1024]{1,0:T(8,128)(2,1)}, bf16[128,1024]{1,0:T(8,128)(2,1)}) custom-call(s32[1]{0:T(128)} %bitcast.3.refs_0_, bf16[256,1024]{1,0:T(8,128)(2,1)} %refs_1_.5, bf16[256,128]{1,0:T(8,128)(2,1)} %refs_2_.3, f32[16,256]{1,0:T(8,128)} %bitcast.30, f32[1,16]{1,0:T(1,128)} %bitcast.32, f32[1024,128]{1,0:T(8,128)} %bitcast.29), custom_call_target="tpu_custom_call" | custom-call | tf_op jit(solution)/shard_map/state_kernel/pallas_call | solution.py:39
  13.2 1.6 %collective-permute-start = (bf16[144,1024]{1,0:T(8,128)(2,1)}, bf16[144,1024]{1,0:T(8,128)(2,1)S(1)}, u32[]{:S(2)}, u32[]{:S(2)}) collective-permute-start(bf16[144,1024]{1,0:T(8,128)(2,1)} %get-tuple-element.83.refs_1_), channel_id=1, source_target_pairs={{0,8},{8,0},{16,24},{24,16},{1,9},{9,1},{17,25},{25,17},{2,10},{10... | collective-permute-start | bytes 884744 | tf_op jit(solution)/shard_map/ppermute | solution.py:529
  14.8 4.7 %intra_kernel.1 = (f32[256,1024]{1,0:T(8,128)}, f32[256,1024]{1,0:T(8,128)}, f32[8,128]{1,0:T(8,128)}) custom-call(bf16[256,1024]{1,0:T(8,128)(2,1)} %refs_1_.5, bf16[256,1024]{1,0:T(8,128)(2,1)} %refs_1_.4, bf16[256,128]{1,0:T(8,128)(2,1)} %refs_2_.3, bf16[256,128]{1,0:T(8,128)(2,1)} %refs_4_.1, f32[16,256]{1,0:T(8,128)} %bitcast.31, f32[1,16]{1,0:T(1,128)} %bitcast.33, ...), custom_call_target="tpu_custom_call" | custom-call | tf_op jit(solution)/shard_map/intra_kernel/pallas_call | solution.py:39
  19.5 3.4 %collective-permute-done.refs_2_.refs_5_ = bf16[144,1024]{1,0:T(8,128)(2,1)S(1)} collective-permute-done((bf16[144,1024]{1,0:T(8,128)(2,1)}, bf16[144,1024]{1,0:T(8,128)(2,1)S(1)}, u32[]{:S(2)}, u32[]{:S(2)}) %collective-permute-start) | collective-permute-done | bytes 294944 | tf_op jit(solution)/shard_map/ppermute | solution.py:529
  22.9 1.0 copy-done.4
  23.9 0.7 copy-done.7
  24.7 1.6 %collective-permute-start.1 = (bf16[128,1024]{1,0:T(8,128)(2,1)S(1)}, bf16[128,1024]{1,0:T(8,128)(2,1)S(1)}, u32[]{:S(2)}, u32[]{:S(2)}) collective-permute-start(bf16[128,1024]{1,0:T(8,128)(2,1)S(1)} %join_kernel.1.refs_6_), channel_id=1, source_target_pairs={{0,16},{8,24},{16,0},{24,8},{1,17},{9,25},{17,1},{25,9},{2,18},{10... | collective-permute-start | bytes 786440 | tf_op jit(solution)/shard_map/ppermute | solution.py:532
  26.3 1.2 copy-done
  27.5 1.2 copy-done.1
  28.8 0.9 copy-done.5
  29.7 0.8 copy-done.6
  30.9 1.8 %collective-permute-done.1.refs_6_ = bf16[128,1024]{1,0:T(8,128)(2,1)S(1)} collective-permute-done((bf16[128,1024]{1,0:T(8,128)(2,1)S(1)}, bf16[128,1024]{1,0:T(8,128)(2,1)S(1)}, u32[]{:S(2)}, u32[]{:S(2)}) %collective-permute-start.1) | collective-permute-done | bytes 262176 | tf_op jit(solution)/shard_map/ppermute | solution.py:532
  32.7 1.3 stream_kernel.1
  34.1 1.3 collective-permute-start.5
  35.4 1.0 collective-permute-done.2.refs_1_
  36.6 1.6 %collective-permute-start.10 = (bf16[2,72,1024]{2,1,0:T(8,128)(2,1)S(1)}, bf16[2,72,1024]{2,1,0:T(8,128)(2,1)S(1)}, u32[]{:S(2)}, u32[]{:S(2)}) collective-permute-start(bf16[2,72,1024]{2,1,0:T(8,128)(2,1)S(1)} %get-tuple-element.96.refs_0_), channel_id=1, source_target_pairs={{0,16},{8,24},{16,0},{24,8},{1,17},{9,25},{17,1},{25,9},{2,18},{10... | collective-permute-start | bytes 884744 | tf_op jit(solution)/shard_map/ppermute | solution.py:532
  38.2 1.5 collective-permute-start.9
  40.1 2.4 %collective-permute-start.3 = (bf16[2,72,1024]{2,1,0:T(8,128)(2,1)S(1)}, bf16[2,72,1024]{2,1,0:T(8,128)(2,1)S(1)}, u32[]{:S(2)}, u32[]{:S(2)}) collective-permute-start(bf16[2,72,1024]{2,1,0:T(8,128)(2,1)S(1)} %get-tuple-element.93), channel_id=1, source_target_pairs={{0,4},{1,5},{2,6},{3,7},{4,0},{5,1},{6,2},{7,3},{8,12},{9,13},{10,... | collective-permute-start | bytes 884744 | tf_op jit(solution)/shard_map/ppermute | solution.py:535
  42.5 6.0 %collective-permute-done.6.refs_1_ = bf16[72,1024]{1,0:T(8,128)(2,1)S(1)} collective-permute-done((bf16[72,1024]{1,0:T(8,128)(2,1)S(1)}, bf16[72,1024]{1,0:T(8,128)(2,1)S(1)}, u32[]{:S(2)}, u32[]{:S(2)}) %collective-permute-start.6) | collective-permute-done | bytes 147488 | tf_op jit(solution)/shard_map/ppermute | solution.py:535
  48.5 0.6 collective-permute-start.8
  49.7 1.5 %collective-permute-start.11 = (bf16[1,72,1024]{2,1,0:T(8,128)(2,1)S(1)}, bf16[1,72,1024]{2,1,0:T(8,128)(2,1)S(1)}, u32[]{:S(2)}, u32[]{:S(2)}) collective-permute-start(bf16[1,72,1024]{2,1,0:T(8,128)(2,1)S(1)} %get-tuple-element.97), channel_id=1, source_target_pairs={{0,8},{8,0},{16,24},{24,16},{1,9},{9,1},{17,25},{25,17},{2,10},{10... | collective-permute-start | bytes 442376 | tf_op jit(solution)/shard_map/ppermute | solution.py:529
  51.3 1.5 collective-permute-start.12
  52.8 4.5 %collective-permute-done.3.refs_1_.refs_0_ = bf16[2,72,1024]{2,1,0:T(8,128)(2,1)S(1)} collective-permute-done((bf16[2,72,1024]{2,1,0:T(8,128)(2,1)S(1)}, bf16[2,72,1024]{2,1,0:T(8,128)(2,1)S(1)}, u32[]{:S(2)}, u32[]{:S(2)}) %collective-permute-start.3) | collective-permute-done | bytes 294944 | tf_op jit(solution)/shard_map/ppermute | solution.py:535
  57.2 1.2 collective-permute-done.8.refs_2_
  58.5 0.6 collective-permute-done.7.refs_1_
  59.1 1.8 %collective-permute-done.11.refs_3_.refs_4_ = bf16[1,72,1024]{2,1,0:T(8,128)(2,1)S(1)} collective-permute-done((bf16[1,72,1024]{2,1,0:T(8,128)(2,1)S(1)}, bf16[1,72,1024]{2,1,0:T(8,128)(2,1)S(1)}, u32[]{:S(2)}, u32[]{:S(2)}) %collective-permute-start.11) | collective-permute-done | bytes 147488 | tf_op jit(solution)/shard_map/ppermute | solution.py:529
  60.9 0.6 collective-permute-start.13
  61.5 1.5 collective-permute-start.14
  63.0 1.8 %collective-permute-start.4 = (bf16[2,72,1024]{2,1,0:T(8,128)(2,1)S(1)}, bf16[2,72,1024]{2,1,0:T(8,128)(2,1)S(1)}, u32[]{:S(2)}, u32[]{:S(2)}) collective-permute-start(bf16[2,72,1024]{2,1,0:T(8,128)(2,1)S(1)} %hold_farthest.1.refs_5_), channel_id=1, source_target_pairs={{0,6},{1,7},{2,4},{3,5},{4,2},{5,3},{6,0},{7,1},{8,14},{9,15},{10,... | collective-permute-start | bytes 884744 | tf_op jit(solution)/shard_map/ppermute | solution.py:535
  64.8 3.3 %up_0.1 = (f32[288,512]{1,0:T(8,128)S(1)}, f32[288,512]{1,0:T(8,128)S(1)}, f32[288,128]{1,0:T(8,128)S(1)}) custom-call(s32[1]{0:T(128)} %bitcast.refs_0_.me, bf16[2,72,1024]{2,1,0:T(8,128)(2,1)S(1)} %get-tuple-element.96.refs_0_, bf16[2,72,1024]{2,1,0:T(8,128)(2,1)S(1)} %collective-permute-done.9.refs_0_.refs_1_, ...), custom_call_target="tpu_custom_call" | custom-call | tf_op jit(solution)/shard_map/up_0/pallas_call | solution.py:282
  68.1 3.9 %collective-permute-done.4.refs_0_ = bf16[2,72,1024]{2,1,0:T(8,128)(2,1)S(1)} collective-permute-done((bf16[2,72,1024]{2,1,0:T(8,128)(2,1)S(1)}, bf16[2,72,1024]{2,1,0:T(8,128)(2,1)S(1)}, u32[]{:S(2)}, u32[]{:S(2)}) %collective-permute-start.4) | collective-permute-done | bytes 294944 | tf_op jit(solution)/shard_map/ppermute | solution.py:535
  72.2 1.5 collective-permute-start.16
  73.7 1.6 %collective-permute-start.15 = (bf16[3,72,1024]{2,1,0:T(8,128)(2,1)S(1)}, bf16[3,72,1024]{2,1,0:T(8,128)(2,1)S(1)}, u32[]{:S(2)}, u32[]{:S(2)}) collective-permute-start(bf16[3,72,1024]{2,1,0:T(8,128)(2,1)S(1)} %get-tuple-element.102.refs_3_), channel_id=1, source_target_pairs={{0,8},{8,0},{16,24},{24,16},{1,9},{9,1},{17,25},{25,17},{2,10},{10... | collective-permute-start | bytes 1327112 | tf_op jit(solution)/shard_map/ppermute | solution.py:529
  75.3 4.2 %collective-permute-start.20 = (bf16[2,40,1024]{2,1,0:T(8,128)(2,1)S(1)}, bf16[2,40,1024]{2,1,0:T(8,128)(2,1)S(1)}, u32[]{:S(2)}, u32[]{:S(2)}) collective-permute-start(bf16[2,40,1024]{2,1,0:T(8,128)(2,1)S(1)} %get-tuple-element.118), channel_id=1, source_target_pairs={{0,4},{1,5},{2,6},{3,7},{4,0},{5,1},{6,2},{7,3},{8,12},{9,13},{10,... | collective-permute-start | bytes 491528 | tf_op jit(solution)/shard_map/ppermute | solution.py:535
  79.5 2.0 %collective-permute-start.21 = (bf16[2,40,1024]{2,1,0:T(8,128)(2,1)S(1)}, bf16[2,40,1024]{2,1,0:T(8,128)(2,1)S(1)}, u32[]{:S(2)}, u32[]{:S(2)}) collective-permute-start(bf16[2,40,1024]{2,1,0:T(8,128)(2,1)S(1)} %get-tuple-element.119), channel_id=1, source_target_pairs={{0,6},{1,7},{2,4},{3,5},{4,2},{5,3},{6,0},{7,1},{8,14},{9,15},{10,... | collective-permute-start | bytes 491528 | tf_op jit(solution)/shard_map/ppermute | solution.py:535
  81.5 3.2 %up_1.1 = (f32[288,512]{1,0:T(8,128)S(1)}, f32[288,512]{1,0:T(8,128)S(1)}, f32[288,128]{1,0:T(8,128)S(1)}) custom-call(s32[1]{0:T(128)} %bitcast.refs_0_.me, bf16[2,72,1024]{2,1,0:T(8,128)(2,1)S(1)} %near_kernel.1.refs_2_.refs_0_, ...), custom_call_target="tpu_custom_call", output_to_operand_aliasing={{0}: (9, {}), {1}: (10, {}), {2}: (11, {})} | custom-call | tf_op jit(solution)/shard_map/up_1/pallas_call | solution.py:282
  84.7 1.3 collective-permute-start.17
  86.0 0.7 collective-permute-start.18
  86.8 3.2 %up_2.1 = (f32[288,512]{1,0:T(8,128)S(1)}, f32[288,512]{1,0:T(8,128)S(1)}, f32[288,128]{1,0:T(8,128)S(1)}) custom-call(s32[1]{0:T(128)} %bitcast.refs_0_.me, bf16[2,72,1024]{2,1,0:T(8,128)(2,1)S(1)} %collective-permute-done.3.refs_1_.refs_0_, ...), custom_call_target="tpu_custom_call", output_to_operand_aliasing={{0}: (9, {}), {1}: (10, {}), {2}: (11, {})} | custom-call | tf_op jit(solution)/shard_map/up_2/pallas_call | solution.py:282
  90.0 1.2 collective-permute-done.18.refs_4_
  91.2 3.5 %up_3.1 = (bf16[72,512]{1,0:T(8,128)(2,1)S(1)}, bf16[216,512]{1,0:T(8,128)(2,1)S(1)}) custom-call(s32[1]{0:T(128)} %bitcast.refs_0_.me, bf16[2,72,1024]{2,1,0:T(8,128)(2,1)S(1)} %collective-permute-done.4.refs_0_, bf16[3,72,1024]{2,1,0:T(8,128)(2,1)S(1)} %collective-permute-done.15.refs_0_.refs_4_.refs_1_, ...), custom_call_target="tpu_custom_call" | custom-call | tf_op jit(solution)/shard_map/up_3/pallas_call | solution.py:282
  94.7 4.2 %down_through.1 = (bf16[9,16,1024]{2,1,0:T(8,128)(2,1)S(1)}, bf16[9,16,1024]{2,1,0:T(8,128)(2,1)S(1)}, bf16[9,16,1024]{2,1,0:T(8,128)(2,1)S(1)}, bf16[9,16,1024]{2,1,0:T(8,128)(2,1)S(1)}) custom-call(bf16[72,512]{1,0:T(8,128)(2,1)S(1)} %get-tuple-element.124.act_ref, bf16[512,8192]{1,0:T(8,128)(2,1)} %bitcast.27), custom_call_target="tpu_custom_call" | custom-call | tf_op jit(solution)/shard_map/down_through/pallas_call | solution.py:372
  98.9 0.8 collective-permute-start.22
  99.7 0.6 collective-permute-start.23
  100.3 5.1 %down_rest.1 = (bf16[9,16,1024]{2,1,0:T(8,128)(2,1)S(1)}, bf16[9,16,1024]{2,1,0:T(8,128)(2,1)S(1)}, bf16[9,16,1024]{2,1,0:T(8,128)(2,1)S(1)}, bf16[9,16,1024]{2,...) custom-call(bf16[216,512]{1,0:T(8,128)(2,1)S(1)} %get-tuple-element., ...), custom_call_target="tpu_custom_call" | custom-call | tf_op jit(solution)/shard_map/down_rest/pallas_call | solution.py:372
  105.4 2.4 %collective-permute-done.22.refs_0_ = bf16[9,16,1024]{2,1,0:T(8,128)(2,1)S(1)} collective-permute-done((bf16[9,16,1024]{2,1,0:T(8,128)(2,1)S(1)}, bf16[9,16,1024]{2,1,0:T(8,128)(2,1)S(1)}, u32[]{:S(2)}, u32[]{:S(2)}) %collective-permute-start.22) | collective-permute-done | bytes 294944 | tf_op jit(solution)/shard_map/ppermute | solution.py:529
  108.4 2.0 %collective-permute-start.24 = (bf16[9,16,1024]{2,1,0:T(8,128)(2,1)S(1)}, bf16[9,16,1024]{2,1,0:T(8,128)(2,1)S(1)}, u32[]{:S(2)}, u32[]{:S(2)}) collective-permute-start(bf16[9,16,1024]{2,1,0:T(8,128)(2,1)S(1)} %get-tuple-element.133), channel_id=1, source_target_pairs={{0,8},{8,0},{16,24},{24,16},{1,9},{9,1},{17,25},{25,17},{2,10},{10... | collective-permute-start | bytes 884744 | tf_op jit(solution)/shard_map/ppermute | solution.py:529
  110.6 1.9 %collective-permute-start.29 = (bf16[9,16,1024]{2,1,0:T(8,128)(2,1)S(1)}, bf16[9,16,1024]{2,1,0:T(8,128)(2,1)S(1)}, u32[]{:S(2)}, u32[]{:S(2)}) collective-permute-start(bf16[9,16,1024]{2,1,0:T(8,128)(2,1)S(1)} %get-tuple-element.140), channel_id=1, source_target_pairs={{0,16},{8,24},{16,0},{24,8},{1,17},{9,25},{17,1},{25,9},{2,18},{10... | collective-permute-start | bytes 884744 | tf_op jit(solution)/shard_map/ppermute | solution.py:532
  112.6 5.7 %collective-permute-done.24.refs_1_ = bf16[9,16,1024]{2,1,0:T(8,128)(2,1)S(1)} collective-permute-done((bf16[9,16,1024]{2,1,0:T(8,128)(2,1)S(1)}, bf16[9,16,1024]{2,1,0:T(8,128)(2,1)S(1)}, u32[]{:S(2)}, u32[]{:S(2)}) %collective-permute-start.24) | collective-permute-done | bytes 294944 | tf_op jit(solution)/shard_map/ppermute | solution.py:529
  118.3 2.0 %collective-permute-done.25.refs_2_ = bf16[9,16,1024]{2,1,0:T(8,128)(2,1)S(1)} collective-permute-done((bf16[9,16,1024]{2,1,0:T(8,128)(2,1)S(1)}, bf16[9,16,1024]{2,1,0:T(8,128)(2,1)S(1)}, u32[]{:S(2)}, u32[]{:S(2)}) %collective-permute-start.25) | collective-permute-done | bytes 294944 | tf_op jit(solution)/shard_map/ppermute | solution.py:532
  120.8 1.9 %collective-permute-start.34 = (bf16[9,16,1024]{2,1,0:T(8,128)(2,1)S(1)}, bf16[9,16,1024]{2,1,0:T(8,128)(2,1)S(1)}, u32[]{:S(2)}, u32[]{:S(2)}) collective-permute-start(bf16[9,16,1024]{2,1,0:T(8,128)(2,1)S(1)} %get-tuple-element.145.refs_6_), channel_id=1, source_target_pairs={{0,6},{1,7},{2,4},{3,5},{4,2},{5,3},{6,0},{7,1},{8,14},{9,15},{10,... | collective-permute-start | bytes 884744 | tf_op jit(solution)/shard_map/ppermute | solution.py:535
  122.7 1.9 %collective-permute-done.28.refs_0_ = bf16[9,16,1024]{2,1,0:T(8,128)(2,1)S(1)} collective-permute-done((bf16[9,16,1024]{2,1,0:T(8,128)(2,1)S(1)}, bf16[9,16,1024]{2,1,0:T(8,128)(2,1)S(1)}, u32[]{:S(2)}, u32[]{:S(2)}) %collective-permute-start.28) | collective-permute-done | bytes 294944 | tf_op jit(solution)/shard_map/ppermute | solution.py:529
  124.6 2.0 %collective-permute-done.29.refs_1_ = bf16[9,16,1024]{2,1,0:T(8,128)(2,1)S(1)} collective-permute-done((bf16[9,16,1024]{2,1,0:T(8,128)(2,1)S(1)}, bf16[9,16,1024]{2,1,0:T(8,128)(2,1)S(1)}, u32[]{:S(2)}, u32[]{:S(2)}) %collective-permute-start.29) | collective-permute-done | bytes 294944 | tf_op jit(solution)/shard_map/ppermute | solution.py:532
  127.1 3.8 %collective-permute-done.26.refs_1_ = bf16[9,16,1024]{2,1,0:T(8,128)(2,1)S(1)} collective-permute-done((bf16[9,16,1024]{2,1,0:T(8,128)(2,1)S(1)}, bf16[9,16,1024]{2,1,0:T(8,128)(2,1)S(1)}, u32[]{:S(2)}, u32[]{:S(2)}) %collective-permute-start.26) | collective-permute-done | bytes 294944 | tf_op jit(solution)/shard_map/ppermute | solution.py:529
  130.9 1.3 collective-permute-done.27.refs_2_
  132.3 0.9 collective-permute-start.30
  133.4 6.3 %collective-permute-start.36 = (bf16[9,16,1024]{2,1,0:T(8,128)(2,1)S(1)}, bf16[9,16,1024]{2,1,0:T(8,128)(2,1)S(1)}, u32[]{:S(2)}, u32[]{:S(2)}) collective-permute-start(bf16[9,16,1024]{2,1,0:T(8,128)(2,1)S(1)} %get-tuple-element.153), channel_id=1, source_target_pairs={{0,4},{1,5},{2,6},{3,7},{4,0},{5,1},{6,2},{7,3},{8,12},{9,13},{10,... | collective-permute-start | bytes 884744 | tf_op jit(solution)/shard_map/ppermute | solution.py:535
  140.1 7.6 %collective-permute-done.36.refs_2_.refs_6_ = bf16[9,16,1024]{2,1,0:T(8,128)(2,1)S(1)} collective-permute-done((bf16[9,16,1024]{2,1,0:T(8,128)(2,1)S(1)}, bf16[9,16,1024]{2,1,0:T(8,128)(2,1)S(1)}, u32[]{:S(2)}, u32[]{:S(2)}) %collective-permute-start.36) | collective-permute-done | bytes 294944 | tf_op jit(solution)/shard_map/ppermute | solution.py:535
  148.1 2.0 %collective-permute-done.37.refs_3_ = bf16[2,9,16,1024]{3,2,1,0:T(8,128)(2,1)S(1)} collective-permute-done((bf16[2,9,16,1024]{3,2,1,0:T(8,128)(2,1)S(1)}, bf16[2,9,16,1024]{3,2,1,0:T(8,128)(2,1)S(1)}, u32[]{:S(2)}, u32[]{:S(2)}) %collective-permute-start.37) | collective-permute-done | bytes 589856 | tf_op jit(solution)/shard_map/ppermute | solution.py:535
  150.1 1.9 %mix_kernel.1 = bf16[32,8192]{1,0:T(8,128)(2,1)} custom-call(s32[1]{0:T(128)} %bitcast.refs_0_.me, s32[2,32]{1,0:T(2,128)S(1)} %bitcast.17, f32[2,32]{1,0:T(2,128)S(1)} %bitcast.18, bf16[2,9,16,1024]{3,2,1,0:T(8,128)(2,1)S(1)} %collective-permute-done.37.refs_3_, bf16[9,16,1024]{2,1,0:T(8,128)(2,1)S(1)} %finish_0.1.refs_0_.refs_4_, ...), custom_call_target="tpu_custom_call" | custom-call | tf_op jit(solution)/shard_map/mix_kernel/pallas_call | solution.py:39
  (64 shorter events, 5.1 us)
Async XLA Ops:
  0.0 1.0 copy-start.3
  1.0 0.7 copy-start.8
  2.8 62.0 %copy-start.2 = (f32[8192]{0:T(1024)S(1)}, f32[8192]{0:T(1024)}, u32[]{:S(2)}) copy-start(f32[8192]{0:T(1024)} %param.24) | copy-start | bytes 98308
  2.8 23.5 %all-to-all-start = ((bf16[8,32,1152]{2,1,0:T(8,128)(2,1)}), bf16[8,32,1152]{2,1,0:T(8,128)(2,1)S(1)}, u32[]{:S(2)}, u32[]{:S(2)}) async-start(bf16[8,32,1152]{2,1,0:T(8,128)(2,1)} %pack_kernel.1), calls=%async_computation | async-start | bytes 1179648 | tf_op jit(solution)/shard_map/all_to_all | solution.py:548
  13.2 9.7 %collective-permute-start = (bf16[144,1024]{1,0:T(8,128)(2,1)}, bf16[144,1024]{1,0:T(8,128)(2,1)S(1)}, u32[]{:S(2)}, u32[]{:S(2)}) collective-permute-start(bf16[144,1024]{1,0:T(8,128)(2,1)} %get-tuple-element.83.refs_1_), channel_id=1, source_target_pairs={{0,8},{8,0},{16,24},{24,16},{1,9},{9,1},{17,25},{25,17},{2,10},{10... | collective-permute-start | bytes 884744 | tf_op jit(solution)/shard_map/ppermute | solution.py:529
  22.9 1.0 copy-start.4
  23.9 0.7 copy-start.7
  24.7 8.0 %collective-permute-start.1 = (bf16[128,1024]{1,0:T(8,128)(2,1)S(1)}, bf16[128,1024]{1,0:T(8,128)(2,1)S(1)}, u32[]{:S(2)}, u32[]{:S(2)}) collective-permute-start(bf16[128,1024]{1,0:T(8,128)(2,1)S(1)} %join_kernel.1.refs_6_), channel_id=1, source_target_pairs={{0,16},{8,24},{16,0},{24,8},{1,17},{9,25},{17,1},{25,9},{2,18},{10... | collective-permute-start | bytes 786440 | tf_op jit(solution)/shard_map/ppermute | solution.py:532
  26.3 1.2 copy-start
  27.5 1.2 copy-start.1
  28.8 0.9 copy-start.5
  29.7 0.8 copy-start.6
  34.0 2.4 %collective-permute-start.2 = (bf16[4,104,1024]{2,1,0:T(8,128)(2,1)S(1)}, bf16[4,104,1024]{2,1,0:T(8,128)(2,1)S(1)}, u32[]{:S(2)}, u32[]{:S(2)}) collective-permute-start(bf16[4,104,1024]{2,1,0:T(8,128)(2,1)S(1)} %get-tuple-element.91), channel_id=1, source_target_pairs={{0,1},{1,0},{2,3},{3,2},{4,5},{5,4},{6,7},{7,6},{8,9},{9,8},{10,11... | collective-permute-start | bytes 2555912 | tf_op jit(solution)/shard_map/ppermute | solution.py:535
  34.1 8.3 %collective-permute-start.5 = (bf16[72,1024]{1,0:T(8,128)(2,1)S(1)}, bf16[72,1024]{1,0:T(8,128)(2,1)S(1)}, u32[]{:S(2)}, u32[]{:S(2)}) collective-permute-start(bf16[72,1024]{1,0:T(8,128)(2,1)S(1)} %get-tuple-element.94), channel_id=1, source_target_pairs={{0,2},{1,3},{2,0},{3,1},{4,6},{5,7},{6,4},{7,5},{8,10},{9,11},{10,... | collective-permute-start | bytes 442376 | tf_op jit(solution)/shard_map/ppermute | solution.py:535
  36.6 13.1 %collective-permute-start.10 = (bf16[2,72,1024]{2,1,0:T(8,128)(2,1)S(1)}, bf16[2,72,1024]{2,1,0:T(8,128)(2,1)S(1)}, u32[]{:S(2)}, u32[]{:S(2)}) collective-permute-start(bf16[2,72,1024]{2,1,0:T(8,128)(2,1)S(1)} %get-tuple-element.96.refs_0_), channel_id=1, source_target_pairs={{0,16},{8,24},{16,0},{24,8},{1,17},{9,25},{17,1},{25,9},{2,18},{10... | collective-permute-start | bytes 884744 | tf_op jit(solution)/shard_map/ppermute | solution.py:532
  38.2 11.5 %collective-permute-start.9 = (bf16[2,72,1024]{2,1,0:T(8,128)(2,1)S(1)}, bf16[2,72,1024]{2,1,0:T(8,128)(2,1)S(1)}, u32[]{:S(2)}, u32[]{:S(2)}) collective-permute-start(bf16[2,72,1024]{2,1,0:T(8,128)(2,1)S(1)} %get-tuple-element.96.refs_0_), channel_id=1, source_target_pairs={{0,8},{8,0},{16,24},{24,16},{1,9},{9,1},{17,25},{25,17},{2,10},{10... | collective-permute-start | bytes 884744 | tf_op jit(solution)/shard_map/ppermute | solution.py:529
  39.6 8.9 %collective-permute-start.6 = (bf16[72,1024]{1,0:T(8,128)(2,1)S(1)}, bf16[72,1024]{1,0:T(8,128)(2,1)S(1)}, u32[]{:S(2)}, u32[]{:S(2)}) collective-permute-start(bf16[72,1024]{1,0:T(8,128)(2,1)S(1)} %get-tuple-element.95), channel_id=1, source_target_pairs={{0,3},{1,2},{2,1},{3,0},{4,7},{5,6},{6,5},{7,4},{8,11},{9,10},{10,... | collective-permute-start | bytes 442376 | tf_op jit(solution)/shard_map/ppermute | solution.py:535
  40.1 17.1 %collective-permute-start.3 = (bf16[2,72,1024]{2,1,0:T(8,128)(2,1)S(1)}, bf16[2,72,1024]{2,1,0:T(8,128)(2,1)S(1)}, u32[]{:S(2)}, u32[]{:S(2)}) collective-permute-start(bf16[2,72,1024]{2,1,0:T(8,128)(2,1)S(1)} %get-tuple-element.93), channel_id=1, source_target_pairs={{0,4},{1,5},{2,6},{3,7},{4,0},{5,1},{6,2},{7,3},{8,12},{9,13},{10,... | collective-permute-start | bytes 884744 | tf_op jit(solution)/shard_map/ppermute | solution.py:535
  48.5 9.9 %collective-permute-start.8 = (bf16[2,72,1024]{2,1,0:T(8,128)(2,1)S(1)}, bf16[2,72,1024]{2,1,0:T(8,128)(2,1)S(1)}, u32[]{:S(2)}, u32[]{:S(2)}) collective-permute-start(bf16[2,72,1024]{2,1,0:T(8,128)(2,1)S(1)} %near_kernel.1.refs_2_.refs_0_), channel_id=1, source_target_pairs={{0,16},{8,24},{16,0},{24,8},{1,17},{9,25},{17,1},{25,9},{2,18},{10... | collective-permute-start | bytes 884744 | tf_op jit(solution)/shard_map/ppermute | solution.py:532
  49.1 9.9 %collective-permute-start.7 = (bf16[2,72,1024]{2,1,0:T(8,128)(2,1)S(1)}, bf16[2,72,1024]{2,1,0:T(8,128)(2,1)S(1)}, u32[]{:S(2)}, u32[]{:S(2)}) collective-permute-start(bf16[2,72,1024]{2,1,0:T(8,128)(2,1)S(1)} %near_kernel.1.refs_2_.refs_0_), channel_id=1, source_target_pairs={{0,8},{8,0},{16,24},{24,16},{1,9},{9,1},{17,25},{25,17},{2,10},{10... | collective-permute-start | bytes 884744 | tf_op jit(solution)/shard_map/ppermute | solution.py:529
  49.7 11.1 %collective-permute-start.11 = (bf16[1,72,1024]{2,1,0:T(8,128)(2,1)S(1)}, bf16[1,72,1024]{2,1,0:T(8,128)(2,1)S(1)}, u32[]{:S(2)}, u32[]{:S(2)}) collective-permute-start(bf16[1,72,1024]{2,1,0:T(8,128)(2,1)S(1)} %get-tuple-element.97), channel_id=1, source_target_pairs={{0,8},{8,0},{16,24},{24,16},{1,9},{9,1},{17,25},{25,17},{2,10},{10... | collective-permute-start | bytes 442376 | tf_op jit(solution)/shard_map/ppermute | solution.py:529
  51.3 9.6 %collective-permute-start.12 = (bf16[1,72,1024]{2,1,0:T(8,128)(2,1)S(1)}, bf16[1,72,1024]{2,1,0:T(8,128)(2,1)S(1)}, u32[]{:S(2)}, u32[]{:S(2)}) collective-permute-start(bf16[1,72,1024]{2,1,0:T(8,128)(2,1)S(1)} %get-tuple-element.98), channel_id=1, source_target_pairs={{0,16},{8,24},{16,0},{24,8},{1,17},{9,25},{17,1},{25,9},{2,18},{10... | collective-permute-start | bytes 442376 | tf_op jit(solution)/shard_map/ppermute | solution.py:532
  60.9 11.1 %collective-permute-start.13 = (bf16[3,72,1024]{2,1,0:T(8,128)(2,1)S(1)}, bf16[3,72,1024]{2,1,0:T(8,128)(2,1)S(1)}, u32[]{:S(2)}, u32[]{:S(2)}) collective-permute-start(bf16[3,72,1024]{2,1,0:T(8,128)(2,1)S(1)} %get-tuple-element.99), channel_id=1, source_target_pairs={{0,8},{8,0},{16,24},{24,16},{1,9},{9,1},{17,25},{25,17},{2,10},{10... | collective-permute-start | bytes 1327112 | tf_op jit(solution)/shard_map/ppermute | solution.py:529
  61.5 10.6 %collective-permute-start.14 = (bf16[3,72,1024]{2,1,0:T(8,128)(2,1)S(1)}, bf16[3,72,1024]{2,1,0:T(8,128)(2,1)S(1)}, u32[]{:S(2)}, u32[]{:S(2)}) collective-permute-start(bf16[3,72,1024]{2,1,0:T(8,128)(2,1)S(1)} %get-tuple-element.100), channel_id=1, source_target_pairs={{0,16},{8,24},{16,0},{24,8},{1,17},{9,25},{17,1},{25,9},{2,18},{10... | collective-permute-start | bytes 1327112 | tf_op jit(solution)/shard_map/ppermute | solution.py:532
  63.0 9.0 %collective-permute-start.4 = (bf16[2,72,1024]{2,1,0:T(8,128)(2,1)S(1)}, bf16[2,72,1024]{2,1,0:T(8,128)(2,1)S(1)}, u32[]{:S(2)}, u32[]{:S(2)}) collective-permute-start(bf16[2,72,1024]{2,1,0:T(8,128)(2,1)S(1)} %hold_farthest.1.refs_5_), channel_id=1, source_target_pairs={{0,6},{1,7},{2,4},{3,5},{4,2},{5,3},{6,0},{7,1},{8,14},{9,15},{10,... | collective-permute-start | bytes 884744 | tf_op jit(solution)/shard_map/ppermute | solution.py:535
  72.2 12.5 %collective-permute-start.16 = (bf16[3,72,1024]{2,1,0:T(8,128)(2,1)S(1)}, bf16[3,72,1024]{2,1,0:T(8,128)(2,1)S(1)}, u32[]{:S(2)}, u32[]{:S(2)}) collective-permute-start(bf16[3,72,1024]{2,1,0:T(8,128)(2,1)S(1)} %get-tuple-element.103), channel_id=1, source_target_pairs={{0,16},{8,24},{16,0},{24,8},{1,17},{9,25},{17,1},{25,9},{2,18},{10... | collective-permute-start | bytes 1327112 | tf_op jit(solution)/shard_map/ppermute | solution.py:532
  73.7 11.0 %collective-permute-start.15 = (bf16[3,72,1024]{2,1,0:T(8,128)(2,1)S(1)}, bf16[3,72,1024]{2,1,0:T(8,128)(2,1)S(1)}, u32[]{:S(2)}, u32[]{:S(2)}) collective-permute-start(bf16[3,72,1024]{2,1,0:T(8,128)(2,1)S(1)} %get-tuple-element.102.refs_3_), channel_id=1, source_target_pairs={{0,8},{8,0},{16,24},{24,16},{1,9},{9,1},{17,25},{25,17},{2,10},{10... | collective-permute-start | bytes 1327112 | tf_op jit(solution)/shard_map/ppermute | solution.py:529
  75.3 14.7 %collective-permute-start.20 = (bf16[2,40,1024]{2,1,0:T(8,128)(2,1)S(1)}, bf16[2,40,1024]{2,1,0:T(8,128)(2,1)S(1)}, u32[]{:S(2)}, u32[]{:S(2)}) collective-permute-start(bf16[2,40,1024]{2,1,0:T(8,128)(2,1)S(1)} %get-tuple-element.118), channel_id=1, source_target_pairs={{0,4},{1,5},{2,6},{3,7},{4,0},{5,1},{6,2},{7,3},{8,12},{9,13},{10,... | collective-permute-start | bytes 491528 | tf_op jit(solution)/shard_map/ppermute | solution.py:535
  79.5 10.5 %collective-permute-start.21 = (bf16[2,40,1024]{2,1,0:T(8,128)(2,1)S(1)}, bf16[2,40,1024]{2,1,0:T(8,128)(2,1)S(1)}, u32[]{:S(2)}, u32[]{:S(2)}) collective-permute-start(bf16[2,40,1024]{2,1,0:T(8,128)(2,1)S(1)} %get-tuple-element.119), channel_id=1, source_target_pairs={{0,6},{1,7},{2,4},{3,5},{4,2},{5,3},{6,0},{7,1},{8,14},{9,15},{10,... | collective-permute-start | bytes 491528 | tf_op jit(solution)/shard_map/ppermute | solution.py:535
  81.5 8.5 %collective-permute-start.19 = (bf16[2,40,1024]{2,1,0:T(8,128)(2,1)S(1)}, bf16[2,40,1024]{2,1,0:T(8,128)(2,1)S(1)}, u32[]{:S(2)}, u32[]{:S(2)}) collective-permute-start(bf16[2,40,1024]{2,1,0:T(8,128)(2,1)S(1)} %get-tuple-element.109.refs_11_), channel_id=1, source_target_pairs={{0,2},{1,3},{2,0},{3,1},{4,6},{5,7},{6,4},{7,5},{8,10},{9,11},{10,... | collective-permute-start | bytes 491528 | tf_op jit(solution)/shard_map/ppermute | solution.py:535
  84.7 5.3 %collective-permute-start.17 = (bf16[1,72,1024]{2,1,0:T(8,128)(2,1)S(1)}, bf16[1,72,1024]{2,1,0:T(8,128)(2,1)S(1)}, u32[]{:S(2)}, u32[]{:S(2)}) collective-permute-start(bf16[1,72,1024]{2,1,0:T(8,128)(2,1)S(1)} %get-tuple-element.111), channel_id=1, source_target_pairs={{0,16},{8,24},{16,0},{24,8},{1,17},{9,25},{17,1},{25,9},{2,18},{10... | collective-permute-start | bytes 442376 | tf_op jit(solution)/shard_map/ppermute | solution.py:532
  86.0 5.1 %collective-permute-start.18 = (bf16[1,72,1024]{2,1,0:T(8,128)(2,1)S(1)}, bf16[1,72,1024]{2,1,0:T(8,128)(2,1)S(1)}, u32[]{:S(2)}, u32[]{:S(2)}) collective-permute-start(bf16[1,72,1024]{2,1,0:T(8,128)(2,1)S(1)} %get-tuple-element.112), channel_id=1, source_target_pairs={{0,8},{8,0},{16,24},{24,16},{1,9},{9,1},{17,25},{25,17},{2,10},{10... | collective-permute-start | bytes 442376 | tf_op jit(solution)/shard_map/ppermute | solution.py:529
  98.9 8.9 %collective-permute-start.22 = (bf16[9,16,1024]{2,1,0:T(8,128)(2,1)S(1)}, bf16[9,16,1024]{2,1,0:T(8,128)(2,1)S(1)}, u32[]{:S(2)}, u32[]{:S(2)}) collective-permute-start(bf16[9,16,1024]{2,1,0:T(8,128)(2,1)S(1)} %get-tuple-element.125), channel_id=1, source_target_pairs={{0,8},{8,0},{16,24},{24,16},{1,9},{9,1},{17,25},{25,17},{2,10},{10... | collective-permute-start | bytes 884744 | tf_op jit(solution)/shard_map/ppermute | solution.py:529
  99.7 8.6 %collective-permute-start.23 = (bf16[9,16,1024]{2,1,0:T(8,128)(2,1)S(1)}, bf16[9,16,1024]{2,1,0:T(8,128)(2,1)S(1)}, u32[]{:S(2)}, u32[]{:S(2)}) collective-permute-start(bf16[9,16,1024]{2,1,0:T(8,128)(2,1)S(1)} %get-tuple-element.126), channel_id=1, source_target_pairs={{0,16},{8,24},{16,0},{24,8},{1,17},{9,25},{17,1},{25,9},{2,18},{10... | collective-permute-start | bytes 884744 | tf_op jit(solution)/shard_map/ppermute | solution.py:532
  100.3 49.7 %copy-start.9 = (s32[32,2]{0,1:T(2,128)S(1)}, s32[32,2]{0,1:T(2,128)}, u32[]{:S(2)}) copy-start(s32[32,2]{0,1:T(2,128)} %param.25) | copy-start | bytes 772
  100.3 49.8 %copy-start.10 = (f32[32,2]{0,1:T(2,128)S(1)}, f32[32,2]{0,1:T(2,128)}, u32[]{:S(2)}) copy-start(f32[32,2]{0,1:T(2,128)} %param.26) | copy-start | bytes 772
  108.4 9.8 %collective-permute-start.24 = (bf16[9,16,1024]{2,1,0:T(8,128)(2,1)S(1)}, bf16[9,16,1024]{2,1,0:T(8,128)(2,1)S(1)}, u32[]{:S(2)}, u32[]{:S(2)}) collective-permute-start(bf16[9,16,1024]{2,1,0:T(8,128)(2,1)S(1)} %get-tuple-element.133), channel_id=1, source_target_pairs={{0,8},{8,0},{16,24},{24,16},{1,9},{9,1},{17,25},{25,17},{2,10},{10... | collective-permute-start | bytes 884744 | tf_op jit(solution)/shard_map/ppermute | solution.py:529
  110.4 9.8 %collective-permute-start.25 = (bf16[9,16,1024]{2,1,0:T(8,128)(2,1)S(1)}, bf16[9,16,1024]{2,1,0:T(8,128)(2,1)S(1)}, u32[]{:S(2)}, u32[]{:S(2)}) collective-permute-start(bf16[9,16,1024]{2,1,0:T(8,128)(2,1)S(1)} %get-tuple-element.134), channel_id=1, source_target_pairs={{0,16},{8,24},{16,0},{24,8},{1,17},{9,25},{17,1},{25,9},{2,18},{10... | collective-permute-start | bytes 884744 | tf_op jit(solution)/shard_map/ppermute | solution.py:532
  110.5 14.1 %collective-permute-start.28 = (bf16[9,16,1024]{2,1,0:T(8,128)(2,1)S(1)}, bf16[9,16,1024]{2,1,0:T(8,128)(2,1)S(1)}, u32[]{:S(2)}, u32[]{:S(2)}) collective-permute-start(bf16[9,16,1024]{2,1,0:T(8,128)(2,1)S(1)} %get-tuple-element.139), channel_id=1, source_target_pairs={{0,8},{8,0},{16,24},{24,16},{1,9},{9,1},{17,25},{25,17},{2,10},{10... | collective-permute-start | bytes 884744 | tf_op jit(solution)/shard_map/ppermute | solution.py:529
  110.6 15.9 %collective-permute-start.29 = (bf16[9,16,1024]{2,1,0:T(8,128)(2,1)S(1)}, bf16[9,16,1024]{2,1,0:T(8,128)(2,1)S(1)}, u32[]{:S(2)}, u32[]{:S(2)}) collective-permute-start(bf16[9,16,1024]{2,1,0:T(8,128)(2,1)S(1)} %get-tuple-element.140), channel_id=1, source_target_pairs={{0,16},{8,24},{16,0},{24,8},{1,17},{9,25},{17,1},{25,9},{2,18},{10... | collective-permute-start | bytes 884744 | tf_op jit(solution)/shard_map/ppermute | solution.py:532
  120.4 10.5 %collective-permute-start.26 = (bf16[9,16,1024]{2,1,0:T(8,128)(2,1)S(1)}, bf16[9,16,1024]{2,1,0:T(8,128)(2,1)S(1)}, u32[]{:S(2)}, u32[]{:S(2)}) collective-permute-start(bf16[9,16,1024]{2,1,0:T(8,128)(2,1)S(1)} %get-tuple-element.137), channel_id=1, source_target_pairs={{0,8},{8,0},{16,24},{24,16},{1,9},{9,1},{17,25},{25,17},{2,10},{10... | collective-permute-start | bytes 884744 | tf_op jit(solution)/shard_map/ppermute | solution.py:529
  120.7 11.5 %collective-permute-start.27 = (bf16[9,16,1024]{2,1,0:T(8,128)(2,1)S(1)}, bf16[9,16,1024]{2,1,0:T(8,128)(2,1)S(1)}, u32[]{:S(2)}, u32[]{:S(2)}) collective-permute-start(bf16[9,16,1024]{2,1,0:T(8,128)(2,1)S(1)} %get-tuple-element.138), channel_id=1, source_target_pairs={{0,16},{8,24},{16,0},{24,8},{1,17},{9,25},{17,1},{25,9},{2,18},{10... | collective-permute-start | bytes 884744 | tf_op jit(solution)/shard_map/ppermute | solution.py:532
  120.8 12.6 %collective-permute-start.34 = (bf16[9,16,1024]{2,1,0:T(8,128)(2,1)S(1)}, bf16[9,16,1024]{2,1,0:T(8,128)(2,1)S(1)}, u32[]{:S(2)}, u32[]{:S(2)}) collective-permute-start(bf16[9,16,1024]{2,1,0:T(8,128)(2,1)S(1)} %get-tuple-element.145.refs_6_), channel_id=1, source_target_pairs={{0,6},{1,7},{2,4},{3,5},{4,2},{5,3},{6,0},{7,1},{8,14},{9,15},{10,... | collective-permute-start | bytes 884744 | tf_op jit(solution)/shard_map/ppermute | solution.py:535
  126.7 13.0 %collective-permute-start.32 = (bf16[9,16,1024]{2,1,0:T(8,128)(2,1)S(1)}, bf16[9,16,1024]{2,1,0:T(8,128)(2,1)S(1)}, u32[]{:S(2)}, u32[]{:S(2)}) collective-permute-start(bf16[9,16,1024]{2,1,0:T(8,128)(2,1)S(1)} %get-tuple-element.151), channel_id=1, source_target_pairs={{0,8},{8,0},{16,24},{24,16},{1,9},{9,1},{17,25},{25,17},{2,10},{10... | collective-permute-start | bytes 884744 | tf_op jit(solution)/shard_map/ppermute | solution.py:529
  127.0 12.7 %collective-permute-start.33 = (bf16[9,16,1024]{2,1,0:T(8,128)(2,1)S(1)}, bf16[9,16,1024]{2,1,0:T(8,128)(2,1)S(1)}, u32[]{:S(2)}, u32[]{:S(2)}) collective-permute-start(bf16[9,16,1024]{2,1,0:T(8,128)(2,1)S(1)} %get-tuple-element.152), channel_id=1, source_target_pairs={{0,16},{8,24},{16,0},{24,8},{1,17},{9,25},{17,1},{25,9},{2,18},{10... | collective-permute-start | bytes 884744 | tf_op jit(solution)/shard_map/ppermute | solution.py:532
  132.3 7.6 %collective-permute-start.30 = (bf16[9,16,1024]{2,1,0:T(8,128)(2,1)S(1)}, bf16[9,16,1024]{2,1,0:T(8,128)(2,1)S(1)}, u32[]{:S(2)}, u32[]{:S(2)}) collective-permute-start(bf16[9,16,1024]{2,1,0:T(8,128)(2,1)S(1)} %get-tuple-element.148), channel_id=1, source_target_pairs={{0,8},{8,0},{16,24},{24,16},{1,9},{9,1},{17,25},{25,17},{2,10},{10... | collective-permute-start | bytes 884744 | tf_op jit(solution)/shard_map/ppermute | solution.py:529
  133.2 6.7 %collective-permute-start.31 = (bf16[9,16,1024]{2,1,0:T(8,128)(2,1)S(1)}, bf16[9,16,1024]{2,1,0:T(8,128)(2,1)S(1)}, u32[]{:S(2)}, u32[]{:S(2)}) collective-permute-start(bf16[9,16,1024]{2,1,0:T(8,128)(2,1)S(1)} %get-tuple-element.149), channel_id=1, source_target_pairs={{0,16},{8,24},{16,0},{24,8},{1,17},{9,25},{17,1},{25,9},{2,18},{10... | collective-permute-start | bytes 884744 | tf_op jit(solution)/shard_map/ppermute | solution.py:532
  133.4 14.3 %collective-permute-start.36 = (bf16[9,16,1024]{2,1,0:T(8,128)(2,1)S(1)}, bf16[9,16,1024]{2,1,0:T(8,128)(2,1)S(1)}, u32[]{:S(2)}, u32[]{:S(2)}) collective-permute-start(bf16[9,16,1024]{2,1,0:T(8,128)(2,1)S(1)} %get-tuple-element.153), channel_id=1, source_target_pairs={{0,4},{1,5},{2,6},{3,7},{4,0},{5,1},{6,2},{7,3},{8,12},{9,13},{10,... | collective-permute-start | bytes 884744 | tf_op jit(solution)/shard_map/ppermute | solution.py:535
  139.9 8.1 %collective-permute-start.35 = (bf16[9,16,1024]{2,1,0:T(8,128)(2,1)S(1)}, bf16[9,16,1024]{2,1,0:T(8,128)(2,1)S(1)}, u32[]{:S(2)}, u32[]{:S(2)}) collective-permute-start(bf16[9,16,1024]{2,1,0:T(8,128)(2,1)S(1)} %finish_1.1), channel_id=1, source_target_pairs={{0,2},{1,3},{2,0},{3,1},{4,6},{5,7},{6,4},{7,5},{8,10},{9,11},{10,... | collective-permute-start | bytes 884744 | tf_op jit(solution)/shard_map/ppermute | solution.py:535
  148.0 2.1 %collective-permute-start.37 = (bf16[2,9,16,1024]{3,2,1,0:T(8,128)(2,1)S(1)}, bf16[2,9,16,1024]{3,2,1,0:T(8,128)(2,1)S(1)}, u32[]{:S(2)}, u32[]{:S(2)}) collective-permute-start(bf16[2,9,16,1024]{3,2,1,0:T(8,128)(2,1)S(1)} %second_kernel.1), channel_id=1, source_target_pairs={{0,1},{1,0},{2,3},{3,2},{4,5},{5,4},{6,7},{7,6},{8,9},{9,8},{10,11... | collective-permute-start | bytes 1769480 | tf_op jit(solution)/shard_map/ppermute | solution.py:535
